TPU v7x, 512 devices: a whole 4x8x8 slice. The times are simulated.
512 devices in a mesh: dp: 128 (over z, y, core), mp: 4 (over x).
Axes of the slice: x: 4, y: 8, z: 8, core: 2. Of those that a mesh axis runs over, the one named last changes fastest.
Arguments:
- query_feats: bfloat16 [512, 1024], P('dp'), may hold values from -6 to 6
- item_feats: bfloat16 [131072, 1024], P('dp'), may hold values from -6 to 6
- w_in: bfloat16 [1024, 1024], P(None, 'mp'), may hold values from -0.1875 to 0.1875
- w_out: bfloat16 [1024, 256], P('mp'), may hold values from -0.1875 to 0.1875
- negatives: int32 [512, 128], P('dp'), may hold values from 0 to 131071, as said below
- positives: int32 [512], P('dp'), may hold values from 0 to 131071, as said below
- owner_map: int32 [131072], replicated, may hold values from 0 to 131071, as said below
Outputs:
- grad_in: bfloat16 [1024, 1024], P(None, 'mp')
- grad_out: bfloat16 [1024, 256], P('mp')
Inputs may be any that keep to these rules, and one draw needn't show every extreme that they name: A permutation of the item ids: item i is row owner_map[i] of item_feats, stored on dp device owner_map[i] // 1024. The hard negatives of the 4 queries of one dp device name at most 16 items stored on any one dp device, counted with repeats; for the queries of dp device i, dp device (i + 64) mod 128 stores exactly 16 of them. `positives`: the positive of a query is stored on the query's own dp device.
All inputs are finite; a program needn't handle non-finite values.
Results may differ from a plain program's by a relative error of at most 0.013.
Values may be sent and summed in bfloat16 or wider, within the bound.
No kernel may reach another device: no remote copies, remote signals or barrier semaphores. Data moves between devices by JAX's collectives and lax.ppermute only.
A program may use at most 64 MiB of HBM per device.

v0:
```python
import math

import jax
import jax.numpy as jnp
from jax import lax
from jax.sharding import PartitionSpec as P


def local(query_feats, item_feats, w_in, w_out, negatives, positives, owner_map):
    dp_count = lax.axis_size("dp")
    own_index = lax.axis_index("dp")
    query_count = query_feats.shape[0]
    item_count = item_feats.shape[0]
    negative_count = negatives.shape[1]
    score_scale = 4.0 / math.sqrt(w_out.shape[1])
    capacity = 4 * query_count * negative_count // dp_count
    features = jnp.concatenate([query_feats, item_feats], 0)
    preact = jnp.dot(features, w_in, preferred_element_type=jnp.float32)
    hidden = jnp.maximum(preact, 0.0).astype(jnp.bfloat16)
    partial_out = jnp.dot(hidden, w_out, preferred_element_type=jnp.float32)
    layer_out = lax.psum(partial_out, "mp")
    embedding = jnp.tanh(layer_out)
    emb16 = embedding.astype(jnp.bfloat16)
    width = emb16.shape[1]
    query_emb = emb16[:query_count]
    item_emb = emb16[query_count:]
    query32 = query_emb.astype(jnp.float32)
    neg_rows = jnp.take(owner_map, negatives.reshape(-1), axis=0)
    owners = neg_rows // item_count
    local_rows = neg_rows - owners * item_count
    onehot = (owners[:, None] == jnp.arange(dp_count, dtype=jnp.int32)[None, :]).astype(jnp.int32)
    running = jnp.cumsum(onehot, 0)
    slots = jnp.sum(running * onehot, 1) - 1
    request = jnp.zeros((dp_count, capacity), jnp.int32).at[owners, slots].set(local_rows)
    pos_local = jnp.take(owner_map, positives, axis=0) - own_index * item_count
    pos_emb = jnp.take(item_emb, pos_local, axis=0)
    pos_score = jnp.einsum("qd,qd->q", query_emb, pos_emb, preferred_element_type=jnp.float32)
    asked_rows = lax.all_to_all(request, "dp", split_axis=0, concat_axis=0, tiled=True)
    fetched = jnp.take(item_emb, asked_rows, axis=0)
    replies, asked_rows = (
        lax.all_to_all(fetched, "dp", split_axis=0, concat_axis=0, tiled=True),
        asked_rows,
    )
    neg_emb = replies[owners, slots].reshape(query_count, negative_count, width)
    scored = jnp.einsum("qd,qkd->qk", query_emb, neg_emb, preferred_element_type=jnp.float32)
    pos_exp = jnp.exp(score_scale * pos_score)
    neg_exp = jnp.exp(score_scale * scored)
    denominator = pos_exp + jnp.sum(neg_exp, 1)
    pos_grad = pos_exp / denominator - 1.0
    neg_grad = neg_exp / denominator[:, None]
    pair_neg = (score_scale * neg_grad[:, :, None] * query32[:, None, :]).astype(jnp.bfloat16)
    query_grad = score_scale * (
        pos_grad[:, None] * pos_emb.astype(jnp.float32)
        + jnp.sum(neg_grad[:, :, None] * neg_emb.astype(jnp.float32), 1)
    )
    outgoing = jnp.zeros((dp_count, capacity, width), jnp.bfloat16)
    outgoing = outgoing.at[owners, slots].set(pair_neg.reshape(-1, width))
    returned = lax.all_to_all(outgoing, "dp", split_axis=0, concat_axis=0, tiled=True)
    item_grad = jnp.zeros((item_count, width), jnp.float32)
    item_grad = item_grad.at[asked_rows.reshape(-1)].add(
        returned.reshape(-1, width).astype(jnp.float32)
    )
    pair_pos = (score_scale * pos_grad[:, None] * query32).astype(jnp.bfloat16)
    item_grad = item_grad.at[pos_local].add(pair_pos.astype(jnp.float32))
    emb_grad = jnp.concatenate([query_grad, item_grad], 0)
    tanh_grad = (emb_grad * (1.0 - embedding * embedding)).astype(jnp.bfloat16)
    out_term = lax.dot_general(
        hidden, tanh_grad, (((0,), (0,)), ((), ())), preferred_element_type=jnp.float32
    )
    hidden_grad = lax.dot_general(
        tanh_grad, w_out, (((1,), (1,)), ((), ())), preferred_element_type=jnp.float32
    )
    preact_grad = jnp.where(preact > 0, hidden_grad, 0.0).astype(jnp.bfloat16)
    in_term = lax.dot_general(
        features, preact_grad, (((0,), (0,)), ((), ())), preferred_element_type=jnp.float32
    )
    summed_in, summed_out = lax.psum((in_term, out_term), "dp")
    return (summed_in.astype(jnp.bfloat16), summed_out.astype(jnp.bfloat16))


def solution(mesh):
    return jax.shard_map(
        local,
        mesh=mesh,
        in_specs=(
            P("dp", None),
            P("dp", None),
            P(None, "mp"),
            P("mp", None),
            P("dp", None),
            P("dp"),
            P(),
        ),
        out_specs=(P(None, "mp"), P("mp", None)),
        check_vma=False,
    )
```

profile of v0, /device:TPU:1, one launch (start us, length us, event | category | flops | bytes accessed | tf_op | source)
XLA Modules:
  0.0 757.0 jit_solution(6012564183738899778)
XLA Ops:
  7.2 1.0 copy-done
  8.2 2.3 fusion.4
  10.5 1.0 copy-done.2
  11.5 1.3 fusion.14
  12.9 0.7 copy-done.6
  13.5 0.4 copy-done.1
  13.9 3.1 gather_fusion.2
  17.2 0.2 fusion.11
  17.5 0.2 fusion.10
  17.8 24.6 %scatter_fusion = s32[128,16]{0,1:T(8,128)S(1)} fusion(s32[128,16]{0,1:T(8,128)S(1)} %broadcast_in_dim.66, s32[512]{0:T(512)S(1)} %bitcast.62, s32[512]{0:T(512)S(1)} %get-tuple-element.10), kind=kCustom, calls=%fused_computation.5 | custom fusion | bytes 10240 | tf_op jit(solution)/shard_map/scatter | solution.py:34
  42.5 29.7 %all_to_all.25 = s32[128,1,16]{2,1,0:T(1,128)S(1)} all-to-all(s32[128,1,16]{2,1,0:T(1,128)S(1)} %copy.18), channel_id=1, replica_groups=mesh['dp'=128,'mp'=4] {'dp'}, dimensions={0} | all-to-all | bytes 16384 | tf_op jit(solution)/shard_map/all_to_all | solution.py:38
  72.5 1.6 all-reduce.4.cloned.1.call-done
  74.1 1.4 tanh_convert_fusion
  75.6 7.5 gather_fusion.3
  83.2 1.2 broadcast_select_fusion
  84.4 15.7 %all-to-all-start.1 = ((bf16[128,16,256]{2,1,0:T(8,128)(2,1)}), bf16[128,16,256]{2,1,0:T(8,128)(2,1)S(1)}, u32[]{:S(2)}, u32[]{:S(2)}) async-start(bf16[128,16,256]{2,1,0:T(8,128)(2,1)} %broadcast_select_fusion), calls=%async_computation.1 | async-start | bytes 2097152 | tf_op jit(solution)/shard_map/all_to_all | solution.py:41
  100.2 0.6 gather_fusion
  100.8 0.6 gather_fusion.1
  101.6 29.4 %all-to-all-done.1 = bf16[128,16,256]{2,1,0:T(8,128)(2,1)S(1)} async-done(((bf16[128,16,256]{2,1,0:T(8,128)(2,1)}), bf16[128,16,256]{2,1,0:T(8,128)(2,1)S(1)}, u32[]{:S(2)}, u32[]{:S(2)}) %all-to-all-start.1) | async-done | bytes 1048608 | tf_op jit(solution)/shard_map/all_to_all | solution.py:41
  131.0 3.2 gather_fusion.4
  134.8 1.1 broadcast_in_dim.74
  135.8 55.4 %scatter_fusion.1 = bf16[128,16,256]{2,1,0:T(8,128)(2,1)} fusion(bf16[128,16,256]{2,1,0:T(8,128)(2,1)} %broadcast_in_dim.74, s32[512]{0:T(512)S(1)} %bitcast.63, bf16[512,256]{1,0:T(8,128)(2,1)S(1)} %fusion.8), kind=kCustom, calls=%fused_computation.6 | custom fusion | bytes 790528 | tf_op jit(solution)/shard_map/scatter | solution.py:57
  191.2 6.8 all-to-all-start.2
  198.0 0.5 broadcast.415
  198.5 0.8 reduce.5
  199.6 29.2 %all-to-all-done.2 = bf16[128,16,256]{2,1,0:T(8,128)(2,1)S(1)} async-done(((bf16[128,16,256]{2,1,0:T(8,128)(2,1)}), bf16[128,16,256]{2,1,0:T(8,128)(2,1)S(1)}, u32[]{:S(2)}, u32[]{:S(2)}) %all-to-all-start.2) | async-done | bytes 1048608 | tf_op jit(solution)/shard_map/all_to_all | solution.py:58
  228.9 13.0 %scatter_custom_fusion.2 = f32[1024,256]{1,0:T(8,128)} fusion(s32[2048]{0:T(1024)S(1)} %bitcast.78, bf16[2048,256]{1,0:T(8,128)(2,1)S(1)} %bitcast.66, f32[]{:T(128)} %constant.55.clone.1), kind=kCustom, calls=%fused_computation.12 | custom fusion | flops 1048576 | bytes 2097156 | tf_op jit(solution)/shard_map/scatter-add | solution.py:60
  241.9 2.8 scatter_custom_fusion.3
  244.7 1.6 fusion.5
  246.3 3.9 fusion.3
  250.3 0.4 fusion.13
  250.6 499.6 %all-reduce.5 = (bf16[1024,256]{1,0:T(8,128)(2,1)}, bf16[256,256]{1,0:T(8,128)(2,1)}) all-reduce(f32[1024,256]{1,0:T(8,128)} %fusion.3, f32[256,256]{1,0:T(8,128)S(1)} %fusion.13), channel_id=1, replica_groups=mesh['dp'=128,'mp'=4] {'dp'}, use_global_device_ids=true, to_apply=%region_10.11 | all-reduce | flops 327680 | bytes 1966080 | tf_op jit(solution)/shard_map/psum | solution.py:77
  (53 shorter events, 2.0 us)
Async XLA Ops:
  7.2 1.0 copy-start
  7.2 4.3 copy-start.5
  7.2 67.0 %all-reduce.4.cloned.1.call-start = ((), (), s32[]{:S(2)}) async-start(), calls=%async_computation.3 | async-start | bytes 2113536 | tf_op jit(solution)/shard_map/psum | solution.py:21
  10.5 1.0 copy-start.2
  12.8 0.7 copy-start.6
  12.8 1.1 copy-start.1
  84.4 15.7 %copy-start.7 = (s32[4]{0:T(128)S(1)}, s32[4]{0:T(128)}, u32[]{:S(2)}) copy-start(s32[4]{0:T(128)} %param.12) | copy-start | bytes 52
  84.4 46.6 %all-to-all-start.1 = ((bf16[128,16,256]{2,1,0:T(8,128)(2,1)}), bf16[128,16,256]{2,1,0:T(8,128)(2,1)S(1)}, u32[]{:S(2)}, u32[]{:S(2)}) async-start(bf16[128,16,256]{2,1,0:T(8,128)(2,1)} %broadcast_select_fusion), calls=%async_computation.1 | async-start | bytes 2097152 | tf_op jit(solution)/shard_map/all_to_all | solution.py:41
  191.2 37.7 %all-to-all-start.2 = ((bf16[128,16,256]{2,1,0:T(8,128)(2,1)}), bf16[128,16,256]{2,1,0:T(8,128)(2,1)S(1)}, u32[]{:S(2)}, u32[]{:S(2)}) async-start(bf16[128,16,256]{2,1,0:T(8,128)(2,1)} %scatter_fusion.1), calls=%async_computation.2 | async-start | bytes 2097152 | tf_op jit(solution)/shard_map/all_to_all | solution.py:58
  228.9 15.9 %copy-start.4 = (f32[1028,256]{1,0:T(8,128)S(1)}, f32[1028,256]{1,0:T(8,128)}, u32[]{:S(2)}) copy-start(f32[1028,256]{1,0:T(8,128)} %all-reduce.4.cloned.1.call-done) | copy-start | bytes 3158020
  244.7 1.6 copy-start.3
  244.7 1.6 copy-start.8
Sparse Core Ops, SparseCore 0:
  13.0 61.1 all-reduce.3
where the time goes:
time: 762 us; the launch traced here: 757 us
  blocking collectives  529 us (69%)
  local copies, waits for them, and re-layouts  100 us (13%)
  waiting for transfers between devices  60.3 us (8%)
  starting transfers between devices  22.5 us (3%)
  other arithmetic  22.3 us (3%)
  between operations  14.3 us (2%)
  matrix products  8.08 us (1%)
    psum x1, blocking collectives, local(): summed_in, summed_out = lax.psum((in_term, out_term), 'dp')  500 us
    scatter x1, local copies, waits for them, and re-layouts, local(): outgoing = outgoing.at[owners, slots].set(pair_neg.reshape(-1, width))  55.4 us
    all_to_all x1, blocking collectives, local(): lax.all_to_all(request, 'dp', split_axis=0, concat_axis=0, tiled=True)  29.7 us
    all_to_all x1, waiting for transfers between devices, local(): lax.all_to_all(fetched, 'dp', split_axis=0, concat_axis=0, tiled=True)  29.4 us
    all_to_all x1, waiting for transfers between devices, local(): lax.all_to_all(outgoing, 'dp', split_axis=0, concat_axis=0, tiled=True)  29.2 us
    scatter x1, local copies, waits for them, and re-layouts, local(): jnp.zeros((dp_count, capacity), jnp.int32).at[owners, slots].set(local_rows)  24.6 us
    all_to_all x1, starting transfers between devices, local(): lax.all_to_all(fetched, 'dp', split_axis=0, concat_axis=0, tiled=True)  15.7 us
  transfers between devices with their start and end apart: 3, of which 3 were waited for; matrix products, arithmetic and copies ran while one was open for 4% of the time, Pallas kernels for 0%

commit v1 on v0

v1 whole, which is shorter than its diff:
```python
import math

import jax
import jax.numpy as jnp
from jax import lax
from jax.sharding import Mesh, PartitionSpec as P

F32 = jnp.float32
BF16 = jnp.bfloat16
DP = ("z", "y", "c")


def exchange(blocks, axes):
    return lax.all_to_all(blocks, axes, split_axis=0, concat_axis=0, tiled=True)


def spread(block, axes):
    count = lax.axis_size(axes)
    return exchange(jnp.broadcast_to(block[None], (count,) + block.shape), axes)


def total(blocks):
    return jnp.sum(blocks.astype(F32), 0)


def request_codes(negatives, owner_map, dp_count, item_count, capacity):
    query_count, negative_count = negatives.shape
    rows = jnp.take(owner_map, negatives.reshape(-1), axis=0)
    pairs = rows.shape[0]
    owners = rows // item_count
    code = rows - owners * item_count + 1
    owner_hot = owners[:, None] == jnp.arange(dp_count, dtype=jnp.int32)[None, :]
    earlier = jnp.arange(pairs)[:, None] >= jnp.arange(pairs)[None, :]
    running = jnp.dot(earlier.astype(BF16), owner_hot.astype(BF16), preferred_element_type=F32)
    slot = jnp.sum(jnp.where(owner_hot, running, 0.0), 1).astype(jnp.int32) - 1
    query = jnp.arange(pairs, dtype=jnp.int32) // negative_count
    place = query * capacity + slot
    place_hot = place[:, None] == jnp.arange(query_count * capacity, dtype=jnp.int32)[None, :]
    high = jnp.where(place_hot, (code // 32)[:, None], 0).astype(BF16)
    low = jnp.where(place_hot, (code % 32)[:, None], 0).astype(BF16)
    return lax.dot_general(
        owner_hot.astype(BF16),
        jnp.concatenate([high, low], 1),
        (((0,), (0,)), ((), ())),
        preferred_element_type=F32,
    ).astype(BF16)


def local(query_feats, item_feats, w_in, w_out, negatives, positives, owner_map):
    dp_count = lax.axis_size(DP)
    own_index = lax.axis_index(DP)
    z_count, y_count, c_count = (lax.axis_size(a) for a in DP)
    x_count = lax.axis_size("x")
    yc_count = y_count * c_count
    query_count = query_feats.shape[0]
    item_count = item_feats.shape[0]
    width = w_out.shape[1]
    negative_count = negatives.shape[1]
    scale = 4.0 / math.sqrt(width)
    capacity = 4 * query_count * negative_count // dp_count
    queries = query_count * dp_count

    codes = request_codes(negatives, owner_map, dp_count, item_count, capacity)
    pos_local = jnp.take(owner_map, positives, axis=0) - own_index * item_count

    hidden = jnp.maximum(jnp.dot(item_feats, w_in, preferred_element_type=F32), 0.0).astype(BF16)
    hidden_q = jnp.maximum(jnp.dot(query_feats, w_in, preferred_element_type=F32), 0.0).astype(BF16)
    partial = jnp.dot(hidden, w_out, preferred_element_type=F32)
    partial_q = jnp.dot(hidden_q, w_out, preferred_element_type=F32)
    share = item_count // x_count
    blocks = jnp.concatenate(
        [
            partial.reshape(x_count, share, width),
            jnp.broadcast_to(jnp.pad(partial_q, ((0, 4), (0, 0)))[None], (x_count, 8, width)),
        ],
        1,
    )
    own = jnp.tanh(total(exchange(blocks, "x")))
    emb_q = own[share : share + query_count]
    item_emb = lax.all_gather(own[:share], "x", axis=0, tiled=True)

    message = jnp.concatenate(
        [
            jnp.broadcast_to(emb_q.astype(BF16).reshape(1, -1), (dp_count, query_count * width)),
            codes,
        ],
        1,
    )
    asked = exchange(message, DP)
    all_q = asked[:, : query_count * width].reshape(queries, width)
    got = asked[:, query_count * width :].astype(F32)
    half = query_count * capacity
    wanted = (got[:, :half] * 32.0 + got[:, half:]).astype(jnp.int32)
    wanted = wanted.reshape(queries, capacity).T

    emb16 = item_emb.astype(BF16)
    row_id = jnp.arange(item_count, dtype=jnp.int32)
    column = jnp.arange(queries, dtype=jnp.int32)
    own_column = column - own_index * query_count
    pos_of = jnp.where(
        (own_column >= 0) & (own_column < query_count),
        jnp.sum(jnp.where(own_column[None, :] == jnp.arange(query_count)[:, None], pos_local[:, None], 0), 0),
        -1,
    )
    pos_hot = row_id[:, None] == pos_of[None, :]
    counts = jnp.sum((wanted[:, None, :] == row_id[None, :, None] + 1).astype(F32), 0)
    scores = lax.dot_general(emb16, all_q, (((1,), (1,)), ((), ())), preferred_element_type=F32)
    weight = (counts + pos_hot.astype(F32)) * jnp.exp(scale * scores)
    part_d = jnp.sum(weight, 0)
    part_u = lax.dot_general(
        weight.astype(BF16), emb16, (((0,), (0,)), ((), ())), preferred_element_type=F32
    ).astype(BF16)

    def split(d):
        high = d.astype(BF16)
        low = (d - high.astype(F32)).astype(BF16)
        return jnp.concatenate([high.reshape(-1, width), low.reshape(-1, width)], 0)

    d_rows = queries // width

    def joined(rows):
        return (rows[:d_rows] + rows[d_rows : 2 * d_rows]).reshape(queries)

    zq = queries // z_count
    first = total(
        exchange(
            jnp.concatenate(
                [
                    part_u.reshape(z_count, zq, width),
                    jnp.broadcast_to(jnp.pad(split(part_d), ((0, 4), (0, 0)))[None], (z_count, 8, width)),
                ],
                1,
            ),
            "z",
        )
    )
    second = total(
        exchange(
            jnp.concatenate(
                [
                    first[:zq].astype(BF16).reshape(yc_count, query_count, width),
                    jnp.broadcast_to(split(joined(first[zq:]))[None], (yc_count, 2 * d_rows, width)),
                ],
                1,
            ),
            ("y", "c"),
        )
    )
    denominator = joined(second[query_count:])
    own_d = lax.dynamic_slice(denominator, (own_index * query_count,), (query_count,))
    pos_emb = jnp.take(emb16, pos_local, axis=0).astype(F32)
    query_grad = scale * (second[:query_count] / own_d[:, None] - pos_emb)
    coefficient = scale * (weight / denominator[None, :] - pos_hot.astype(F32))
    item_grad = jnp.dot(coefficient.astype(BF16), all_q, preferred_element_type=F32)
    tanh_grad = (item_grad * (1.0 - item_emb * item_emb)).astype(BF16)
    tanh_grad_q = (query_grad * (1.0 - emb_q * emb_q)).astype(BF16)

    def back(feats, hid, grad):
        out_term = lax.dot_general(hid, grad, (((0,), (0,)), ((), ())), preferred_element_type=F32)
        hid_grad = lax.dot_general(grad, w_out, (((1,), (1,)), ((), ())), preferred_element_type=F32)
        pre_grad = jnp.where(hid > 0, hid_grad, 0.0).astype(BF16)
        in_term = lax.dot_general(feats, pre_grad, (((0,), (0,)), ((), ())), preferred_element_type=F32)
        return in_term, out_term

    in_i, out_i = back(item_feats, hidden, tanh_grad)
    in_q, out_q = back(query_feats, hidden_q, tanh_grad_q)
    grads = jnp.concatenate([in_i + in_q, out_i + out_q], 0)
    depth = grads.shape[0]
    grads = total(exchange(grads.astype(BF16).reshape(c_count, depth // c_count, width), "c"))
    grads = total(exchange(grads.astype(BF16).reshape(y_count, -1, width), "y"))
    grads = total(spread(grads.astype(BF16), "z")).astype(BF16)
    grads = spread(grads, "y").reshape(-1, width)
    grads = spread(grads, "c").reshape(-1, width)
    return grads[: w_in.shape[0]], grads[w_in.shape[0] :]


def solution(mesh):
    grid = Mesh(mesh.devices.reshape(8, 8, 2, 4), ("z", "y", "c", "x"))
    return jax.shard_map(
        local,
        mesh=grid,
        in_specs=(
            P(DP, None),
            P(DP, None),
            P(None, "x"),
            P("x", None),
            P(DP, None),
            P(DP),
            P(),
        ),
        out_specs=(P(None, "x"), P("x", None)),
        check_vma=False,
    )
```

time: 762 us -> 205 us (0.27)
  blocking collectives: 529 us -> 73 us
  local copies, waits for them, and re-layouts: 100 us -> 14.2 us
  waiting for transfers between devices: 60.3 us -> 35.3 us
  starting transfers between devices: 22.5 us -> 38.8 us
  other arithmetic: 22.3 us -> 12.6 us
  matrix products: 8.08 us -> 16 us
    psum x1 -> x0, blocking collectives: 500 us -> none  [local(): summed_in, summed_out = lax.psum((in_term, out_term), 'dp')]
    scatter x2 -> x0, local copies, waits for them, and re-layouts: 80 us -> none  [the longest x1 55.4 us: local(): outgoing = outgoing.at[owners, slots].set(pair_neg.reshape(-1, width))]
    all_to_all x1 -> x6, blocking collectives: 29.7 us -> 73 us  [exchange(): return lax.all_to_all(blocks, axes, split_axis=0, concat_axis=0, tiled=True)]
    all_to_all x2 -> x3, waiting for transfers between devices: 58.7 us -> 27.4 us  [exchange(): return lax.all_to_all(blocks, axes, split_axis=0, concat_axis=0, tiled=True)]
    all_to_all x2 -> x3, starting transfers between devices: 22.5 us -> 38.7 us  [exchange(): return lax.all_to_all(blocks, axes, split_axis=0, concat_axis=0, tiled=True)]
    scatter-add x2 -> x0, other arithmetic: 15.9 us -> none  [the longest x1 13 us: local(): item_grad.at[asked_rows.reshape(-1)]]
    gather x4 -> x2, local copies, waits for them, and re-layouts: 14.4 us -> 3.71 us  [the longest x1 3.14 us: request_codes(): rows = jnp.take(owner_map, negatives.reshape(-1), axis=0)]
    dot_general x5 -> x13, matrix products: 8.08 us -> 16 us  [the longest x2 5.03 us: back(): lax.dot_general(feats, pre_grad, (((0,), (0,)), ((), ())), preferred_elem...]
  transfers between devices with their start and end apart: 3 -> 4, of which waited for: 3 -> 4; matrix products, arithmetic and copies ran while one was open for 4% -> 6% of each run, Pallas kernels for 0% -> 0%
where the time goes in v1:
time: 205 us; the launch traced here: 204 us
  blocking collectives  73 us (36%)
  starting transfers between devices  38.8 us (19%)
  waiting for transfers between devices  35.3 us (17%)
  matrix products  16 us (8%)
  between operations  14.5 us (7%)
  local copies, waits for them, and re-layouts  14.2 us (7%)
  other arithmetic  12.6 us (6%)
    all_to_all x6, blocking collectives, exchange(): return lax.all_to_all(blocks, axes, split_axis=0, concat_axis=0, tiled=True)  73 us
    all_to_all x3, starting transfers between devices, exchange(): return lax.all_to_all(blocks, axes, split_axis=0, concat_axis=0, tiled=True)  38.7 us
    all_to_all x3, waiting for transfers between devices, exchange(): return lax.all_to_all(blocks, axes, split_axis=0, concat_axis=0, tiled=True)  27.4 us
    all_gather x1, waiting for transfers between devices, local(): item_emb = lax.all_gather(own[:share], 'x', axis=0, tiled=True)  7.19 us
    unnamed x34, local copies, waits for them, and re-layouts  5.44 us
    dot_general x2, matrix products, back(): lax.dot_general(feats, pre_grad, (((0,), (0,)), ((), ())), preferred_elem...  5.03 us
    reduce_sum x1, other arithmetic, local(): jnp.sum((wanted[:, None, :] == row_id[None, :, None] + 1).astype(F32), 0)  4.75 us
  transfers between devices with their start and end apart: 4, of which 4 were waited for; matrix products, arithmetic and copies ran while one was open for 6% of the time, Pallas kernels for 0%

profile of v1, /device:TPU:1, one launch (start us, length us, event | category | flops | bytes accessed | tf_op | source)
XLA Modules:
  0.0 204.5 jit_solution(251496680617814727)
XLA Ops:
  7.2 1.4 fusion.11
  8.9 1.8 fusion.4
  11.2 1.1 pad_maximum_fusion
  12.4 4.8 %all-to-all-start = ((f32[4,264,256]{2,1,0:T(8,128)}), f32[4,264,256]{2,1,0:T(8,128)}, u32[]{:S(2)}, u32[]{:S(2)}) async-start(f32[4,264,256]{2,1,0:T(8,128)} %pad_maximum_fusion), calls=%async_computation | async-start | bytes 2162688 | tf_op jit(solution)/shard_map/all_to_all | solution.py:14
  17.2 3.1 %gather_fusion = s32[512]{0:T(512)S(1)} fusion(s32[131072]{0:T(1024)S(1)} %copy-done.1, s32[1024]{0:T(1024)S(1)} %pad_clamp_fusion.2), kind=kCustom, calls=%fused_computation | custom fusion | bytes 6144 | tf_op jit(solution)/shard_map/jit(_take)/gather | solution.py:28
  21.5 5.7 %all-to-all-done = f32[4,264,256]{2,1,0:T(8,128)} async-done(((f32[4,264,256]{2,1,0:T(8,128)}), f32[4,264,256]{2,1,0:T(8,128)}, u32[]{:S(2)}, u32[]{:S(2)}) %all-to-all-start) | async-done | bytes 1081376 | tf_op jit(solution)/shard_map/all_to_all | solution.py:14
  27.2 1.3 reduce_sum.101
  30.1 0.7 maximum_bitcast_fusion
  31.3 1.7 reduce.3
  33.1 1.1 reshape.252
  34.1 23.6 %all-to-all-start.1 = ((bf16[128,2,576]{2,1,0:T(2,128)(2,1)}), bf16[128,2,576]{2,1,0:T(2,128)(2,1)S(1)}, u32[]{:S(2)}, u32[]{:S(2)}) async-start(bf16[128,2,576]{2,1,0:T(2,128)(2,1)} %reshape.252), calls=%async_computation.1 | async-start | bytes 655360 | tf_op jit(solution)/shard_map/all_to_all | solution.py:14
  59.8 14.5 %all-to-all-done.1 = bf16[128,2,576]{2,1,0:T(2,128)(2,1)S(1)} async-done(((bf16[128,2,576]{2,1,0:T(2,128)(2,1)}), bf16[128,2,576]{2,1,0:T(2,128)(2,1)S(1)}, u32[]{:S(2)}, u32[]{:S(2)}) %all-to-all-start.1) | async-done | bytes 294944 | tf_op jit(solution)/shard_map/all_to_all | solution.py:14
  74.9 0.9 reshape.220
  76.1 4.8 %convert_reduce_fusion = f32[1024,512]{1,0:T(8,128)} fusion(s32[16,512]{1,0:T(8,128)S(1)} %copy.33, s32[1024]{0:T(1024)S(1)} %iota_add_fusion), kind=kLoop, calls=%fused_computation.3 | loop fusion | flops 24641536 | bytes 2134016 | tf_op jit(solution)/shard_map/reduce_sum | solution.py:106
  80.8 7.2 %all-gather.2.cloned.1.call-done = f32[1024,256]{1,0:T(8,128)} async-done(((f32[256,256]{1,0:T(8,128)}), f32[1024,256]{1,0:T(8,128)}) %all-gather.2.cloned.1.call-update) | async-done | bytes 1048592 | tf_op jit(solution)/shard_map/all_gather | solution.py:80
  88.0 1.3 convert_element_type.127
  89.3 2.3 %fusion.50 = (f32[512]{0:T(512)S(1)}, f32[1024,512]{1,0:T(8,128)S(1)}) fusion(bf16[1024,256]{1,0:T(8,128)(2,1)S(1)} %convert_element_type.127, bf16[512,256]{1,0:T(8,128)(2,1)S(1)} %copy-done.6, f32[1024,512]{1,0:T(8,128)} %convert_reduce_fusion, s32[512]{0:T(512)S(1)} %and_select_fusion.1), kind=kOutput, calls=%fused_computation.123 | convolution fusion | flops 271580672 | bytes 4984832 | tf_op jit(solution)/shard_map/dot_general | solution.py:107
  91.6 1.3 copy-done.2
  93.6 16.9 %all_to_all.52 = bf16[8,72,256]{2,1,0:T(8,128)(2,1)S(1)} all-to-all(bf16[8,72,256]{2,1,0:T(8,128)(2,1)S(1)} %pad_maximum_fusion.2), channel_id=1, replica_groups=mesh['z'=8,'y'=8,'c'=2,'x'=4] {'z'}, dimensions={0} | all-to-all | bytes 589824 | tf_op jit(solution)/shard_map/all_to_all | solution.py:14
  111.2 10.3 %all-to-all-start.3 = ((bf16[16,8,256]{2,1,0:T(8,128)(2,1)}), bf16[16,8,256]{2,1,0:T(8,128)(2,1)S(1)}, u32[]{:S(2)}, u32[]{:S(2)}) async-start(bf16[16,8,256]{2,1,0:T(8,128)(2,1)} %pad_maximum_fusion.3), calls=%async_computation.3 | async-start | bytes 131072 | tf_op jit(solution)/shard_map/all_to_all | solution.py:14
  122.1 7.2 %all-to-all-done.3 = bf16[16,8,256]{2,1,0:T(8,128)(2,1)S(1)} async-done(((bf16[16,8,256]{2,1,0:T(8,128)(2,1)}), bf16[16,8,256]{2,1,0:T(8,128)(2,1)S(1)}, u32[]{:S(2)}, u32[]{:S(2)}) %all-to-all-start.3) | async-done | bytes 65568 | tf_op jit(solution)/shard_map/all_to_all | solution.py:14
  129.4 2.6 %fusion.3 = bf16[1024,256]{1,0:T(8,128)(2,1)S(1)} fusion(bf16[512,256]{1,0:T(8,128)(2,1)} %reshape.220, f32[1024,256]{1,0:T(8,128)} %all-gather.2.cloned.1.call-done, f32[1024,512]{1,0:T(8,128)} %copy-done.2, f32[512]{0:T(512)S(1)} %bitcast.70, s32[512]{0:T(512)S(1)} %and_select_fusion.1), kind=kOutput, calls=%fused_computation.14 | convolution fusion | flops 272629760 | bytes 3936256 | tf_op jit(solution)/shard_map/dot_general | solution.py:154
  132.0 0.8 copy-done.7
  133.2 3.2 %fusion.8 = f32[256,1024]{1,0:T(8,128)} fusion(bf16[1024,1024]{1,0:T(8,128)(2,1)S(1)} %copy-done, bf16[1024,256]{1,0:T(8,128)(2,1)} %copy-done.7, bf16[256,256]{1,0:T(8,128)(2,1)S(1)} %copy-done.4, bf16[1024,256]{1,0:T(8,128)(2,1)S(1)} %fusion.4), kind=kOutput, calls=%fused_computation.19 | convolution fusion | flops 671875072 | bytes 4325376 | tf_op jit(solution)/shard_map/dot_general | solution.py:162
  136.5 1.0 fusion.9
  137.5 1.8 fusion.7
  139.4 4.1 %all_to_all.53 = bf16[2,640,256]{1,2,0:T(8,128)(2,1)S(1)} all-to-all(bf16[2,640,256]{1,2,0:T(8,128)(2,1)S(1)} %bitcast.60), channel_id=1, replica_groups=mesh['z'=8,'y'=8,'c'=2,'x'=4] {'c'}, dimensions={0} | all-to-all | bytes 1310720 | tf_op jit(solution)/shard_map/all_to_all | solution.py:14
  143.8 16.1 %all_to_all.54 = bf16[8,80,256]{2,1,0:T(8,128)(2,1)S(1)} all-to-all(bf16[8,80,256]{2,1,0:T(8,128)(2,1)S(1)} %bitcast.61), channel_id=1, replica_groups=mesh['z'=8,'y'=8,'c'=2,'x'=4] {'y'}, dimensions={0} | all-to-all | bytes 655360 | tf_op jit(solution)/shard_map/all_to_all | solution.py:14
  160.0 15.5 %all_to_all.55 = bf16[8,80,256]{2,1,0:T(8,128)(2,1)S(1)} all-to-all(bf16[8,80,256]{2,1,0:T(8,128)(2,1)S(1)} %broadcast_in_dim.135), channel_id=1, replica_groups=mesh['z'=8,'y'=8,'c'=2,'x'=4] {'z'}, dimensions={0} | all-to-all | bytes 655360 | tf_op jit(solution)/shard_map/all_to_all | solution.py:14
  175.6 13.7 %all_to_all.56 = bf16[8,80,256]{2,1,0:T(8,128)(2,1)S(1)} all-to-all(bf16[8,80,256]{2,1,0:T(8,128)(2,1)S(1)} %broadcast_in_dim.136), channel_id=1, replica_groups=mesh['z'=8,'y'=8,'c'=2,'x'=4] {'y'}, dimensions={0} | all-to-all | bytes 655360 | tf_op jit(solution)/shard_map/all_to_all | solution.py:14
  189.3 6.8 %all_to_all.57 = bf16[2,640,256]{2,1,0:T(8,128)(2,1)S(1)} all-to-all(bf16[2,640,256]{2,1,0:T(8,128)(2,1)S(1)} %broadcast_in_dim.138), channel_id=1, replica_groups=mesh['z'=8,'y'=8,'c'=2,'x'=4] {'c'}, dimensions={0} | all-to-all | bytes 1310720 | tf_op jit(solution)/shard_map/all_to_all | solution.py:14
  196.8 0.8 slice.81
  (92 shorter events, 10.4 us)
Async XLA Ops:
  7.2 1.8 copy-start
  8.9 1.8 copy-start.3
  11.2 6.0 %copy-start.9 = (s32[4,128]{1,0:T(4,128)S(1)}, s32[4,128]{1,0:T(4,128)}, u32[]{:S(2)}) copy-start(s32[4,128]{1,0:T(4,128)} %param.11) | copy-start | bytes 6148
  11.2 6.0 %copy-start.1 = (s32[131072]{0:T(1024)S(1)}, s32[131072]{0:T(1024)}, u32[]{:S(2)}) copy-start(s32[131072]{0:T(1024)} %param.13) | copy-start | bytes 1572868
  12.4 14.9 %all-to-all-start = ((f32[4,264,256]{2,1,0:T(8,128)}), f32[4,264,256]{2,1,0:T(8,128)}, u32[]{:S(2)}, u32[]{:S(2)}) async-start(f32[4,264,256]{2,1,0:T(8,128)} %pad_maximum_fusion), calls=%async_computation | async-start | bytes 2162688 | tf_op jit(solution)/shard_map/all_to_all | solution.py:14
  17.2 4.3 %copy-start.12 = (s32[4]{0:T(128)S(1)}, s32[4]{0:T(128)}, u32[]{:S(2)}) copy-start(s32[4]{0:T(128)} %param.12) | copy-start | bytes 52
  28.6 30.5 %copy-start.13 = (s32[4]{0:T(128)S(1)}, s32[4]{0:T(128)}, u32[]{:S(2)}) copy-start(s32[4]{0:T(128)} %param.12) | copy-start | bytes 52
  28.6 0.7 copy-start.5
  34.1 40.2 %all-to-all-start.1 = ((bf16[128,2,576]{2,1,0:T(2,128)(2,1)}), bf16[128,2,576]{2,1,0:T(2,128)(2,1)S(1)}, u32[]{:S(2)}, u32[]{:S(2)}) async-start(bf16[128,2,576]{2,1,0:T(2,128)(2,1)} %reshape.252), calls=%async_computation.1 | async-start | bytes 655360 | tf_op jit(solution)/shard_map/all_to_all | solution.py:14
  57.7 30.3 %all-gather.2.cloned.1.call-start = ((), (), s32[]{:S(2)}) async-start(), calls=%async_computation.9 | async-start | bytes 1310720 | tf_op jit(solution)/shard_map/all_gather | solution.py:80
  59.1 0.6 copy-start.10
  75.8 13.5 %copy-start.6 = (bf16[512,256]{1,0:T(8,128)(2,1)S(1)}, bf16[512,256]{1,0:T(8,128)(2,1)}, u32[]{:S(2)}) copy-start(bf16[512,256]{1,0:T(8,128)(2,1)} %reshape.220) | copy-start | bytes 786436
  91.6 1.4 copy-start.2
  93.0 28.6 %copy-start.11 = (s32[4]{0:T(128)S(1)}, s32[4]{0:T(128)}, u32[]{:S(2)}) copy-start(s32[4]{0:T(128)} %copy-done.10) | copy-start | bytes 52
  111.2 18.1 %all-to-all-start.3 = ((bf16[16,8,256]{2,1,0:T(8,128)(2,1)}), bf16[16,8,256]{2,1,0:T(8,128)(2,1)S(1)}, u32[]{:S(2)}, u32[]{:S(2)}) async-start(bf16[16,8,256]{2,1,0:T(8,128)(2,1)} %pad_maximum_fusion.3), calls=%async_computation.3 | async-start | bytes 131072 | tf_op jit(solution)/shard_map/all_to_all | solution.py:14
  129.4 3.8 %copy-start.4 = (bf16[256,256]{1,0:T(8,128)(2,1)S(1)}, bf16[256,256]{1,0:T(8,128)(2,1)}, u32[]{:S(2)}) copy-start(bf16[256,256]{1,0:T(8,128)(2,1)} %param.10) | copy-start | bytes 393220
  132.0 0.8 copy-start.7
  133.2 4.3 %copy-start.8 = (bf16[4,1024]{1,0:T(4,128)(2,1)S(1)}, bf16[4,1024]{1,0:T(4,128)(2,1)}, u32[]{:S(2)}) copy-start(bf16[4,1024]{1,0:T(4,128)(2,1)} %param.7) | copy-start | bytes 24580
Sparse Core Ops, SparseCore 0:
  60.7 27.3 all-gather.1

commit v2 on v1

v2 whole, which is shorter than its diff:
```python
import functools
import math

import jax
import jax.numpy as jnp
from jax import lax
from jax.experimental import pallas as pl
from jax.experimental.pallas import tpu as pltpu
from jax.sharding import Mesh, PartitionSpec as P

F32 = jnp.float32
BF16 = jnp.bfloat16
DP = ("z", "y", "c")
YCZ = ("y", "c", "z")
ROWS = 256
VMEM = 48 * 1024 * 1024


def exchange(blocks, axes):
    return lax.all_to_all(blocks, axes, split_axis=0, concat_axis=0, tiled=True)


def spread(block, axes):
    count = lax.axis_size(axes)
    return exchange(jnp.broadcast_to(block[None], (count,) + block.shape), axes)


def total(blocks):
    return jnp.sum(blocks.astype(F32), 0)


def dot(a, b):
    return jnp.dot(a, b, preferred_element_type=F32)


def dot_rows(a, b):
    return lax.dot_general(a, b, (((0,), (0,)), ((), ())), preferred_element_type=F32)


def dot_lanes(a, b):
    return lax.dot_general(a, b, (((1,), (1,)), ((), ())), preferred_element_type=F32)


def forward_kernel(q_ref, x_ref, w_in_ref, w_out_ref, part_ref, hid_ref, hid_q_ref, keep, rows):
    @pl.when(pl.program_id(0) == 0)
    def _():
        few = q_ref.shape[0]
        hid_q = jnp.maximum(dot(q_ref[...], w_in_ref[...]), 0.0)
        rows[...] = jnp.zeros_like(rows)
        rows[:few, :] = hid_q
        hid_q_ref[...] = rows[...].astype(BF16)
        keep[...] = dot(hid_q_ref[...], w_out_ref[...])

    hid = jnp.maximum(dot(x_ref[...], w_in_ref[...]), 0.0).astype(BF16)
    hid_ref[...] = hid
    part_ref[0, : hid.shape[0], :] = dot(hid, w_out_ref[...])
    part_ref[0, hid.shape[0] :, :] = keep[:8, :]


def forward(query_feats, item_feats, w_in, w_out):
    few, feats = query_feats.shape
    items = item_feats.shape[0]
    units = w_in.shape[1]
    width = w_out.shape[1]
    steps = items // ROWS
    return pl.pallas_call(
        forward_kernel,
        grid=(steps,),
        in_specs=[
            pl.BlockSpec((few, feats), lambda i: (0, 0)),
            pl.BlockSpec((ROWS, feats), lambda i: (i, 0)),
            pl.BlockSpec((feats, units), lambda i: (0, 0)),
            pl.BlockSpec((units, width), lambda i: (0, 0)),
        ],
        out_specs=[
            pl.BlockSpec((1, ROWS + 8, width), lambda i: (i, 0, 0)),
            pl.BlockSpec((ROWS, units), lambda i: (i, 0)),
            pl.BlockSpec((16, units), lambda i: (0, 0)),
        ],
        out_shape=[
            jax.ShapeDtypeStruct((steps, ROWS + 8, width), F32),
            jax.ShapeDtypeStruct((items, units), BF16),
            jax.ShapeDtypeStruct((16, units), BF16),
        ],
        scratch_shapes=[pltpu.VMEM((16, width), F32), pltpu.VMEM((16, units), F32)],
        compiler_params=pltpu.CompilerParams(vmem_limit_bytes=VMEM),
    )(query_feats, item_feats, w_in, w_out)


def position_row(info_ref, queries, few):
    lane = lax.broadcasted_iota(jnp.int32, (1, queries), 1)
    row = jnp.zeros((1, queries), F32)
    for i in range(few):
        row = jnp.where(lane == info_ref[few] + i, (info_ref[i] + 1).astype(F32), row)
    return row


def row_ids(shape):
    first = pl.program_id(0) * shape[0] + 1
    return (lax.broadcasted_iota(jnp.int32, shape, 0) + first).astype(F32)


def score_kernel(few, scale, info_ref, e_ref, msg_ref, weight_ref, u_ref, d_ref, codes, total_u, total_d):
    step = pl.program_id(0)
    queries = msg_ref.shape[0]
    width = e_ref.shape[1]
    slots = codes.shape[0] - 8

    @pl.when(step == 0)
    def _():
        turned = msg_ref[:, width:].astype(F32).T
        codes[:slots, :] = turned[:slots] * 32.0 + turned[slots : 2 * slots]
        codes[slots:, :] = jnp.broadcast_to(position_row(info_ref, queries, few), (8, queries))
        total_u[...] = jnp.zeros_like(total_u)
        total_d[...] = jnp.zeros_like(total_d)

    e16 = e_ref[...].astype(BF16)
    scores = dot_lanes(e16, msg_ref[:, :width])
    ids = row_ids(scores.shape)
    count = jnp.zeros_like(scores)
    for s in range(slots + 1):
        count = count + jnp.where(codes[s : s + 1, :] == ids, 1.0, 0.0)
    weight = count * jnp.exp(scale * scores)
    weight_ref[...] = weight
    total_d[...] += jnp.sum(weight, 0, keepdims=True)
    total_u[...] += dot_rows(weight.astype(BF16), e16)

    @pl.when(step == pl.num_programs(0) - 1)
    def _():
        u_ref[...] = total_u[...].astype(BF16)
        d_ref[...] = total_d[...]


def score(info, item_emb, message, few, capacity, scale):
    items, width = item_emb.shape
    queries, wide = message.shape
    return pl.pallas_call(
        functools.partial(score_kernel, few, scale),
        grid=(items // ROWS,),
        in_specs=[
            pl.BlockSpec(memory_space=pltpu.SMEM),
            pl.BlockSpec((ROWS, width), lambda i: (i, 0)),
            pl.BlockSpec((queries, wide), lambda i: (0, 0)),
        ],
        out_specs=[
            pl.BlockSpec((ROWS, queries), lambda i: (i, 0)),
            pl.BlockSpec((queries, width), lambda i: (0, 0)),
            pl.BlockSpec((1, queries), lambda i: (0, 0)),
        ],
        out_shape=[
            jax.ShapeDtypeStruct((items, queries), F32),
            jax.ShapeDtypeStruct((queries, width), BF16),
            jax.ShapeDtypeStruct((1, queries), F32),
        ],
        scratch_shapes=[
            pltpu.VMEM((capacity + 8, queries), F32),
            pltpu.VMEM((queries, width), F32),
            pltpu.VMEM((1, queries), F32),
        ],
        compiler_params=pltpu.CompilerParams(vmem_limit_bytes=VMEM),
    )(info, item_emb, message)


def backward_kernel(
    few, scale, info_ref, sums_ref, weight_ref, e_ref, msg_ref, hid_ref, x_ref, w_out_ref,
    emb_q_ref, hid_q_ref, q_ref, out_ref, factor, denom, pos, pos_emb, in_total, out_total,
):
    step = pl.program_id(0)
    queries = msg_ref.shape[0]
    width = e_ref.shape[1]
    feats = x_ref.shape[1]

    @pl.when(step == 0)
    def _():
        sums = jnp.sum(sums_ref[...].astype(F32), 0)
        d = sums[few : few + 2] + sums[few + 2 : few + 4]
        d = jnp.concatenate([d[0:1], d[1:2]], 1)
        denom[...] = d
        factor[...] = scale / d
        pos[...] = position_row(info_ref, queries, few)
        pos_emb[...] = jnp.zeros_like(pos_emb)
        in_total[...] = jnp.zeros_like(in_total)
        out_total[...] = jnp.zeros_like(out_total)

    def accumulate(hid, grad, feats_rows):
        out_total[...] += dot_rows(hid, grad)
        hid_grad = dot_lanes(grad, w_out_ref[...])
        pre_grad = jnp.where(hid > 0, hid_grad, 0.0).astype(BF16)
        in_total[...] += dot_rows(pre_grad, feats_rows)

    e = e_ref[...]
    weight = weight_ref[...]
    hot = jnp.where(pos[...] == row_ids(weight.shape), scale, 0.0)
    coefficient = (weight * factor[...] - hot).astype(BF16)
    item_grad = dot(coefficient, msg_ref[:, :width])
    accumulate(hid_ref[...], (item_grad * (1.0 - e * e)).astype(BF16), x_ref[...])

    lane = lax.broadcasted_iota(jnp.int32, (16, ROWS), 1) + step * ROWS
    line = lax.broadcasted_iota(jnp.int32, (16, ROWS), 0)
    picked = jnp.zeros((16, ROWS), F32)
    for i in range(few):
        picked = jnp.where((line == i) & (lane == info_ref[i]), 1.0, picked)
    pos_emb[...] += dot(picked.astype(BF16), e.astype(BF16))

    @pl.when(step == pl.num_programs(0) - 1)
    def _():
        sums = jnp.sum(sums_ref[...].astype(F32), 0)
        sums = jnp.concatenate([sums, jnp.zeros_like(sums)], 0)
        line = lax.broadcasted_iota(jnp.int32, (16, queries), 0)
        column = lax.broadcasted_iota(jnp.int32, (16, queries), 1)
        own_d = jnp.sum(jnp.where(column == line + info_ref[few], denom[...], 0.0), 1, keepdims=True)
        live = lax.broadcasted_iota(jnp.int32, sums.shape, 0) < few
        emb_q = emb_q_ref[...]
        grad = scale * (sums / own_d - pos_emb[...]) * (1.0 - emb_q * emb_q)
        accumulate(hid_q_ref[...], jnp.where(live, grad, 0.0).astype(BF16), q_ref[...])
        out_ref[:feats, :] = in_total[...].astype(BF16).T
        out_ref[feats:, :] = out_total[...].astype(BF16)


def backward(info, sums, weight, item_emb, message, hidden, item_feats, w_out, emb_q, hidden_q, feats_q, few, scale):
    items, width = item_emb.shape
    queries, wide = message.shape
    feats = item_feats.shape[1]
    units = hidden.shape[1]

    def whole(a):
        return pl.BlockSpec(a.shape, lambda i: (0,) * a.ndim)

    def part(a):
        return pl.BlockSpec((ROWS, a.shape[1]), lambda i: (i, 0))

    return pl.pallas_call(
        functools.partial(backward_kernel, few, scale),
        grid=(items // ROWS,),
        in_specs=[
            pl.BlockSpec(memory_space=pltpu.SMEM),
            whole(sums),
            part(weight),
            part(item_emb),
            whole(message),
            part(hidden),
            part(item_feats),
            whole(w_out),
            whole(emb_q),
            whole(hidden_q),
            whole(feats_q),
        ],
        out_specs=pl.BlockSpec((feats + units, width), lambda i: (0, 0)),
        out_shape=jax.ShapeDtypeStruct((feats + units, width), BF16),
        scratch_shapes=[
            pltpu.VMEM((1, queries), F32),
            pltpu.VMEM((1, queries), F32),
            pltpu.VMEM((1, queries), F32),
            pltpu.VMEM((16, width), F32),
            pltpu.VMEM((units, feats), F32),
            pltpu.VMEM((units, width), F32),
        ],
        compiler_params=pltpu.CompilerParams(vmem_limit_bytes=VMEM),
    )(info, sums, weight, item_emb, message, hidden, item_feats, w_out, emb_q, hidden_q, feats_q)


def request_codes(rows, query_count, item_count, capacity, order, dp_count):
    pairs = rows.shape[0]
    owners = rows // item_count
    code = rows - owners * item_count + 1
    owner_hot = order(owners)[:, None] == jnp.arange(dp_count, dtype=jnp.int32)[None, :]
    earlier = jnp.arange(pairs)[:, None] >= jnp.arange(pairs)[None, :]
    running = dot(earlier.astype(BF16), owner_hot.astype(BF16))
    slot = jnp.sum(jnp.where(owner_hot, running, 0.0), 1).astype(jnp.int32) - 1
    query = jnp.arange(pairs, dtype=jnp.int32) // (pairs // query_count)
    place = query * 2 * capacity + slot
    places = jnp.arange(query_count * 2 * capacity, dtype=jnp.int32)[None, :]
    high = jnp.where(place[:, None] == places, (code // 32)[:, None], 0)
    low = jnp.where(place[:, None] + capacity == places, (code % 32)[:, None], 0)
    return dot_rows(owner_hot.astype(BF16), (high + low).astype(BF16)).astype(BF16)


def local(query_feats, item_feats, w_in, w_out, negatives, positives, owner_map):
    dp_count = lax.axis_size(DP)
    own_index = lax.axis_index(DP)
    z_count = lax.axis_size("z")
    x_count = lax.axis_size("x")
    yc_count = dp_count // z_count
    few = query_feats.shape[0]
    item_count = item_feats.shape[0]
    width = w_out.shape[1]
    negative_count = negatives.shape[1]
    scale = 4.0 / math.sqrt(width)
    capacity = 4 * few * negative_count // dp_count
    queries = few * dp_count

    blocks, hidden, hidden_q = forward(query_feats, item_feats, w_in, w_out)
    arrived = exchange(blocks, "x")

    named = jnp.concatenate([negatives.reshape(-1), positives])
    rows = jnp.take(owner_map, named, axis=0)
    pos_local = rows[few * negative_count :] - own_index * item_count
    info = jnp.concatenate([pos_local, lax.axis_index(YCZ).reshape(1) * few])
    codes = request_codes(
        rows[: few * negative_count],
        few,
        item_count,
        capacity,
        lambda o: (o % yc_count) * z_count + o // yc_count,
        dp_count,
    )
    codes = codes.reshape(dp_count, few, 2 * capacity)
    codes = jnp.pad(codes, ((0, 0), (0, 0), (0, 128 - 2 * capacity)))

    own = jnp.tanh(total(arrived[:, :ROWS]))
    own_q = jnp.tanh(total(arrived[:, ROWS:]))
    sent_q = jnp.broadcast_to(own_q[None, :few].astype(BF16), (dp_count, few, width))
    message = exchange(jnp.concatenate([sent_q, codes], 2), YCZ)
    message = message.reshape(queries, width + 128)
    item_emb = spread(own, "x").reshape(item_count, width)

    weight, part_u, part_d = score(info, item_emb, message, few, capacity, scale)

    def split(d):
        high = d.astype(BF16)
        low = (d - high.astype(F32)).astype(BF16)
        return jnp.concatenate([high.reshape(-1, width), low.reshape(-1, width)], 0)

    d_rows = queries // width
    mine = queries // yc_count
    first = total(
        exchange(
            jnp.concatenate(
                [
                    part_u.reshape(yc_count, mine, width),
                    jnp.broadcast_to(
                        jnp.pad(split(part_d), ((0, 8 - 2 * d_rows), (0, 0)))[None], (yc_count, 8, width)
                    ),
                ],
                1,
            ),
            ("y", "c"),
        )
    )
    d_part = first[mine : mine + d_rows] + first[mine + d_rows : mine + 2 * d_rows]
    sums = exchange(
        jnp.concatenate(
            [
                first[:mine].astype(BF16).reshape(z_count, few, width),
                jnp.broadcast_to(split(d_part)[None], (z_count, 2 * d_rows, width)),
            ],
            1,
        ),
        "z",
    )
    emb_q = jnp.pad(own_q, ((0, 8), (0, 0)))
    feats_q = jnp.pad(query_feats, ((0, 16 - few), (0, 0)))
    grads = backward(
        info, sums, weight, item_emb, message, hidden, item_feats, w_out, emb_q, hidden_q, feats_q, few, scale
    )
    depth = grads.shape[0]
    c_count, y_count = lax.axis_size("c"), lax.axis_size("y")
    grads = total(exchange(grads.reshape(c_count, depth // c_count, width), "c"))
    grads = total(exchange(grads.astype(BF16).reshape(y_count, -1, width), "y"))
    grads = total(spread(grads.astype(BF16), "z")).astype(BF16)
    grads = spread(grads, "y").reshape(-1, width)
    grads = spread(grads, "c").reshape(-1, width)
    return grads[: w_in.shape[0]], grads[w_in.shape[0] :]


def solution(mesh):
    grid = Mesh(mesh.devices.reshape(8, 8, 2, 4), ("z", "y", "c", "x"))
    return jax.shard_map(
        local,
        mesh=grid,
        in_specs=(
            P(DP, None),
            P(DP, None),
            P(None, "x"),
            P("x", None),
            P(DP, None),
            P(DP),
            P(),
        ),
        out_specs=(P(None, "x"), P("x", None)),
        check_vma=False,
    )
```

time: 205 us -> 185 us (0.902)
  matrix products: 16 us -> 0.9 us
  Pallas kernels: 0 us -> 14.4 us
  between operations: 14.5 us -> 0.92 us
  other arithmetic: 12.6 us -> 2.3 us
  waiting for transfers between devices: 35.3 us -> 45.3 us
  starting transfers between devices: 38.8 us -> 35.2 us
  blocking collectives: 73 us -> 70.9 us
    all_to_all x3 -> x4, waiting for transfers between devices: 27.4 us -> 45.3 us  [exchange(): return lax.all_to_all(blocks, axes, split_axis=0, concat_axis=0, tiled=True)]
    dot_general x13 -> x2, matrix products: 16 us -> 0.9 us  [the longest x1 0.59 us: dot_rows(): lax.dot_general(a, b, (((0,), (0,)), ((), ())), preferred_element_type=F32)]
    pallas_call x0 -> x3, Pallas kernels: none -> 14.4 us  [the longest x1 5.76 us: score(): pl.pallas_call(functools.partial(score_kernel, few, scale), grid=(items /...]
    all_gather x1 -> x0, waiting for transfers between devices: 7.19 us -> none  [local(): item_emb = lax.all_gather(own[:share], 'x', axis=0, tiled=True)]
    reduce_sum x2 -> x0, other arithmetic: 4.84 us -> none  [the longest x1 4.75 us: local(): jnp.sum((wanted[:, None, :] == row_id[None, :, None] + 1).astype(F32), 0)]
    all_to_all x3 -> x4, starting transfers between devices: 38.7 us -> 35.2 us  [exchange(): return lax.all_to_all(blocks, axes, split_axis=0, concat_axis=0, tiled=True)]
    all_to_all x2 -> x0, other arithmetic: 2.47 us -> none  [exchange(): return lax.all_to_all(blocks, axes, split_axis=0, concat_axis=0, tiled=True)]
    all_to_all x6, blocking collectives: 73 us -> 70.9 us  [exchange(): return lax.all_to_all(blocks, axes, split_axis=0, concat_axis=0, tiled=True)]
  transfers between devices with their start and end apart: 4 -> 4, of which waited for: 4 -> 4; matrix products, arithmetic and copies ran while one was open for 6% -> 3% of each run, Pallas kernels for 0% -> 0%
where the time goes in v2:
time: 185 us; the launch traced here: 184 us
  blocking collectives  70.9 us (38%)
  waiting for transfers between devices  45.3 us (24%)
  starting transfers between devices  35.2 us (19%)
  Pallas kernels  14.4 us (8%)
  local copies, waits for them, and re-layouts  13.9 us (8%)
  other arithmetic  2.3 us (1%)
    all_to_all x6, blocking collectives, exchange(): return lax.all_to_all(blocks, axes, split_axis=0, concat_axis=0, tiled=True)  70.9 us
    all_to_all x4, waiting for transfers between devices, exchange(): return lax.all_to_all(blocks, axes, split_axis=0, concat_axis=0, tiled=True)  45.3 us
    all_to_all x4, starting transfers between devices, exchange(): return lax.all_to_all(blocks, axes, split_axis=0, concat_axis=0, tiled=True)  35.2 us
    unnamed x22, local copies, waits for them, and re-layouts  7.24 us
    pallas_call x1, Pallas kernels, score(): pl.pallas_call(functools.partial(score_kernel, few, scale), grid=(items /...  5.76 us
    pallas_call x1, Pallas kernels, backward(): pl.pallas_call(functools.partial(backward_kernel, few, scale), grid=(item...  5.5 us
  transfers between devices with their start and end apart: 4, of which 4 were waited for; matrix products, arithmetic and copies ran while one was open for 3% of the time, Pallas kernels for 0%

profile of v2, /device:TPU:1, one launch (start us, length us, event | category | flops | bytes accessed | tf_op | source)
XLA Modules:
  0.0 183.9 jit_solution(4207025248822596560)
XLA Ops:
  0.7 1.6 copy-done.1
  2.3 1.0 copy-done.4
  3.3 0.9 copy-done.5
  4.2 0.7 copy-done.7
  4.9 3.1 %shard_map.86 = (f32[4,264,256]{2,1,0:T(8,128)}, bf16[1024,256]{1,0:T(8,128)(2,1)S(1)}, bf16[16,256]{1,0:T(8,128)(2,1)S(1)}) custom-call(bf16[4,1024]{1,0:T(4,128)(2,1)S(1)} %copy-done.7, bf16[1024,1024]{1,0:T(8,128)(2,1)S(1)} %copy-done.1, bf16[1024,256]{1,0:T(8,128)(2,1)S(1)} %copy-done.4, bf16[256,256]{1,0:T(8,128)(2,1)S(1)} %copy-done.5), custom_call_target="tpu_custom_call" | custom-call | tf_op jit(solution)/shard_map/pallas_call | solution.py:66
  8.1 5.0 %all-to-all-start = ((f32[4,264,256]{2,1,0:T(8,128)}), f32[4,264,256]{2,1,0:T(8,128)S(1)}, u32[]{:S(2)}, u32[]{:S(2)}) async-start(f32[4,264,256]{2,1,0:T(8,128)} %get-tuple-element.8), calls=%async_computation | async-start | bytes 2162688 | tf_op jit(solution)/shard_map/all_to_all | solution.py:20
  13.1 3.6 %gather_fusion = s32[516]{0:T(1024)S(1)} fusion(s32[131072]{0:T(1024)S(1)} %copy-done, s32[1024]{0:T(1024)S(1)} %pad_clamp_fusion), kind=kCustom, calls=%fused_computation | custom fusion | bytes 6192 | tf_op jit(solution)/shard_map/jit(_take)/gather | solution.py:296
  16.7 0.3 fusion
  17.1 0.6 convolution_convert_fusion
  17.8 5.2 %all-to-all-done = f32[4,264,256]{2,1,0:T(8,128)S(1)} async-done(((f32[4,264,256]{2,1,0:T(8,128)}), f32[4,264,256]{2,1,0:T(8,128)S(1)}, u32[]{:S(2)}, u32[]{:S(2)}) %all-to-all-start) | async-done | bytes 1081376 | tf_op jit(solution)/shard_map/all_to_all | solution.py:20
  23.1 1.0 fusion.2
  24.1 23.4 %all-to-all-start.2 = ((bf16[128,4,384]{2,1,0:T(4,128)(2,1)}), bf16[128,4,384]{2,1,0:T(4,128)(2,1)S(1)}, u32[]{:S(2)}, u32[]{:S(2)}) async-start(bf16[128,4,384]{2,1,0:T(4,128)(2,1)} %fusion.2), calls=%async_computation.2 | async-start | bytes 786432 | tf_op jit(solution)/shard_map/all_to_all | solution.py:20
  47.6 18.0 %all-to-all-done.2 = bf16[128,4,384]{2,1,0:T(4,128)(2,1)S(1)} async-done(((bf16[128,4,384]{2,1,0:T(4,128)(2,1)}), bf16[128,4,384]{2,1,0:T(4,128)(2,1)S(1)}, u32[]{:S(2)}, u32[]{:S(2)}) %all-to-all-start.2) | async-done | bytes 393248 | tf_op jit(solution)/shard_map/all_to_all | solution.py:20
  65.6 1.1 broadcast_in_dim.45
  66.7 3.5 %all-to-all-start.1 = ((f32[4,256,256]{2,1,0:T(8,128)}), f32[4,256,256]{2,1,0:T(8,128)S(1)}, u32[]{:S(2)}, u32[]{:S(2)}) async-start(f32[4,256,256]{2,1,0:T(8,128)} %broadcast_in_dim.45), calls=%async_computation.1 | async-start | bytes 2097152 | tf_op jit(solution)/shard_map/all_to_all | solution.py:20
  70.4 14.9 %all-to-all-done.1 = f32[4,256,256]{2,1,0:T(8,128)S(1)} async-done(((f32[4,256,256]{2,1,0:T(8,128)}), f32[4,256,256]{2,1,0:T(8,128)S(1)}, u32[]{:S(2)}, u32[]{:S(2)}) %all-to-all-start.1) | async-done | bytes 1048608 | tf_op jit(solution)/shard_map/all_to_all | solution.py:20
  85.3 5.8 %shard_map.87 = (f32[1024,512]{1,0:T(8,128)S(1)}, bf16[512,256]{1,0:T(8,128)(2,1)S(1)}, f32[1,512]{1,0:T(1,128)S(1)}) custom-call(s32[5]{0:T(128)S(1)} %pad_add_fusion.info_ref, f32[1024,256]{1,0:T(8,128)S(1)} %bitcast.11, bf16[512,384]{1,0:T(8,128)(2,1)S(1)} %reshape.173.msg_ref), custom_call_target="tpu_custom_call" | custom-call | tf_op jit(solution)/shard_map/pallas_call | solution.py:137
  91.1 1.3 copy-done.2
  92.6 16.5 %all_to_all.50 = bf16[16,40,256]{2,1,0:T(8,128)(2,1)S(1)} all-to-all(bf16[16,40,256]{2,1,0:T(8,128)(2,1)S(1)} %pad_maximum_fusion), channel_id=1, replica_groups=mesh['z'=8,'y'=8,'c'=2,'x'=4] {'y','c'}, dimensions={0} | all-to-all | bytes 655360 | tf_op jit(solution)/shard_map/all_to_all | solution.py:20
  109.2 0.6 pad_maximum_fusion.1
  109.8 3.3 %all-to-all-start.4 = ((bf16[8,8,256]{2,1,0:T(8,128)(2,1)}), bf16[8,8,256]{2,1,0:T(8,128)(2,1)S(1)}, u32[]{:S(2)}, u32[]{:S(2)}) async-start(bf16[8,8,256]{2,1,0:T(8,128)(2,1)} %pad_maximum_fusion.1), calls=%async_computation.4 | async-start | bytes 65536 | tf_op jit(solution)/shard_map/all_to_all | solution.py:20
  113.2 7.2 %all-to-all-done.4.sums_ref = bf16[8,8,256]{2,1,0:T(8,128)(2,1)S(1)} async-done(((bf16[8,8,256]{2,1,0:T(8,128)(2,1)}), bf16[8,8,256]{2,1,0:T(8,128)(2,1)S(1)}, u32[]{:S(2)}, u32[]{:S(2)}) %all-to-all-start.4) | async-done | bytes 32800 | tf_op jit(solution)/shard_map/all_to_all | solution.py:20
  120.4 1.6 copy-done.3
  122.0 5.5 %shard_map.88 = bf16[1280,256]{1,0:T(8,128)(2,1)S(1)} custom-call(s32[5]{0:T(128)S(1)} %pad_add_fusion.info_ref, bf16[8,8,256]{2,1,0:T(8,128)(2,1)S(1)} %all-to-all-done.4.sums_ref, f32[1024,512]{1,0:T(8,128)S(1)} %copy-done.3, f32[1024,256]{1,0:T(8,128)S(1)} %bitcast.12, bf16[512,384]{1,0:T(8,128)(2,1)S(1)} %reshape.173.msg_ref, ...), custom_call_target="tpu_custom_call" | custom-call | tf_op jit(solution)/shard_map/pallas_call | solution.py:232
  127.5 4.3 %all_to_all.51 = bf16[2,640,256]{2,1,0:T(8,128)(2,1)S(1)} all-to-all(bf16[2,640,256]{2,1,0:T(8,128)(2,1)S(1)} %bitcast.13), channel_id=1, replica_groups=mesh['z'=8,'y'=8,'c'=2,'x'=4] {'c'}, dimensions={0} | all-to-all | bytes 1310720 | tf_op jit(solution)/shard_map/all_to_all | solution.py:20
  131.8 0.3 reduce_sum.76
  132.1 15.6 %all_to_all.52 = bf16[8,80,256]{2,1,0:T(8,128)(2,1)S(1)} all-to-all(bf16[8,80,256]{2,1,0:T(8,128)(2,1)S(1)} %bitcast.17), channel_id=1, replica_groups=mesh['z'=8,'y'=8,'c'=2,'x'=4] {'y'}, dimensions={0} | all-to-all | bytes 655360 | tf_op jit(solution)/shard_map/all_to_all | solution.py:20
  147.7 13.4 %all_to_all.53 = bf16[8,80,256]{2,1,0:T(8,128)(2,1)S(1)} all-to-all(bf16[8,80,256]{2,1,0:T(8,128)(2,1)S(1)} %broadcast_in_dim.89), channel_id=1, replica_groups=mesh['z'=8,'y'=8,'c'=2,'x'=4] {'z'}, dimensions={0} | all-to-all | bytes 655360 | tf_op jit(solution)/shard_map/all_to_all | solution.py:20
  161.2 12.9 %all_to_all.54 = bf16[8,80,256]{2,1,0:T(8,128)(2,1)S(1)} all-to-all(bf16[8,80,256]{2,1,0:T(8,128)(2,1)S(1)} %broadcast_in_dim.90), channel_id=1, replica_groups=mesh['z'=8,'y'=8,'c'=2,'x'=4] {'y'}, dimensions={0} | all-to-all | bytes 655360 | tf_op jit(solution)/shard_map/all_to_all | solution.py:20
  174.1 8.2 %all_to_all.55 = bf16[2,640,256]{2,1,0:T(8,128)(2,1)S(1)} all-to-all(bf16[2,640,256]{2,1,0:T(8,128)(2,1)S(1)} %broadcast_in_dim.92), channel_id=1, replica_groups=mesh['z'=8,'y'=8,'c'=2,'x'=4] {'c'}, dimensions={0} | all-to-all | bytes 1310720 | tf_op jit(solution)/shard_map/all_to_all | solution.py:20
  182.4 0.7 slice.51
  183.0 0.8 slice.50
  (50 shorter events, 1.0 us)
Async XLA Ops:
  0.6 12.5 %copy-start = (s32[131072]{0:T(1024)S(1)}, s32[131072]{0:T(1024)}, u32[]{:S(2)}) copy-start(s32[131072]{0:T(1024)} %param.13) | copy-start | bytes 1572868
  0.6 1.7 copy-start.1
  2.3 1.0 copy-start.4
  3.3 0.9 copy-start.5
  4.2 0.7 copy-start.7
  8.1 5.0 %copy-start.9 = (s32[4,128]{1,0:T(4,128)S(1)}, s32[4,128]{1,0:T(4,128)}, u32[]{:S(2)}) copy-start(s32[4,128]{1,0:T(4,128)} %param.11) | copy-start | bytes 6148
  8.1 5.0 %copy-start.10 = (s32[4]{0:T(128)S(1)}, s32[4]{0:T(128)}, u32[]{:S(2)}) copy-start(s32[4]{0:T(128)} %param.12) | copy-start | bytes 52
  8.1 14.9 %all-to-all-start = ((f32[4,264,256]{2,1,0:T(8,128)}), f32[4,264,256]{2,1,0:T(8,128)S(1)}, u32[]{:S(2)}, u32[]{:S(2)}) async-start(f32[4,264,256]{2,1,0:T(8,128)} %get-tuple-element.8), calls=%async_computation | async-start | bytes 2162688 | tf_op jit(solution)/shard_map/all_to_all | solution.py:20
  24.1 41.5 %all-to-all-start.2 = ((bf16[128,4,384]{2,1,0:T(4,128)(2,1)}), bf16[128,4,384]{2,1,0:T(4,128)(2,1)S(1)}, u32[]{:S(2)}, u32[]{:S(2)}) async-start(bf16[128,4,384]{2,1,0:T(4,128)(2,1)} %fusion.2), calls=%async_computation.2 | async-start | bytes 786432 | tf_op jit(solution)/shard_map/all_to_all | solution.py:20
  66.7 18.6 %all-to-all-start.1 = ((f32[4,256,256]{2,1,0:T(8,128)}), f32[4,256,256]{2,1,0:T(8,128)S(1)}, u32[]{:S(2)}, u32[]{:S(2)}) async-start(f32[4,256,256]{2,1,0:T(8,128)} %broadcast_in_dim.45), calls=%async_computation.1 | async-start | bytes 2097152 | tf_op jit(solution)/shard_map/all_to_all | solution.py:20
  91.1 1.4 copy-start.2
  92.4 20.7 %copy-start.8 = (bf16[4,1024]{1,0:T(4,128)(2,1)S(1)}, bf16[4,1024]{1,0:T(4,128)(2,1)}, u32[]{:S(2)}) copy-start(bf16[4,1024]{1,0:T(4,128)(2,1)} %q_ref.1) | copy-start | bytes 24580
  92.4 28.0 %copy-start.6 = (bf16[256,256]{1,0:T(8,128)(2,1)S(1)}, bf16[256,256]{1,0:T(8,128)(2,1)}, u32[]{:S(2)}) copy-start(bf16[256,256]{1,0:T(8,128)(2,1)} %w_out_ref.3) | copy-start | bytes 393220
  109.8 10.6 %all-to-all-start.4 = ((bf16[8,8,256]{2,1,0:T(8,128)(2,1)}), bf16[8,8,256]{2,1,0:T(8,128)(2,1)S(1)}, u32[]{:S(2)}, u32[]{:S(2)}) async-start(bf16[8,8,256]{2,1,0:T(8,128)(2,1)} %pad_maximum_fusion.1), calls=%async_computation.4 | async-start | bytes 65536 | tf_op jit(solution)/shard_map/all_to_all | solution.py:20
  120.4 1.6 copy-start.3

commit v3 on v0

v3 whole, which is shorter than its diff:
```python
import functools
import math

import jax
import jax.numpy as jnp
from jax import lax
from jax.experimental import pallas as pl
from jax.experimental.pallas import tpu as pltpu
from jax.sharding import Mesh, PartitionSpec as P

F32 = jnp.float32
BF16 = jnp.bfloat16
DP = ("z", "y", "c")
YCZ = ("y", "c", "z")
ROWS = 256
VMEM = 20 * 1024 * 1024


def exchange(blocks, axes):
    return lax.all_to_all(blocks, axes, split_axis=0, concat_axis=0, tiled=True)


def spread(block, axes):
    count = lax.axis_size(axes)
    return exchange(jnp.broadcast_to(block[None], (count,) + block.shape), axes)


def total(blocks):
    return jnp.sum(blocks.astype(F32), 0)


def dot(a, b):
    return jnp.dot(a, b, preferred_element_type=F32)


def dot_rows(a, b):
    return lax.dot_general(a, b, (((0,), (0,)), ((), ())), preferred_element_type=F32)


def dot_lanes(a, b):
    return lax.dot_general(a, b, (((1,), (1,)), ((), ())), preferred_element_type=F32)


def forward_kernel(
    q_ref, x_hbm, w_in_hbm, w_out_hbm, part_hbm, hid_ref, hid_q_ref, x_buf, w_in_buf, w_out_buf, part_buf, rows, sems
):
    steps = part_buf.shape[0]
    few = q_ref.shape[0]
    chunks = [pl.ds(i * ROWS, ROWS) for i in range(steps)]
    loads = [
        pltpu.make_async_copy(w_in_hbm, w_in_buf, sems.at[0]),
        pltpu.make_async_copy(w_out_hbm, w_out_buf, sems.at[1]),
    ]
    for i, chunk in enumerate(chunks):
        loads.append(pltpu.make_async_copy(x_hbm.at[chunk, :], x_buf.at[chunk, :], sems.at[2 + i]))
    for load in loads:
        load.start()
    rows[...] = jnp.zeros_like(rows)
    loads[0].wait()
    rows[:few, :] = jnp.maximum(dot(q_ref[...], w_in_buf[...]), 0.0)
    hid_q = rows[...].astype(BF16)
    hid_q_ref[...] = hid_q
    loads[1].wait()
    keep = dot(hid_q, w_out_buf[...])[:8]
    stores = []
    for i, chunk in enumerate(chunks):
        loads[2 + i].wait()
        hid = jnp.maximum(dot(x_buf[chunk, :], w_in_buf[...]), 0.0).astype(BF16)
        hid_ref[chunk, :] = hid
        part_buf[i, :ROWS, :] = dot(hid, w_out_buf[...])
        part_buf[i, ROWS:, :] = keep
        stores.append(pltpu.make_async_copy(part_buf.at[i], part_hbm.at[i], sems.at[2 + steps + i]))
        stores[i].start()
    for store in stores:
        store.wait()


def forward(query_feats, item_feats, w_in, w_out):
    items, feats = item_feats.shape
    units = w_in.shape[1]
    width = w_out.shape[1]
    steps = items // ROWS
    anywhere = pl.BlockSpec(memory_space=pltpu.HBM)
    near = pl.BlockSpec(memory_space=pltpu.VMEM)
    return pl.pallas_call(
        forward_kernel,
        in_specs=[near, anywhere, anywhere, anywhere],
        out_specs=[anywhere, near, near],
        out_shape=[
            jax.ShapeDtypeStruct((steps, ROWS + 8, width), F32),
            jax.ShapeDtypeStruct((items, units), BF16),
            jax.ShapeDtypeStruct((16, units), BF16),
        ],
        scratch_shapes=[
            pltpu.VMEM((items, feats), BF16),
            pltpu.VMEM((feats, units), BF16),
            pltpu.VMEM((units, width), BF16),
            pltpu.VMEM((steps, ROWS + 8, width), F32),
            pltpu.VMEM((16, units), F32),
            pltpu.SemaphoreType.DMA((2 + 2 * steps,)),
        ],
        compiler_params=pltpu.CompilerParams(vmem_limit_bytes=VMEM),
    )(query_feats, item_feats, w_in, w_out)


def row_ids(block, shape):
    return (lax.broadcasted_iota(jnp.int32, shape, 0) + block * shape[0]).astype(F32)


def score_kernel(
    few, slots, scale, info_ref, own_ref, by1_ref, by2_ref, by3_ref, msg_ref,
    weight_ref, e_ref, all_q_ref, pay_ref, code, digit, total_u,
):
    queries = msg_ref.shape[0]
    width = e_ref.shape[1]
    group = queries // few
    near = (own_ref, by1_ref, by2_ref, by3_ref)
    for far, ref in enumerate(near):
        first = lax.rem(info_ref[few + 1] + len(near) - far, len(near)) * ROWS
        e_ref[pl.ds(pl.multiple_of(first, ROWS), ROWS), :] = ref[...]

    line = lax.broadcasted_iota(jnp.int32, (queries, queries), 0)
    column = lax.broadcasted_iota(jnp.int32, (queries, queries), 1)
    order = jnp.where(column == (line % group) * few + line // group, 1.0, 0.0).astype(BF16)
    turned = dot(order, msg_ref[...])
    all_q = turned[:, :width].astype(BF16)
    all_q_ref[...] = all_q
    asked = turned[:group, width:].T
    who = asked[2 * slots : 3 * slots]
    code[:slots, :] = jnp.where(who > 0.0, asked[:slots] * 32.0 + asked[slots : 2 * slots], -1.0)
    power = jnp.zeros_like(who)
    for i in range(few):
        power = jnp.where(who == i + 1.0, 32.0**i, power)
    digit[:slots, :] = power
    lane = lax.broadcasted_iota(jnp.int32, (1, group), 1)
    for i in range(few):
        code[slots + i : slots + i + 1, :] = jnp.where(lane == info_ref[few], info_ref[i], -1).astype(F32)
        digit[slots + i : slots + i + 1, :] = jnp.full((1, group), 32.0**i, F32)

    total_d = jnp.zeros((1, queries), F32)
    for block in range(e_ref.shape[0] // ROWS):
        chunk = pl.ds(block * ROWS, ROWS)
        e16 = e_ref[chunk, :].astype(BF16)
        grown = jnp.exp(scale * dot_lanes(e16, all_q))
        ids = row_ids(block, (ROWS, group))
        digits = jnp.zeros((ROWS, group), F32)
        for s in range(slots + few):
            digits = digits + jnp.where(code[s : s + 1, :] == ids, digit[s : s + 1, :], 0.0)
        digits = digits.astype(jnp.int32)
        times = [((digits >> (5 * i)) & 31).astype(F32) for i in range(few)]
        weight = jnp.concatenate(times, 1) * grown
        weight_ref[chunk, :] = weight
        total_d = total_d + jnp.sum(weight, 0, keepdims=True)
        part = dot_rows(weight.astype(BF16), e16)
        total_u[...] = part if block == 0 else total_u[...] + part

    d = jnp.concatenate([total_d[:, i * width : (i + 1) * width] for i in range(queries // width)], 0)
    high = d.astype(BF16).astype(F32)
    tail = jnp.concatenate([high, d - high, jnp.zeros((8 - 2 * d.shape[0], width), F32)], 0)
    for y in range(pay_ref.shape[0]):
        mine = [total_u[i * group + y * 8 : i * group + y * 8 + 8, :] for i in range(few)]
        pay_ref[y] = jnp.concatenate([*mine, tail], 0).astype(BF16)


def score(info, embs, message, few, slots, scale, peers):
    share, width = embs[0].shape
    items = share * len(embs)
    queries, wide = message.shape
    near = pl.BlockSpec(memory_space=pltpu.VMEM)
    return pl.pallas_call(
        functools.partial(score_kernel, few, slots, scale),
        in_specs=[pl.BlockSpec(memory_space=pltpu.SMEM)] + [near] * (len(embs) + 1),
        out_specs=[near] * 4,
        out_shape=[
            jax.ShapeDtypeStruct((items, queries), F32),
            jax.ShapeDtypeStruct((items, width), F32),
            jax.ShapeDtypeStruct((queries, width), BF16),
            jax.ShapeDtypeStruct((peers, queries // peers + 8, width), BF16),
        ],
        scratch_shapes=[
            pltpu.VMEM((slots + 8, queries // few), F32),
            pltpu.VMEM((slots + 8, queries // few), F32),
            pltpu.VMEM((queries, width), F32),
        ],
        compiler_params=pltpu.CompilerParams(vmem_limit_bytes=VMEM),
    )(info, *embs, message)


def backward_kernel(
    few, scale, info_ref, sums_ref, weight_ref, e_ref, all_q_ref, hid_ref, x_ref, w_out_ref,
    emb_q_ref, hid_q_ref, q_ref, out_ref, tanh_grad, pre_grad,
):
    queries = all_q_ref.shape[0]
    items, width = e_ref.shape
    feats = x_ref.shape[1]
    group = queries // few
    sums = jnp.sum(sums_ref[...].astype(F32), 0)
    d = sums[few : few + 2] + sums[few + 2 : few + 4]
    d = jnp.concatenate([d[0:1], d[1:2]], 1)
    factor = scale / d
    lane = lax.broadcasted_iota(jnp.int32, (1, queries), 1)
    position = jnp.full((1, queries), -1.0, F32)
    for i in range(few):
        position = jnp.where(lane == info_ref[few] + i * group, info_ref[i].astype(F32), position)

    pos_emb = jnp.zeros((16, width), F32)
    for block in range(items // ROWS):
        chunk = pl.ds(block * ROWS, ROWS)
        e = e_ref[chunk, :]
        hot = jnp.where(position == row_ids(block, (ROWS, queries)), scale, 0.0)
        coefficient = (weight_ref[chunk, :] * factor - hot).astype(BF16)
        grad = (dot(coefficient, all_q_ref[...]) * (1.0 - e * e)).astype(BF16)
        tanh_grad[chunk, :] = grad
        hid_grad = dot_lanes(grad, w_out_ref[...])
        pre_grad[chunk, :] = jnp.where(hid_ref[chunk, :] > 0, hid_grad, 0.0).astype(BF16)
        place = lax.broadcasted_iota(jnp.int32, (16, ROWS), 1) + block * ROWS
        line = lax.broadcasted_iota(jnp.int32, (16, ROWS), 0)
        picked = jnp.zeros((16, ROWS), F32)
        for i in range(few):
            picked = jnp.where((line == i) & (place == info_ref[i]), 1.0, picked)
        pos_emb = pos_emb + dot(picked.astype(BF16), e.astype(BF16))

    line = lax.broadcasted_iota(jnp.int32, (8, queries), 0)
    own_lane = lax.broadcasted_iota(jnp.int32, (8, queries), 1)
    own_d = jnp.sum(jnp.where(own_lane == line * group + info_ref[few], d, 0.0), 1, keepdims=True)
    live = lax.broadcasted_iota(jnp.int32, (8, width), 0) < few
    emb_q = emb_q_ref[...]
    grad = scale * (sums / own_d - pos_emb[:8]) * (1.0 - emb_q * emb_q)
    grad = jnp.where(live, grad, 0.0)
    grad_q = jnp.concatenate([grad, jnp.zeros_like(grad)], 0).astype(BF16)
    hid_q = hid_q_ref[...]
    pre_grad_q = jnp.where(hid_q > 0, dot_lanes(grad_q, w_out_ref[...]), 0.0).astype(BF16)
    out_ref[feats:, :] = (dot_rows(hid_ref[...], tanh_grad[...]) + dot_rows(hid_q, grad_q)).astype(BF16)
    in_total = dot_rows(pre_grad[...], x_ref[...]) + dot_rows(pre_grad_q, q_ref[...])
    out_ref[:feats, :] = in_total.astype(BF16).T


def backward(info, sums, weight, item_emb, all_q, hidden, item_feats, w_out, emb_q, hidden_q, feats_q, few, scale):
    items, width = item_emb.shape
    feats = item_feats.shape[1]
    units = hidden.shape[1]
    near = pl.BlockSpec(memory_space=pltpu.VMEM)
    return pl.pallas_call(
        functools.partial(backward_kernel, few, scale),
        in_specs=[pl.BlockSpec(memory_space=pltpu.SMEM)] + [near] * 10,
        out_specs=near,
        out_shape=jax.ShapeDtypeStruct((feats + units, width), BF16),
        scratch_shapes=[pltpu.VMEM((items, width), BF16), pltpu.VMEM((items, units), BF16)],
        compiler_params=pltpu.CompilerParams(vmem_limit_bytes=VMEM),
    )(info, sums, weight, item_emb, all_q, hidden, item_feats, w_out, emb_q, hidden_q, feats_q)


def request_codes(rows, query_count, item_count, capacity, order, dp_count):
    pairs = rows.shape[0]
    owners = rows // item_count
    code = rows - owners * item_count
    owner_hot = order(owners)[:, None] == jnp.arange(dp_count, dtype=jnp.int32)[None, :]
    earlier = jnp.arange(pairs)[:, None] >= jnp.arange(pairs)[None, :]
    running = dot(earlier.astype(BF16), owner_hot.astype(BF16))
    slot = jnp.sum(jnp.where(owner_hot, running, 0.0), 1).astype(jnp.int32) - 1
    who = jnp.arange(pairs, dtype=jnp.int32) // (pairs // query_count) + 1
    lane = jnp.arange(128, dtype=jnp.int32)[None, :]
    value = jnp.zeros((pairs, 128), jnp.int32)
    for at, part in enumerate((code // 32, code % 32, who)):
        value = jnp.where(slot[:, None] + at * capacity == lane, part[:, None], value)
    return dot_rows(owner_hot.astype(BF16), value.astype(BF16)).astype(BF16)


def local(query_feats, item_feats, w_in, w_out, negatives, positives, owner_map):
    dp_count = lax.axis_size(DP)
    own_index = lax.axis_index(DP)
    z_count = lax.axis_size("z")
    x_count = lax.axis_size("x")
    yc_count = dp_count // z_count
    few = query_feats.shape[0]
    item_count = item_feats.shape[0]
    width = w_out.shape[1]
    negative_count = negatives.shape[1]
    scale = 4.0 / math.sqrt(width)
    capacity = 4 * few * negative_count // dp_count
    queries = few * dp_count

    blocks, hidden, hidden_q = forward(query_feats, item_feats, w_in, w_out)
    arrived = exchange(blocks, "x")

    named = jnp.concatenate([negatives.reshape(-1), positives])
    rows = jnp.take(owner_map, named, axis=0)
    pos_local = rows[few * negative_count :] - own_index * item_count
    info = jnp.concatenate([pos_local, jnp.stack([lax.axis_index(YCZ), lax.axis_index("x")])])
    codes = request_codes(
        rows[: few * negative_count],
        few,
        item_count,
        capacity,
        lambda o: (o % yc_count) * z_count + o // yc_count,
        dp_count,
    )
    codes = jnp.pad(codes[:, None, :], ((0, 0), (0, few - 1), (0, 0)))

    own = jnp.tanh(total(arrived[:, :ROWS]))
    own_q = jnp.tanh(total(arrived[:, ROWS:]))
    sent_q = jnp.broadcast_to(own_q[None, :few].astype(BF16), (dp_count, few, width))
    message = exchange(jnp.concatenate([sent_q, codes], 2), YCZ)
    message = message.reshape(queries, width + 128)
    embs = [own]
    for far in range(1, x_count):
        embs.append(lax.ppermute(own, "x", [(i, (i + far) % x_count) for i in range(x_count)]))

    weight, item_emb, all_q, pay = score(info, embs, message, few, capacity, scale, yc_count)
    first = total(exchange(pay, ("y", "c")))
    mine = queries // yc_count
    d_rows = queries // width
    d_part = first[mine : mine + d_rows] + first[mine + d_rows : mine + 2 * d_rows]
    high = d_part.astype(BF16)
    tail = jnp.concatenate([high, (d_part - high.astype(F32)).astype(BF16)], 0)
    sums = exchange(
        jnp.concatenate(
            [
                first[:mine].astype(BF16).reshape(few, z_count, width).transpose(1, 0, 2),
                jnp.broadcast_to(tail[None], (z_count, 2 * d_rows, width)),
            ],
            1,
        ),
        "z",
    )
    feats_q = jnp.pad(query_feats, ((0, 16 - few), (0, 0)))
    grads = backward(
        info, sums, weight, item_emb, all_q, hidden, item_feats, w_out, own_q, hidden_q, feats_q, few, scale
    )
    depth = grads.shape[0]
    c_count, y_count = lax.axis_size("c"), lax.axis_size("y")
    grads = total(exchange(grads.reshape(c_count, depth // c_count, width), "c"))
    grads = total(exchange(grads.astype(BF16).reshape(y_count, -1, width), "y"))
    grads = total(spread(grads.astype(BF16), "z")).astype(BF16)
    grads = spread(grads, "y").reshape(-1, width)
    grads = spread(grads, "c").reshape(-1, width)
    return grads[: w_in.shape[0]], grads[w_in.shape[0] :]


def solution(mesh):
    grid = Mesh(mesh.devices.reshape(8, 8, 2, 4), ("z", "y", "c", "x"))
    return jax.shard_map(
        local,
        mesh=grid,
        in_specs=(
            P(DP, None),
            P(DP, None),
            P(None, "x"),
            P("x", None),
            P(DP, None),
            P(DP),
            P(),
        ),
        out_specs=(P(None, "x"), P("x", None)),
        check_vma=False,
    )
```

time: 762 us -> 175 us (0.23)
  blocking collectives: 529 us -> 76.5 us
  local copies, waits for them, and re-layouts: 100 us -> 17.7 us
  waiting for transfers between devices: 60.3 us -> 21.9 us
  starting transfers between devices: 22.5 us -> 43.2 us
  other arithmetic: 22.3 us -> 2.23 us
  between operations: 14.3 us -> 0.97 us
  Pallas kernels: 0 us -> 10.7 us
    psum x1 -> x0, blocking collectives: 500 us -> none  [local(): summed_in, summed_out = lax.psum((in_term, out_term), 'dp')]
    scatter x2 -> x0, local copies, waits for them, and re-layouts: 80 us -> none  [the longest x1 55.4 us: local(): outgoing = outgoing.at[owners, slots].set(pair_neg.reshape(-1, width))]
    all_to_all x1 -> x6, blocking collectives: 29.7 us -> 76.5 us  [exchange(): return lax.all_to_all(blocks, axes, split_axis=0, concat_axis=0, tiled=True)]
    all_to_all x2 -> x3, waiting for transfers between devices: 58.7 us -> 21.6 us  [exchange(): return lax.all_to_all(blocks, axes, split_axis=0, concat_axis=0, tiled=True)]
    scatter-add x2 -> x0, other arithmetic: 15.9 us -> none  [the longest x1 13 us: local(): item_grad.at[asked_rows.reshape(-1)]]
    all_to_all x2 -> x3, starting transfers between devices: 22.5 us -> 34.8 us  [exchange(): return lax.all_to_all(blocks, axes, split_axis=0, concat_axis=0, tiled=True)]
    gather x5 -> x1, local copies, waits for them, and re-layouts: 15 us -> 3.56 us  [local(): rows = jnp.take(owner_map, named, axis=0)]
    pallas_call x0 -> x3, Pallas kernels: none -> 10.7 us  [the longest x1 3.7 us: forward(): pl.pallas_call(forward_kernel, in_specs=[near, anywhere, anywhere, anywhe...]
  transfers between devices with their start and end apart: 3 -> 6, of which waited for: 3 -> 4; matrix products, arithmetic and copies ran while one was open for 4% -> 3% of each run, Pallas kernels for 0% -> 0%
where the time goes in v3:
time: 175 us; the launch traced here: 174 us
  blocking collectives  76.5 us (44%)
  starting transfers between devices  43.2 us (25%)
  waiting for transfers between devices  21.9 us (13%)
  local copies, waits for them, and re-layouts  17.7 us (10%)
  Pallas kernels  10.7 us (6%)
  other arithmetic  2.23 us (1%)
    all_to_all x6, blocking collectives, exchange(): return lax.all_to_all(blocks, axes, split_axis=0, concat_axis=0, tiled=True)  76.5 us
    all_to_all x3, starting transfers between devices, exchange(): return lax.all_to_all(blocks, axes, split_axis=0, concat_axis=0, tiled=True)  34.8 us
    all_to_all x3, waiting for transfers between devices, exchange(): return lax.all_to_all(blocks, axes, split_axis=0, concat_axis=0, tiled=True)  21.6 us
    unnamed x37, local copies, waits for them, and re-layouts  12.4 us
    ppermute x3, starting transfers between devices, local(): lax.ppermute(own, 'x', [(i, (i + far) % x_count) for i in range(x_count)])  8.42 us
    pallas_call x1, Pallas kernels, forward(): pl.pallas_call(forward_kernel, in_specs=[near, anywhere, anywhere, anywhe...  3.7 us
    pallas_call x1, Pallas kernels, score(): pl.pallas_call(functools.partial(score_kernel, few, slots, scale), in_spe...  3.64 us
    gather x1, local copies, waits for them, and re-layouts, local(): rows = jnp.take(owner_map, named, axis=0)  3.56 us
  transfers between devices with their start and end apart: 6, of which 4 were waited for; matrix products, arithmetic and copies ran while one was open for 3% of the time, Pallas kernels for 0%

profile of v3, /device:TPU:1, one launch (start us, length us, event | category | flops | bytes accessed | tf_op | source)
XLA Modules:
  0.0 174.2 jit_solution(7896705631603236860)
XLA Ops:
  0.7 1.6 copy-done.1
  2.3 1.0 copy-done.7
  3.3 0.9 copy-done.10
  4.9 3.7 %shard_map.86 = (f32[4,264,256]{2,1,0:T(8,128)}, bf16[1024,256]{1,0:T(8,128)(2,1)S(1)}, bf16[16,256]{1,0:T(8,128)(2,1)S(1)}) custom-call(bf16[4,1024]{1,0:T(4,128)(2,1)S(1)} %copy-done.14, bf16[1024,1024]{1,0:T(8,128)(2,1)S(1)} %copy-done.1, bf16[1024,256]{1,0:T(8,128)(2,1)S(1)} %copy-done.7, bf16[256,256]{1,0:T(8,128)(2,1)S(1)} %copy-done.10), custom_call_target="tpu_custom_call" | custom-call | tf_op jit(solution)/shard_map/pallas_call | solution.py:85
  8.7 0.8 copy-done.8
  9.4 5.0 %all-to-all-start = ((f32[4,264,256]{2,1,0:T(8,128)}), f32[4,264,256]{2,1,0:T(8,128)S(1)}, u32[]{:S(2)}, u32[]{:S(2)}) async-start(f32[4,264,256]{2,1,0:T(8,128)} %get-tuple-element.9), calls=%async_computation | async-start | bytes 2162688 | tf_op jit(solution)/shard_map/all_to_all | solution.py:20
  14.5 3.6 %gather_fusion = s32[516]{0:T(1024)S(1)} fusion(s32[131072]{0:T(1024)S(1)} %copy-done, s32[1024]{0:T(1024)S(1)} %pad_clamp_fusion), kind=kCustom, calls=%fused_computation | custom fusion | bytes 6192 | tf_op jit(solution)/shard_map/jit(_take)/gather | solution.py:287
  18.4 0.7 fusion.1
  19.3 5.1 %all-to-all-done = f32[4,264,256]{2,1,0:T(8,128)S(1)} async-done(((f32[4,264,256]{2,1,0:T(8,128)}), f32[4,264,256]{2,1,0:T(8,128)S(1)}, u32[]{:S(2)}, u32[]{:S(2)}) %all-to-all-start) | async-done | bytes 1081376 | tf_op jit(solution)/shard_map/all_to_all | solution.py:20
  24.5 0.9 fusion.3
  25.4 23.4 %all-to-all-start.1 = ((bf16[128,4,384]{2,1,0:T(4,128)(2,1)}), bf16[128,4,384]{2,1,0:T(4,128)(2,1)S(1)}, u32[]{:S(2)}, u32[]{:S(2)}) async-start(bf16[128,4,384]{2,1,0:T(4,128)(2,1)} %fusion.3), calls=%async_computation.1 | async-start | bytes 786432 | tf_op jit(solution)/shard_map/all_to_all | solution.py:20
  48.9 2.2 %collective-permute-start = (f32[256,256]{1,0:T(8,128)S(1)}, f32[256,256]{1,0:T(8,128)}, u32[]{:S(2)}, u32[]{:S(2)}) collective-permute-start(f32[256,256]{1,0:T(8,128)S(1)} %tanh.6.own_ref), channel_id=1, source_target_pairs={{0,1},{1,2},{2,3},{3,0},{4,5},{5,6},{6,7},{7,4},{8,9},{9,10},{10,1... | collective-permute-start | bytes 786440 | tf_op jit(solution)/shard_map/ppermute | solution.py:307
  51.1 3.7 %collective-permute-start.1 = (f32[256,256]{1,0:T(8,128)S(1)}, f32[256,256]{1,0:T(8,128)}, u32[]{:S(2)}, u32[]{:S(2)}) collective-permute-start(f32[256,256]{1,0:T(8,128)S(1)} %tanh.6.own_ref), channel_id=1, source_target_pairs={{0,2},{1,3},{2,0},{3,1},{4,6},{5,7},{6,4},{7,5},{8,10},{9,11},{10,... | collective-permute-start | bytes 786440 | tf_op jit(solution)/shard_map/ppermute | solution.py:307
  54.8 2.5 %collective-permute-start.2 = (f32[256,256]{1,0:T(8,128)S(1)}, f32[256,256]{1,0:T(8,128)}, u32[]{:S(2)}, u32[]{:S(2)}) collective-permute-start(f32[256,256]{1,0:T(8,128)S(1)} %tanh.6.own_ref), channel_id=1, source_target_pairs={{0,3},{1,0},{2,1},{3,2},{4,7},{5,4},{6,5},{7,6},{8,11},{9,8},{10,9... | collective-permute-start | bytes 786440 | tf_op jit(solution)/shard_map/ppermute | solution.py:307
  57.5 9.5 %all-to-all-done.1 = bf16[128,4,384]{2,1,0:T(4,128)(2,1)S(1)} async-done(((bf16[128,4,384]{2,1,0:T(4,128)(2,1)}), bf16[128,4,384]{2,1,0:T(4,128)(2,1)S(1)}, u32[]{:S(2)}, u32[]{:S(2)}) %all-to-all-start.1) | async-done | bytes 393248 | tf_op jit(solution)/shard_map/all_to_all | solution.py:20
  67.4 3.6 %shard_map.87 = (f32[1024,512]{1,0:T(8,128)S(1)}, f32[1024,256]{1,0:T(8,128)S(1)}, bf16[512,256]{1,0:T(8,128)(2,1)S(1)}, bf16[16,40,256]{2,1,0:T(8,128)(2,1)S(1)}) custom-call(s32[6]{0:T(128)S(1)} %pad_add_fusion.info_ref, f32[256,256]{1,0:T(8,128)S(1)} %tanh.6.own_ref, f32[256,256]{1,0:T(8,128)} %collective-permute-done.by1_ref, ...), custom_call_target="tpu_custom_call" | custom-call | tf_op jit(solution)/shard_map/pallas_call | solution.py:170
  71.0 1.3 copy-done.3
  72.4 1.0 copy-done.5
  73.3 21.6 %all_to_all.45 = bf16[16,40,256]{2,1,0:T(8,128)(2,1)S(1)} all-to-all(bf16[16,40,256]{2,1,0:T(8,128)(2,1)S(1)} %get-tuple-element.10), channel_id=1, replica_groups=mesh['z'=8,'y'=8,'c'=2,'x'=4] {'y','c'}, dimensions={0} | all-to-all | bytes 655360 | tf_op jit(solution)/shard_map/all_to_all | solution.py:20
  95.7 6.4 %all-to-all-start.3 = ((bf16[8,8,256]{2,1,0:T(8,128)(2,1)}), bf16[8,8,256]{2,1,0:T(8,128)(2,1)S(1)}, u32[]{:S(2)}, u32[]{:S(2)}) async-start(bf16[8,8,256]{2,1,0:T(8,128)(2,1)} %pad_maximum_fusion), calls=%async_computation.3 | async-start | bytes 65536 | tf_op jit(solution)/shard_map/all_to_all | solution.py:20
  102.1 7.0 %all-to-all-done.3.sums_ref = bf16[8,8,256]{2,1,0:T(8,128)(2,1)S(1)} async-done(((bf16[8,8,256]{2,1,0:T(8,128)(2,1)}), bf16[8,8,256]{2,1,0:T(8,128)(2,1)S(1)}, u32[]{:S(2)}, u32[]{:S(2)}) %all-to-all-start.3) | async-done | bytes 32800 | tf_op jit(solution)/shard_map/all_to_all | solution.py:20
  109.1 1.6 copy-done.4
  110.7 1.2 copy-done.6
  111.9 1.0 copy-done.9
  113.0 0.9 copy-done.13
  113.9 3.4 %shard_map.88 = bf16[1280,256]{1,0:T(8,128)(2,1)S(1)} custom-call(s32[6]{0:T(128)S(1)} %pad_add_fusion.info_ref, bf16[8,8,256]{2,1,0:T(8,128)(2,1)S(1)} %all-to-all-done.3.sums_ref, f32[1024,512]{1,0:T(8,128)S(1)} %copy-done.4, f32[1024,256]{1,0:T(8,128)S(1)} %copy-done.6, bf16[512,256]{1,0:T(8,128)(2,1)S(1)} %copy-done.13, bf16[1024,256]{1,0:T(8,128)(2,1)S(1)} %copy-done.9, ...), custom_call_target="tpu_custom_call" | custom-call | tf_op jit(solution)/shard_map/pallas_call | solution.py:243
  117.3 4.7 %all_to_all.46 = bf16[2,640,256]{2,1,0:T(8,128)(2,1)S(1)} all-to-all(bf16[2,640,256]{2,1,0:T(8,128)(2,1)S(1)} %bitcast.16), channel_id=1, replica_groups=mesh['z'=8,'y'=8,'c'=2,'x'=4] {'c'}, dimensions={0} | all-to-all | bytes 1310720 | tf_op jit(solution)/shard_map/all_to_all | solution.py:20
  122.3 15.6 %all_to_all.47 = bf16[8,80,256]{2,1,0:T(8,128)(2,1)S(1)} all-to-all(bf16[8,80,256]{2,1,0:T(8,128)(2,1)S(1)} %bitcast.19), channel_id=1, replica_groups=mesh['z'=8,'y'=8,'c'=2,'x'=4] {'y'}, dimensions={0} | all-to-all | bytes 655360 | tf_op jit(solution)/shard_map/all_to_all | solution.py:20
  138.0 13.4 %all_to_all.48 = bf16[8,80,256]{2,1,0:T(8,128)(2,1)S(1)} all-to-all(bf16[8,80,256]{2,1,0:T(8,128)(2,1)S(1)} %broadcast_in_dim.85), channel_id=1, replica_groups=mesh['z'=8,'y'=8,'c'=2,'x'=4] {'z'}, dimensions={0} | all-to-all | bytes 655360 | tf_op jit(solution)/shard_map/all_to_all | solution.py:20
  151.6 12.9 %all_to_all.49 = bf16[8,80,256]{2,1,0:T(8,128)(2,1)S(1)} all-to-all(bf16[8,80,256]{2,1,0:T(8,128)(2,1)S(1)} %broadcast_in_dim.86), channel_id=1, replica_groups=mesh['z'=8,'y'=8,'c'=2,'x'=4] {'y'}, dimensions={0} | all-to-all | bytes 655360 | tf_op jit(solution)/shard_map/all_to_all | solution.py:20
  164.5 8.2 %all_to_all.50 = bf16[2,640,256]{2,1,0:T(8,128)(2,1)S(1)} all-to-all(bf16[2,640,256]{2,1,0:T(8,128)(2,1)S(1)} %broadcast_in_dim.88), channel_id=1, replica_groups=mesh['z'=8,'y'=8,'c'=2,'x'=4] {'c'}, dimensions={0} | all-to-all | bytes 1310720 | tf_op jit(solution)/shard_map/all_to_all | solution.py:20
  172.7 0.8 slice.50
  (60 shorter events, 3.8 us)
Async XLA Ops:
  0.6 13.8 %copy-start = (s32[131072]{0:T(1024)S(1)}, s32[131072]{0:T(1024)}, u32[]{:S(2)}) copy-start(s32[131072]{0:T(1024)} %param.13) | copy-start | bytes 1572868
  0.6 1.7 copy-start.1
  2.3 1.0 copy-start.7
  3.3 0.9 copy-start.10
  4.2 0.7 copy-start.14
  8.6 0.8 copy-start.8
  9.4 5.0 %copy-start.16 = (s32[4,128]{1,0:T(4,128)S(1)}, s32[4,128]{1,0:T(4,128)}, u32[]{:S(2)}) copy-start(s32[4,128]{1,0:T(4,128)} %param.11) | copy-start | bytes 6148
  9.4 5.0 %copy-start.17 = (s32[4]{0:T(128)S(1)}, s32[4]{0:T(128)}, u32[]{:S(2)}) copy-start(s32[4]{0:T(128)} %param.12) | copy-start | bytes 52
  9.4 14.9 %all-to-all-start = ((f32[4,264,256]{2,1,0:T(8,128)}), f32[4,264,256]{2,1,0:T(8,128)S(1)}, u32[]{:S(2)}, u32[]{:S(2)}) async-start(f32[4,264,256]{2,1,0:T(8,128)} %get-tuple-element.9), calls=%async_computation | async-start | bytes 2162688 | tf_op jit(solution)/shard_map/all_to_all | solution.py:20
  25.4 41.5 %all-to-all-start.1 = ((bf16[128,4,384]{2,1,0:T(4,128)(2,1)}), bf16[128,4,384]{2,1,0:T(4,128)(2,1)S(1)}, u32[]{:S(2)}, u32[]{:S(2)}) async-start(bf16[128,4,384]{2,1,0:T(4,128)(2,1)} %fusion.3), calls=%async_computation.1 | async-start | bytes 786432 | tf_op jit(solution)/shard_map/all_to_all | solution.py:20
  48.9 18.1 %collective-permute-start = (f32[256,256]{1,0:T(8,128)S(1)}, f32[256,256]{1,0:T(8,128)}, u32[]{:S(2)}, u32[]{:S(2)}) collective-permute-start(f32[256,256]{1,0:T(8,128)S(1)} %tanh.6.own_ref), channel_id=1, source_target_pairs={{0,1},{1,2},{2,3},{3,0},{4,5},{5,6},{6,7},{7,4},{8,9},{9,10},{10,1... | collective-permute-start | bytes 786440 | tf_op jit(solution)/shard_map/ppermute | solution.py:307
  51.1 16.0 %collective-permute-start.1 = (f32[256,256]{1,0:T(8,128)S(1)}, f32[256,256]{1,0:T(8,128)}, u32[]{:S(2)}, u32[]{:S(2)}) collective-permute-start(f32[256,256]{1,0:T(8,128)S(1)} %tanh.6.own_ref), channel_id=1, source_target_pairs={{0,2},{1,3},{2,0},{3,1},{4,6},{5,7},{6,4},{7,5},{8,10},{9,11},{10,... | collective-permute-start | bytes 786440 | tf_op jit(solution)/shard_map/ppermute | solution.py:307
  54.8 12.5 %collective-permute-start.2 = (f32[256,256]{1,0:T(8,128)S(1)}, f32[256,256]{1,0:T(8,128)}, u32[]{:S(2)}, u32[]{:S(2)}) collective-permute-start(f32[256,256]{1,0:T(8,128)S(1)} %tanh.6.own_ref), channel_id=1, source_target_pairs={{0,3},{1,0},{2,1},{3,2},{4,7},{5,4},{6,5},{7,6},{8,11},{9,8},{10,9... | collective-permute-start | bytes 786440 | tf_op jit(solution)/shard_map/ppermute | solution.py:307
  67.0 35.0 %copy-start.15 = (bf16[4,1024]{1,0:T(4,128)(2,1)S(1)}, bf16[4,1024]{1,0:T(4,128)(2,1)}, u32[]{:S(2)}) copy-start(bf16[4,1024]{1,0:T(4,128)(2,1)} %q_ref.1) | copy-start | bytes 24580
  67.1 42.1 %copy-start.2 = (bf16[1024,1024]{1,0:T(8,128)(2,1)S(1)}, bf16[1024,1024]{1,0:T(8,128)(2,1)}, u32[]{:S(2)}) copy-start(bf16[1024,1024]{1,0:T(8,128)(2,1)} %x_ref.1) | copy-start | bytes 6291460
  67.1 42.1 %copy-start.11 = (bf16[256,256]{1,0:T(8,128)(2,1)S(1)}, bf16[256,256]{1,0:T(8,128)(2,1)}, u32[]{:S(2)}) copy-start(bf16[256,256]{1,0:T(8,128)(2,1)} %w_out_ref.1) | copy-start | bytes 393220
  71.0 1.3 copy-start.3
  72.4 1.0 copy-start.5
  73.3 21.6 %copy-start.12 = (bf16[512,256]{1,0:T(8,128)(2,1)}, bf16[512,256]{1,0:T(8,128)(2,1)S(1)}, u32[]{:S(2)}) copy-start(bf16[512,256]{1,0:T(8,128)(2,1)S(1)} %get-tuple-element.13.all_q_ref) | copy-start | bytes 786436
  95.7 13.5 %all-to-all-start.3 = ((bf16[8,8,256]{2,1,0:T(8,128)(2,1)}), bf16[8,8,256]{2,1,0:T(8,128)(2,1)S(1)}, u32[]{:S(2)}, u32[]{:S(2)}) async-start(bf16[8,8,256]{2,1,0:T(8,128)(2,1)} %pad_maximum_fusion), calls=%async_computation.3 | async-start | bytes 65536 | tf_op jit(solution)/shard_map/all_to_all | solution.py:20
  109.1 1.6 copy-start.4
  110.7 1.2 copy-start.6
  111.9 1.0 copy-start.9
  113.0 0.9 copy-start.13

commit v4 on v3

--- a/solution.py
+++ b/solution.py
@@ -41,66 +41,91 @@
     return lax.dot_general(a, b, (((1,), (1,)), ((), ())), preferred_element_type=F32)
 
 
+def blocks_of(items):
+    return [pl.ds(i * ROWS, ROWS) for i in range(items // ROWS)]
+
+
+class Copies:
+    def __init__(self, sems):
+        self.sems = sems
+        self.used = 0
+
+    def start(self, source, target):
+        copy = pltpu.make_async_copy(source, target, self.sems.at[self.used])
+        copy.start()
+        self.used += 1
+        return copy
+
+
 def forward_kernel(
-    q_ref, x_hbm, w_in_hbm, w_out_hbm, part_hbm, hid_ref, hid_q_ref, x_buf, w_in_buf, w_out_buf, part_buf, rows, sems
+    q_hbm, x_hbm, w_in_hbm, w_out_hbm, part_hbm, hid_hbm, hid_q_hbm,
+    q_buf, x_buf, w_in_buf, w_out_buf, part_buf, hid_buf, hid_q_buf, rows, sems,
 ):
-    steps = part_buf.shape[0]
-    few = q_ref.shape[0]
-    chunks = [pl.ds(i * ROWS, ROWS) for i in range(steps)]
-    loads = [
-        pltpu.make_async_copy(w_in_hbm, w_in_buf, sems.at[0]),
-        pltpu.make_async_copy(w_out_hbm, w_out_buf, sems.at[1]),
-    ]
+    few = q_buf.shape[0]
+    chunks = blocks_of(x_buf.shape[0])
+    copies = Copies(sems)
+    load_in = copies.start(w_in_hbm, w_in_buf)
+    load_q = copies.start(q_hbm, q_buf)
+    load_x = [copies.start(x_hbm.at[chunks[0], :], x_buf.at[chunks[0], :])]
+    load_out = copies.start(w_out_hbm, w_out_buf)
+    for chunk in chunks[1:]:
+        load_x.append(copies.start(x_hbm.at[chunk, :], x_buf.at[chunk, :]))
+    rows[...] = jnp.zeros_like(rows)
+    load_in.wait()
+    load_q.wait()
+    rows[:few, :] = jnp.maximum(dot(q_buf[...], w_in_buf[...]), 0.0)
+    hid_q_buf[...] = rows[...].astype(BF16)
+    stores = [copies.start(hid_q_buf, hid_q_hbm)]
+    load_out.wait()
+    keep = dot(hid_q_buf[...], w_out_buf[...])[:8]
     for i, chunk in enumerate(chunks):
-        loads.append(pltpu.make_async_copy(x_hbm.at[chunk, :], x_buf.at[chunk, :], sems.at[2 + i]))
-    for load in loads:
-        load.start()
-    rows[...] = jnp.zeros_like(rows)
-    loads[0].wait()
-    rows[:few, :] = jnp.maximum(dot(q_ref[...], w_in_buf[...]), 0.0)
-    hid_q = rows[...].astype(BF16)
-    hid_q_ref[...] = hid_q
-    loads[1].wait()
-    keep = dot(hid_q, w_out_buf[...])[:8]
-    stores = []
-    for i, chunk in enumerate(chunks):
-        loads[2 + i].wait()
+        load_x[i].wait()
         hid = jnp.maximum(dot(x_buf[chunk, :], w_in_buf[...]), 0.0).astype(BF16)
-        hid_ref[chunk, :] = hid
+        hid_buf[chunk, :] = hid
         part_buf[i, :ROWS, :] = dot(hid, w_out_buf[...])
         part_buf[i, ROWS:, :] = keep
-        stores.append(pltpu.make_async_copy(part_buf.at[i], part_hbm.at[i], sems.at[2 + steps + i]))
-        stores[i].start()
+        stores.append(copies.start(part_buf.at[i], part_hbm.at[i]))
+        stores.append(copies.start(hid_buf.at[chunk, :], hid_hbm.at[chunk, :]))
     for store in stores:
         store.wait()
 
 
+FAR = pl.BlockSpec(memory_space=pltpu.HBM)
+NEAR = pl.BlockSpec(memory_space=pltpu.VMEM)
+
+
+def pinned(*arrays):
+    return [pltpu.with_memory_space_constraint(a, pltpu.HBM) for a in arrays]
+
+
 def forward(query_feats, item_feats, w_in, w_out):
+    few = query_feats.shape[0]
     items, feats = item_feats.shape
     units = w_in.shape[1]
     width = w_out.shape[1]
     steps = items // ROWS
-    anywhere = pl.BlockSpec(memory_space=pltpu.HBM)
-    near = pl.BlockSpec(memory_space=pltpu.VMEM)
     return pl.pallas_call(
         forward_kernel,
-        in_specs=[near, anywhere, anywhere, anywhere],
-        out_specs=[anywhere, near, near],
+        in_specs=[FAR] * 4,
+        out_specs=[FAR] * 3,
         out_shape=[
-            jax.ShapeDtypeStruct((steps, ROWS + 8, width), F32),
-            jax.ShapeDtypeStruct((items, units), BF16),
-            jax.ShapeDtypeStruct((16, units), BF16),
+            pltpu.HBM((steps, ROWS + 8, width), F32),
+            pltpu.HBM((items, units), BF16),
+            pltpu.HBM((16, units), BF16),
         ],
         scratch_shapes=[
+            pltpu.VMEM((few, feats), BF16),
             pltpu.VMEM((items, feats), BF16),
             pltpu.VMEM((feats, units), BF16),
             pltpu.VMEM((units, width), BF16),
             pltpu.VMEM((steps, ROWS + 8, width), F32),
+            pltpu.VMEM((items, units), BF16),
+            pltpu.VMEM((16, units), BF16),
             pltpu.VMEM((16, units), F32),
-            pltpu.SemaphoreType.DMA((2 + 2 * steps,)),
+            pltpu.SemaphoreType.DMA((4 + 3 * steps,)),
         ],
         compiler_params=pltpu.CompilerParams(vmem_limit_bytes=VMEM),
-    )(query_feats, item_feats, w_in, w_out)
+    )(*pinned(query_feats, item_feats, w_in, w_out))
 
 
 def row_ids(block, shape):
@@ -109,8 +134,9 @@
 
 def score_kernel(
     few, slots, scale, info_ref, own_ref, by1_ref, by2_ref, by3_ref, msg_ref,
-    weight_ref, e_ref, all_q_ref, pay_ref, code, digit, total_u,
+    weight_hbm, e_hbm, all_q_hbm, pay_hbm, weight_ref, e_ref, all_q_ref, pay_ref, code, digit, total_u, sems,
 ):
+    copies = Copies(sems)
     queries = msg_ref.shape[0]
     width = e_ref.shape[1]
     group = queries // few
@@ -125,6 +151,7 @@
     turned = dot(order, msg_ref[...])
     all_q = turned[:, :width].astype(BF16)
     all_q_ref[...] = all_q
+    stores = [copies.start(e_ref, e_hbm), copies.start(all_q_ref, all_q_hbm)]
     asked = turned[:group, width:].T
     who = asked[2 * slots : 3 * slots]
     code[:slots, :] = jnp.where(who > 0.0, asked[:slots] * 32.0 + asked[slots : 2 * slots], -1.0)
@@ -138,8 +165,7 @@
         digit[slots + i : slots + i + 1, :] = jnp.full((1, group), 32.0**i, F32)
 
     total_d = jnp.zeros((1, queries), F32)
-    for block in range(e_ref.shape[0] // ROWS):
-        chunk = pl.ds(block * ROWS, ROWS)
+    for block, chunk in enumerate(blocks_of(e_ref.shape[0])):
         e16 = e_ref[chunk, :].astype(BF16)
         grown = jnp.exp(scale * dot_lanes(e16, all_q))
         ids = row_ids(block, (ROWS, group))
@@ -150,6 +176,7 @@
         times = [((digits >> (5 * i)) & 31).astype(F32) for i in range(few)]
         weight = jnp.concatenate(times, 1) * grown
         weight_ref[chunk, :] = weight
+        stores.append(copies.start(weight_ref.at[chunk, :], weight_hbm.at[chunk, :]))
         total_d = total_d + jnp.sum(weight, 0, keepdims=True)
         part = dot_rows(weight.astype(BF16), e16)
         total_u[...] = part if block == 0 else total_u[...] + part
@@ -160,36 +187,50 @@
     for y in range(pay_ref.shape[0]):
         mine = [total_u[i * group + y * 8 : i * group + y * 8 + 8, :] for i in range(few)]
         pay_ref[y] = jnp.concatenate([*mine, tail], 0).astype(BF16)
+    stores.append(copies.start(pay_ref, pay_hbm))
+    for store in stores:
+        store.wait()
 
 
 def score(info, embs, message, few, slots, scale, peers):
     share, width = embs[0].shape
     items = share * len(embs)
     queries, wide = message.shape
-    near = pl.BlockSpec(memory_space=pltpu.VMEM)
+    pay = (peers, queries // peers + 8, width)
     return pl.pallas_call(
         functools.partial(score_kernel, few, slots, scale),
-        in_specs=[pl.BlockSpec(memory_space=pltpu.SMEM)] + [near] * (len(embs) + 1),
-        out_specs=[near] * 4,
+        in_specs=[pl.BlockSpec(memory_space=pltpu.SMEM)] + [NEAR] * (len(embs) + 1),
+        out_specs=[FAR] * 4,
         out_shape=[
-            jax.ShapeDtypeStruct((items, queries), F32),
-            jax.ShapeDtypeStruct((items, width), F32),
-            jax.ShapeDtypeStruct((queries, width), BF16),
-            jax.ShapeDtypeStruct((peers, queries // peers + 8, width), BF16),
+            pltpu.HBM((items, queries), F32),
+            pltpu.HBM((items, width), F32),
+            pltpu.HBM((queries, width), BF16),
+            pltpu.HBM(pay, BF16),
         ],
         scratch_shapes=[
+            pltpu.VMEM((items, queries), F32),
+            pltpu.VMEM((items, width), F32),
+            pltpu.VMEM((queries, width), BF16),
+            pltpu.VMEM(pay, BF16),
             pltpu.VMEM((slots + 8, queries // few), F32),
             pltpu.VMEM((slots + 8, queries // few), F32),
             pltpu.VMEM((queries, width), F32),
+            pltpu.SemaphoreType.DMA((3 + items // ROWS,)),
         ],
         compiler_params=pltpu.CompilerParams(vmem_limit_bytes=VMEM),
     )(info, *embs, message)
 
 
 def backward_kernel(
-    few, scale, info_ref, sums_ref, weight_ref, e_ref, all_q_ref, hid_ref, x_ref, w_out_ref,
-    emb_q_ref, hid_q_ref, q_ref, out_ref, tanh_grad, pre_grad,
+    few, scale, info_ref, all_q_hbm, weight_hbm, e_hbm, hid_hbm, sums_ref, w_out_ref, x_ref,
+    emb_q_ref, hid_q_ref, q_ref, out_ref, all_q_ref, weight_ref, e_ref, hid_ref, tanh_grad, pre_grad, sems,
 ):
+    copies = Copies(sems)
+    load_q = copies.start(all_q_hbm, all_q_ref)
+    loads = []
+    for chunk in blocks_of(e_ref.shape[0]):
+        pairs = ((weight_hbm, weight_ref), (e_hbm, e_ref), (hid_hbm, hid_ref))
+        loads.append([copies.start(source.at[chunk, :], target.at[chunk, :]) for source, target in pairs])
     queries = all_q_ref.shape[0]
     items, width = e_ref.shape
     feats = x_ref.shape[1]
@@ -204,8 +245,10 @@
         position = jnp.where(lane == info_ref[few] + i * group, info_ref[i].astype(F32), position)
 
     pos_emb = jnp.zeros((16, width), F32)
-    for block in range(items // ROWS):
-        chunk = pl.ds(block * ROWS, ROWS)
+    load_q.wait()
+    for block, chunk in enumerate(blocks_of(items)):
+        for copy in loads[block]:
+            copy.wait()
         e = e_ref[chunk, :]
         hot = jnp.where(position == row_ids(block, (ROWS, queries)), scale, 0.0)
         coefficient = (weight_ref[chunk, :] * factor - hot).astype(BF16)
@@ -235,19 +278,23 @@
     out_ref[:feats, :] = in_total.astype(BF16).T
 
 
-def backward(info, sums, weight, item_emb, all_q, hidden, item_feats, w_out, emb_q, hidden_q, feats_q, few, scale):
-    items, width = item_emb.shape
-    feats = item_feats.shape[1]
-    units = hidden.shape[1]
-    near = pl.BlockSpec(memory_space=pltpu.VMEM)
+def backward(info, far, near, few, scale):
+    items, width = far[2].shape
+    units = far[3].shape[1]
+    feats = near[2].shape[1]
     return pl.pallas_call(
         functools.partial(backward_kernel, few, scale),
-        in_specs=[pl.BlockSpec(memory_space=pltpu.SMEM)] + [near] * 10,
-        out_specs=near,
+        in_specs=[pl.BlockSpec(memory_space=pltpu.SMEM)] + [FAR] * len(far) + [NEAR] * len(near),
+        out_specs=NEAR,
         out_shape=jax.ShapeDtypeStruct((feats + units, width), BF16),
-        scratch_shapes=[pltpu.VMEM((items, width), BF16), pltpu.VMEM((items, units), BF16)],
+        scratch_shapes=[
+            *[pltpu.VMEM(a.shape, a.dtype) for a in far],
+            pltpu.VMEM((items, width), BF16),
+            pltpu.VMEM((items, units), BF16),
+            pltpu.SemaphoreType.DMA((1 + 3 * (items // ROWS),)),
+        ],
         compiler_params=pltpu.CompilerParams(vmem_limit_bytes=VMEM),
-    )(info, sums, weight, item_emb, all_q, hidden, item_feats, w_out, emb_q, hidden_q, feats_q)
+    )(info, *pinned(*far), *near)
 
 
 def request_codes(rows, query_count, item_count, capacity, order, dp_count):
@@ -324,9 +371,8 @@
         "z",
     )
     feats_q = jnp.pad(query_feats, ((0, 16 - few), (0, 0)))
-    grads = backward(
-        info, sums, weight, item_emb, all_q, hidden, item_feats, w_out, own_q, hidden_q, feats_q, few, scale
-    )
+    near = (sums, w_out, item_feats, own_q, hidden_q, feats_q)
+    grads = backward(info, (all_q, weight, item_emb, hidden), near, few, scale)
     depth = grads.shape[0]
     c_count, y_count = lax.axis_size("c"), lax.axis_size("y")
     grads = total(exchange(grads.reshape(c_count, depth // c_count, width), "c"))

time: 175 us -> 166 us (0.949)
  local copies, waits for them, and re-layouts: 17.7 us -> 5.56 us
  Pallas kernels: 10.7 us -> 14.3 us
    unnamed x37 -> x15, local copies, waits for them, and re-layouts: 12.4 us -> 0.17 us
where the time goes in v4:
time: 166 us
  blocking collectives  76.7 us (46%)
  starting transfers between devices  43.1 us (26%)
  waiting for transfers between devices  21.9 us (13%)
  Pallas kernels  14.3 us (9%)
  local copies, waits for them, and re-layouts  5.56 us (3%)
  other arithmetic  2.23 us (1%)
    all_to_all x6, blocking collectives, exchange(): return lax.all_to_all(blocks, axes, split_axis=0, concat_axis=0, tiled=True)  76.7 us
    all_to_all x3, starting transfers between devices, exchange(): return lax.all_to_all(blocks, axes, split_axis=0, concat_axis=0, tiled=True)  34.6 us
    all_to_all x3, waiting for transfers between devices, exchange(): return lax.all_to_all(blocks, axes, split_axis=0, concat_axis=0, tiled=True)  21.6 us
    ppermute x3, starting transfers between devices, local(): lax.ppermute(own, 'x', [(i, (i + far) % x_count) for i in range(x_count)])  8.42 us
    pallas_call x1, Pallas kernels, backward(): pl.pallas_call(functools.partial(backward_kernel, few, scale), in_specs=[...  5.1 us
    pallas_call x1, Pallas kernels, score(): pl.pallas_call(functools.partial(score_kernel, few, slots, scale), in_spe...  4.63 us
    pallas_call x1, Pallas kernels, forward(): pl.pallas_call(forward_kernel, in_specs=[FAR] * 4, out_specs=[FAR] * 3, o...  4.56 us
    gather x1, local copies, waits for them, and re-layouts, local(): rows = jnp.take(owner_map, named, axis=0)  3.56 us
  transfers between devices with their start and end apart: 6, of which 4 were waited for; matrix products, arithmetic and copies ran while one was open for 3% of the time, Pallas kernels for 0%

profile of v4, /device:TPU:1, one launch (start us, length us, event | category | flops | bytes accessed | tf_op | source)
XLA Modules:
  0.0 165.7 jit_solution(9705982213652552670)
XLA Ops:
  0.6 4.6 %shard_map.86 = (f32[4,264,256]{2,1,0:T(8,128)}, bf16[1024,256]{1,0:T(8,128)(2,1)}, bf16[16,256]{1,0:T(8,128)(2,1)}) custom-call(bf16[4,1024]{1,0:T(4,128)(2,1)} %q_hbm.1, bf16[1024,1024]{1,0:T(8,128)(2,1)} %x_ref.1, bf16[1024,256]{1,0:T(8,128)(2,1)} %w_in_hbm.1, bf16[256,256]{1,0:T(8,128)(2,1)} %w_out_ref.1), custom_call_target="tpu_custom_call" | custom-call | tf_op jit(solution)/shard_map/pallas_call | solution.py:107
  5.2 4.9 %all-to-all-start = ((f32[4,264,256]{2,1,0:T(8,128)}), f32[4,264,256]{2,1,0:T(8,128)S(1)}, u32[]{:S(2)}, u32[]{:S(2)}) async-start(f32[4,264,256]{2,1,0:T(8,128)} %get-tuple-element.9), calls=%async_computation | async-start | bytes 2162688 | tf_op jit(solution)/shard_map/all_to_all | solution.py:20
  10.1 3.6 %gather_fusion = s32[516]{0:T(1024)S(1)} fusion(s32[131072]{0:T(1024)S(1)} %copy-done, s32[1024]{0:T(1024)S(1)} %pad_clamp_fusion), kind=kCustom, calls=%fused_computation | custom fusion | bytes 6192 | tf_op jit(solution)/shard_map/jit(_take)/gather | solution.py:334
  13.8 0.3 fusion
  14.1 0.7 fusion.1
  14.8 0.1 copy.14
  14.9 5.1 %all-to-all-done = f32[4,264,256]{2,1,0:T(8,128)S(1)} async-done(((f32[4,264,256]{2,1,0:T(8,128)}), f32[4,264,256]{2,1,0:T(8,128)S(1)}, u32[]{:S(2)}, u32[]{:S(2)}) %all-to-all-start) | async-done | bytes 1081376 | tf_op jit(solution)/shard_map/all_to_all | solution.py:20
  20.0 0.1 broadcast_in_dim.77
  20.1 0.9 fusion.3
  21.1 23.4 %all-to-all-start.1 = ((bf16[128,4,384]{2,1,0:T(4,128)(2,1)}), bf16[128,4,384]{2,1,0:T(4,128)(2,1)S(1)}, u32[]{:S(2)}, u32[]{:S(2)}) async-start(bf16[128,4,384]{2,1,0:T(4,128)(2,1)} %fusion.3), calls=%async_computation.1 | async-start | bytes 786432 | tf_op jit(solution)/shard_map/all_to_all | solution.py:20
  44.5 0.1 slice_reduce_fusion
  44.6 2.2 %collective-permute-start = (f32[256,256]{1,0:T(8,128)S(1)}, f32[256,256]{1,0:T(8,128)}, u32[]{:S(2)}, u32[]{:S(2)}) collective-permute-start(f32[256,256]{1,0:T(8,128)S(1)} %tanh.6.own_ref), channel_id=1, source_target_pairs={{0,1},{1,2},{2,3},{3,0},{4,5},{5,6},{6,7},{7,4},{8,9},{9,10},{10,1... | collective-permute-start | bytes 786440 | tf_op jit(solution)/shard_map/ppermute | solution.py:354
  46.8 3.7 %collective-permute-start.1 = (f32[256,256]{1,0:T(8,128)S(1)}, f32[256,256]{1,0:T(8,128)}, u32[]{:S(2)}, u32[]{:S(2)}) collective-permute-start(f32[256,256]{1,0:T(8,128)S(1)} %tanh.6.own_ref), channel_id=1, source_target_pairs={{0,2},{1,3},{2,0},{3,1},{4,6},{5,7},{6,4},{7,5},{8,10},{9,11},{10,... | collective-permute-start | bytes 786440 | tf_op jit(solution)/shard_map/ppermute | solution.py:354
  50.5 2.5 %collective-permute-start.2 = (f32[256,256]{1,0:T(8,128)S(1)}, f32[256,256]{1,0:T(8,128)}, u32[]{:S(2)}, u32[]{:S(2)}) collective-permute-start(f32[256,256]{1,0:T(8,128)S(1)} %tanh.6.own_ref), channel_id=1, source_target_pairs={{0,3},{1,0},{2,1},{3,2},{4,7},{5,4},{6,5},{7,6},{8,11},{9,8},{10,9... | collective-permute-start | bytes 786440 | tf_op jit(solution)/shard_map/ppermute | solution.py:354
  53.1 0.1 pad_add_fusion.info_ref
  53.1 9.5 %all-to-all-done.1 = bf16[128,4,384]{2,1,0:T(4,128)(2,1)S(1)} async-done(((bf16[128,4,384]{2,1,0:T(4,128)(2,1)}), bf16[128,4,384]{2,1,0:T(4,128)(2,1)S(1)}, u32[]{:S(2)}, u32[]{:S(2)}) %all-to-all-start.1) | async-done | bytes 393248 | tf_op jit(solution)/shard_map/all_to_all | solution.py:20
  62.6 0.1 reshape.150.msg_ref
  62.8 0.3 collective-permute-done.2.by3_ref
  63.0 4.6 %shard_map.87 = (f32[1024,512]{1,0:T(8,128)}, f32[1024,256]{1,0:T(8,128)}, bf16[512,256]{1,0:T(8,128)(2,1)}, bf16[16,40,256]{2,1,0:T(8,128)(2,1)}) custom-call(s32[6]{0:T(128)S(1)} %pad_add_fusion.info_ref, f32[256,256]{1,0:T(8,128)S(1)} %tanh.6.own_ref, f32[256,256]{1,0:T(8,128)} %collective-permute-done.by1_ref, ...), custom_call_target="tpu_custom_call" | custom-call | tf_op jit(solution)/shard_map/pallas_call | solution.py:200
  67.7 21.8 %all_to_all.45 = bf16[16,40,256]{2,1,0:T(8,128)(2,1)S(1)} all-to-all(bf16[16,40,256]{2,1,0:T(8,128)(2,1)} %get-tuple-element.14), channel_id=1, replica_groups=mesh['z'=8,'y'=8,'c'=2,'x'=4] {'y','c'}, dimensions={0} | all-to-all | bytes 655360 | tf_op jit(solution)/shard_map/all_to_all | solution.py:20
  89.6 0.6 pad_maximum_fusion
  90.2 6.4 %all-to-all-start.3 = ((bf16[8,8,256]{2,1,0:T(8,128)(2,1)}), bf16[8,8,256]{2,1,0:T(8,128)(2,1)S(1)}, u32[]{:S(2)}, u32[]{:S(2)}) async-start(bf16[8,8,256]{2,1,0:T(8,128)(2,1)} %pad_maximum_fusion), calls=%async_computation.3 | async-start | bytes 65536 | tf_op jit(solution)/shard_map/all_to_all | solution.py:20
  96.6 7.0 %all-to-all-done.3.sums_ref = bf16[8,8,256]{2,1,0:T(8,128)(2,1)S(1)} async-done(((bf16[8,8,256]{2,1,0:T(8,128)(2,1)}), bf16[8,8,256]{2,1,0:T(8,128)(2,1)S(1)}, u32[]{:S(2)}, u32[]{:S(2)}) %all-to-all-start.3) | async-done | bytes 32800 | tf_op jit(solution)/shard_map/all_to_all | solution.py:20
  103.7 5.1 %shard_map.88 = bf16[1280,256]{1,0:T(8,128)(2,1)S(1)} custom-call(s32[6]{0:T(128)S(1)} %pad_add_fusion.info_ref, bf16[512,256]{1,0:T(8,128)(2,1)} %get-tuple-element.10.all_q_hbm, f32[1024,512]{1,0:T(8,128)} %get-tuple-element.11.weight_hbm, f32[1024,256]{1,0:T(8,128)} %get-tuple-element.12.e_hbm, bf16[1024,256]{1,0:T(8,128)(2,1)} %get-tuple-element.13.hid_hbm, ...), custom_call_target="tpu_custom_call" | custom-call | tf_op jit(solution)/shard_map/pallas_call | solution.py:285
  108.8 4.7 %all_to_all.46 = bf16[2,640,256]{2,1,0:T(8,128)(2,1)S(1)} all-to-all(bf16[2,640,256]{2,1,0:T(8,128)(2,1)S(1)} %bitcast.16), channel_id=1, replica_groups=mesh['z'=8,'y'=8,'c'=2,'x'=4] {'c'}, dimensions={0} | all-to-all | bytes 1310720 | tf_op jit(solution)/shard_map/all_to_all | solution.py:20
  113.5 0.3 reduce_sum.76
  113.8 15.6 %all_to_all.47 = bf16[8,80,256]{2,1,0:T(8,128)(2,1)S(1)} all-to-all(bf16[8,80,256]{2,1,0:T(8,128)(2,1)S(1)} %bitcast.19), channel_id=1, replica_groups=mesh['z'=8,'y'=8,'c'=2,'x'=4] {'y'}, dimensions={0} | all-to-all | bytes 655360 | tf_op jit(solution)/shard_map/all_to_all | solution.py:20
  129.5 13.4 %all_to_all.48 = bf16[8,80,256]{2,1,0:T(8,128)(2,1)S(1)} all-to-all(bf16[8,80,256]{2,1,0:T(8,128)(2,1)S(1)} %broadcast_in_dim.85), channel_id=1, replica_groups=mesh['z'=8,'y'=8,'c'=2,'x'=4] {'z'}, dimensions={0} | all-to-all | bytes 655360 | tf_op jit(solution)/shard_map/all_to_all | solution.py:20
  143.0 12.9 %all_to_all.49 = bf16[8,80,256]{2,1,0:T(8,128)(2,1)S(1)} all-to-all(bf16[8,80,256]{2,1,0:T(8,128)(2,1)S(1)} %broadcast_in_dim.86), channel_id=1, replica_groups=mesh['z'=8,'y'=8,'c'=2,'x'=4] {'y'}, dimensions={0} | all-to-all | bytes 655360 | tf_op jit(solution)/shard_map/all_to_all | solution.py:20
  156.0 8.2 %all_to_all.50 = bf16[2,640,256]{2,1,0:T(8,128)(2,1)S(1)} all-to-all(bf16[2,640,256]{2,1,0:T(8,128)(2,1)S(1)} %broadcast_in_dim.88), channel_id=1, replica_groups=mesh['z'=8,'y'=8,'c'=2,'x'=4] {'c'}, dimensions={0} | all-to-all | bytes 1310720 | tf_op jit(solution)/shard_map/all_to_all | solution.py:20
  164.2 0.8 slice.50
  165.0 0.7 slice.51
  (38 shorter events, 0.5 us)
Async XLA Ops:
  0.6 9.5 %copy-start = (s32[131072]{0:T(1024)S(1)}, s32[131072]{0:T(1024)}, u32[]{:S(2)}) copy-start(s32[131072]{0:T(1024)} %param.13) | copy-start | bytes 1572868
  5.2 4.9 %copy-start.5 = (s32[4,128]{1,0:T(4,128)S(1)}, s32[4,128]{1,0:T(4,128)}, u32[]{:S(2)}) copy-start(s32[4,128]{1,0:T(4,128)} %param.11) | copy-start | bytes 6148
  5.2 4.9 %copy-start.6 = (s32[4]{0:T(128)S(1)}, s32[4]{0:T(128)}, u32[]{:S(2)}) copy-start(s32[4]{0:T(128)} %param.12) | copy-start | bytes 52
  5.2 14.8 %all-to-all-start = ((f32[4,264,256]{2,1,0:T(8,128)}), f32[4,264,256]{2,1,0:T(8,128)S(1)}, u32[]{:S(2)}, u32[]{:S(2)}) async-start(f32[4,264,256]{2,1,0:T(8,128)} %get-tuple-element.9), calls=%async_computation | async-start | bytes 2162688 | tf_op jit(solution)/shard_map/all_to_all | solution.py:20
  21.1 41.5 %all-to-all-start.1 = ((bf16[128,4,384]{2,1,0:T(4,128)(2,1)}), bf16[128,4,384]{2,1,0:T(4,128)(2,1)S(1)}, u32[]{:S(2)}, u32[]{:S(2)}) async-start(bf16[128,4,384]{2,1,0:T(4,128)(2,1)} %fusion.3), calls=%async_computation.1 | async-start | bytes 786432 | tf_op jit(solution)/shard_map/all_to_all | solution.py:20
  44.6 18.2 %collective-permute-start = (f32[256,256]{1,0:T(8,128)S(1)}, f32[256,256]{1,0:T(8,128)}, u32[]{:S(2)}, u32[]{:S(2)}) collective-permute-start(f32[256,256]{1,0:T(8,128)S(1)} %tanh.6.own_ref), channel_id=1, source_target_pairs={{0,1},{1,2},{2,3},{3,0},{4,5},{5,6},{6,7},{7,4},{8,9},{9,10},{10,1... | collective-permute-start | bytes 786440 | tf_op jit(solution)/shard_map/ppermute | solution.py:354
  46.8 16.0 %collective-permute-start.1 = (f32[256,256]{1,0:T(8,128)S(1)}, f32[256,256]{1,0:T(8,128)}, u32[]{:S(2)}, u32[]{:S(2)}) collective-permute-start(f32[256,256]{1,0:T(8,128)S(1)} %tanh.6.own_ref), channel_id=1, source_target_pairs={{0,2},{1,3},{2,0},{3,1},{4,6},{5,7},{6,4},{7,5},{8,10},{9,11},{10,... | collective-permute-start | bytes 786440 | tf_op jit(solution)/shard_map/ppermute | solution.py:354
  50.5 12.5 %collective-permute-start.2 = (f32[256,256]{1,0:T(8,128)S(1)}, f32[256,256]{1,0:T(8,128)}, u32[]{:S(2)}, u32[]{:S(2)}) collective-permute-start(f32[256,256]{1,0:T(8,128)S(1)} %tanh.6.own_ref), channel_id=1, source_target_pairs={{0,3},{1,0},{2,1},{3,2},{4,7},{5,4},{6,5},{7,6},{8,11},{9,8},{10,9... | collective-permute-start | bytes 786440 | tf_op jit(solution)/shard_map/ppermute | solution.py:354
  62.7 33.9 %copy-start.4 = (bf16[4,1024]{1,0:T(4,128)(2,1)S(1)}, bf16[4,1024]{1,0:T(4,128)(2,1)}, u32[]{:S(2)}) copy-start(bf16[4,1024]{1,0:T(4,128)(2,1)} %q_hbm.1) | copy-start | bytes 24580
  62.7 41.0 %copy-start.1 = (bf16[1024,1024]{1,0:T(8,128)(2,1)S(1)}, bf16[1024,1024]{1,0:T(8,128)(2,1)}, u32[]{:S(2)}) copy-start(bf16[1024,1024]{1,0:T(8,128)(2,1)} %x_ref.1) | copy-start | bytes 6291460
  62.7 40.9 %copy-start.2 = (bf16[256,256]{1,0:T(8,128)(2,1)S(1)}, bf16[256,256]{1,0:T(8,128)(2,1)}, u32[]{:S(2)}) copy-start(bf16[256,256]{1,0:T(8,128)(2,1)} %w_out_ref.1) | copy-start | bytes 393220
  62.7 40.9 %copy-start.3 = (bf16[16,256]{1,0:T(8,128)(2,1)S(1)}, bf16[16,256]{1,0:T(8,128)(2,1)}, u32[]{:S(2)}) copy-start(bf16[16,256]{1,0:T(8,128)(2,1)} %get-tuple-element.15.hid_q_ref) | copy-start | bytes 24580
  90.2 13.5 %all-to-all-start.3 = ((bf16[8,8,256]{2,1,0:T(8,128)(2,1)}), bf16[8,8,256]{2,1,0:T(8,128)(2,1)S(1)}, u32[]{:S(2)}, u32[]{:S(2)}) async-start(bf16[8,8,256]{2,1,0:T(8,128)(2,1)} %pad_maximum_fusion), calls=%async_computation.3 | async-start | bytes 65536 | tf_op jit(solution)/shard_map/all_to_all | solution.py:20

commit v5 on v4

--- a/solution.py
+++ b/solution.py
@@ -134,25 +134,30 @@
 
 def score_kernel(
     few, slots, scale, info_ref, own_ref, by1_ref, by2_ref, by3_ref, msg_ref,
-    weight_hbm, e_hbm, all_q_hbm, pay_hbm, weight_ref, e_ref, all_q_ref, pay_ref, code, digit, total_u, sems,
+    weight_hbm, layer_hbm, all_q_hbm, pay_hbm, weight_ref, layer_ref, all_q_ref, pay_ref, code, digit, total_u, sems,
 ):
     copies = Copies(sems)
-    queries = msg_ref.shape[0]
-    width = e_ref.shape[1]
+    lines = msg_ref.shape[0]
+    width = layer_ref.shape[1]
+    queries = lines * 2
     group = queries // few
     near = (own_ref, by1_ref, by2_ref, by3_ref)
     for far, ref in enumerate(near):
         first = lax.rem(info_ref[few + 1] + len(near) - far, len(near)) * ROWS
-        e_ref[pl.ds(pl.multiple_of(first, ROWS), ROWS), :] = ref[...]
-
-    line = lax.broadcasted_iota(jnp.int32, (queries, queries), 0)
-    column = lax.broadcasted_iota(jnp.int32, (queries, queries), 1)
-    order = jnp.where(column == (line % group) * few + line // group, 1.0, 0.0).astype(BF16)
+        layer_ref[pl.ds(pl.multiple_of(first, ROWS), ROWS), :] = ref[...]
+
+    line = lax.broadcasted_iota(jnp.int32, (lines, lines), 0)
+    column = lax.broadcasted_iota(jnp.int32, (lines, lines), 1)
+    order = jnp.where(column == (line % group) * 2 + line // group, 1.0, 0.0).astype(BF16)
     turned = dot(order, msg_ref[...])
-    all_q = turned[:, :width].astype(BF16)
+    parts = []
+    for i in range(few):
+        first = (i % 2) * width
+        parts.append(turned[(i // 2) * group : (i // 2 + 1) * group, first : first + width])
+    all_q = jnp.concatenate(parts, 0).astype(BF16)
     all_q_ref[...] = all_q
-    stores = [copies.start(e_ref, e_hbm), copies.start(all_q_ref, all_q_hbm)]
-    asked = turned[:group, width:].T
+    stores = [copies.start(layer_ref, layer_hbm), copies.start(all_q_ref, all_q_hbm)]
+    asked = turned[:group, 2 * width :].T
     who = asked[2 * slots : 3 * slots]
     code[:slots, :] = jnp.where(who > 0.0, asked[:slots] * 32.0 + asked[slots : 2 * slots], -1.0)
     power = jnp.zeros_like(who)
@@ -165,8 +170,8 @@
         digit[slots + i : slots + i + 1, :] = jnp.full((1, group), 32.0**i, F32)
 
     total_d = jnp.zeros((1, queries), F32)
-    for block, chunk in enumerate(blocks_of(e_ref.shape[0])):
-        e16 = e_ref[chunk, :].astype(BF16)
+    for block, chunk in enumerate(blocks_of(layer_ref.shape[0])):
+        e16 = jnp.tanh(layer_ref[chunk, :].astype(F32)).astype(BF16)
         grown = jnp.exp(scale * dot_lanes(e16, all_q))
         ids = row_ids(block, (ROWS, group))
         digits = jnp.zeros((ROWS, group), F32)
@@ -175,10 +180,11 @@
         digits = digits.astype(jnp.int32)
         times = [((digits >> (5 * i)) & 31).astype(F32) for i in range(few)]
         weight = jnp.concatenate(times, 1) * grown
-        weight_ref[chunk, :] = weight
+        weight16 = weight.astype(BF16)
+        weight_ref[chunk, :] = weight16
         stores.append(copies.start(weight_ref.at[chunk, :], weight_hbm.at[chunk, :]))
         total_d = total_d + jnp.sum(weight, 0, keepdims=True)
-        part = dot_rows(weight.astype(BF16), e16)
+        part = dot_rows(weight16, e16)
         total_u[...] = part if block == 0 else total_u[...] + part
 
     d = jnp.concatenate([total_d[:, i * width : (i + 1) * width] for i in range(queries // width)], 0)
@@ -192,24 +198,24 @@
         store.wait()
 
 
-def score(info, embs, message, few, slots, scale, peers):
-    share, width = embs[0].shape
-    items = share * len(embs)
-    queries, wide = message.shape
+def score(info, layers, message, few, slots, scale, peers):
+    share, width = layers[0].shape
+    items = share * len(layers)
+    queries = 2 * message.shape[0]
     pay = (peers, queries // peers + 8, width)
     return pl.pallas_call(
         functools.partial(score_kernel, few, slots, scale),
-        in_specs=[pl.BlockSpec(memory_space=pltpu.SMEM)] + [NEAR] * (len(embs) + 1),
+        in_specs=[pl.BlockSpec(memory_space=pltpu.SMEM)] + [NEAR] * (len(layers) + 1),
         out_specs=[FAR] * 4,
         out_shape=[
-            pltpu.HBM((items, queries), F32),
-            pltpu.HBM((items, width), F32),
+            pltpu.HBM((items, queries), BF16),
+            pltpu.HBM((items, width), BF16),
             pltpu.HBM((queries, width), BF16),
             pltpu.HBM(pay, BF16),
         ],
         scratch_shapes=[
-            pltpu.VMEM((items, queries), F32),
-            pltpu.VMEM((items, width), F32),
+            pltpu.VMEM((items, queries), BF16),
+            pltpu.VMEM((items, width), BF16),
             pltpu.VMEM((queries, width), BF16),
             pltpu.VMEM(pay, BF16),
             pltpu.VMEM((slots + 8, queries // few), F32),
@@ -218,64 +224,78 @@
             pltpu.SemaphoreType.DMA((3 + items // ROWS,)),
         ],
         compiler_params=pltpu.CompilerParams(vmem_limit_bytes=VMEM),
-    )(info, *embs, message)
+    )(info, *layers, message)
 
 
 def backward_kernel(
-    few, scale, info_ref, all_q_hbm, weight_hbm, e_hbm, hid_hbm, sums_ref, w_out_ref, x_ref,
-    emb_q_ref, hid_q_ref, q_ref, out_ref, all_q_ref, weight_ref, e_ref, hid_ref, tanh_grad, pre_grad, sems,
+    few, scale, info_ref, all_q_hbm, weight_hbm, layer_hbm, hid_hbm, sums_ref, w_out_ref, x_ref,
+    emb_q_ref, hid_q_ref, q_ref, mine_ref, other_ref,
+    all_q_ref, weight_ref, layer_ref, hid_ref, tanh_grad, pre_grad, summed, sems,
 ):
     copies = Copies(sems)
     load_q = copies.start(all_q_hbm, all_q_ref)
     loads = []
-    for chunk in blocks_of(e_ref.shape[0]):
-        pairs = ((weight_hbm, weight_ref), (e_hbm, e_ref), (hid_hbm, hid_ref))
+    for chunk in blocks_of(layer_ref.shape[0]):
+        pairs = ((weight_hbm, weight_ref), (layer_hbm, layer_ref), (hid_hbm, hid_ref))
         loads.append([copies.start(source.at[chunk, :], target.at[chunk, :]) for source, target in pairs])
     queries = all_q_ref.shape[0]
-    items, width = e_ref.shape
+    items, width = layer_ref.shape
     feats = x_ref.shape[1]
     group = queries // few
     sums = jnp.sum(sums_ref[...].astype(F32), 0)
     d = sums[few : few + 2] + sums[few + 2 : few + 4]
     d = jnp.concatenate([d[0:1], d[1:2]], 1)
-    factor = scale / d
-    lane = lax.broadcasted_iota(jnp.int32, (1, queries), 1)
-    position = jnp.full((1, queries), -1.0, F32)
-    for i in range(few):
-        position = jnp.where(lane == info_ref[few] + i * group, info_ref[i].astype(F32), position)
+    factor = jnp.broadcast_to(scale / d, (8, queries)).T[:, :1]
+    emb_q = emb_q_ref[...]
+    own_q = jnp.concatenate([emb_q, jnp.zeros_like(emb_q)], 0).astype(BF16)
+    load_q.wait()
+    scaled = all_q_ref[...].astype(F32) * factor
+    high = scaled.astype(BF16)
+    low = (scaled - high.astype(F32)).astype(BF16)
 
     pos_emb = jnp.zeros((16, width), F32)
-    load_q.wait()
     for block, chunk in enumerate(blocks_of(items)):
         for copy in loads[block]:
             copy.wait()
-        e = e_ref[chunk, :]
-        hot = jnp.where(position == row_ids(block, (ROWS, queries)), scale, 0.0)
-        coefficient = (weight_ref[chunk, :] * factor - hot).astype(BF16)
-        grad = (dot(coefficient, all_q_ref[...]) * (1.0 - e * e)).astype(BF16)
-        tanh_grad[chunk, :] = grad
-        hid_grad = dot_lanes(grad, w_out_ref[...])
-        pre_grad[chunk, :] = jnp.where(hid_ref[chunk, :] > 0, hid_grad, 0.0).astype(BF16)
+        e = jnp.tanh(layer_ref[chunk, :].astype(F32))
         place = lax.broadcasted_iota(jnp.int32, (16, ROWS), 1) + block * ROWS
         line = lax.broadcasted_iota(jnp.int32, (16, ROWS), 0)
         picked = jnp.zeros((16, ROWS), F32)
         for i in range(few):
             picked = jnp.where((line == i) & (place == info_ref[i]), 1.0, picked)
-        pos_emb = pos_emb + dot(picked.astype(BF16), e.astype(BF16))
+        picked = picked.astype(BF16)
+        pos_emb = pos_emb + dot(picked, e.astype(BF16))
+        weight = weight_ref[chunk, :]
+        item_grad = dot(weight, high) + dot(weight, low) - scale * dot_rows(picked, own_q)
+        grad = (item_grad * (1.0 - e * e)).astype(BF16)
+        tanh_grad[chunk, :] = grad
+        hid_grad = dot_lanes(grad, w_out_ref[...])
+        pre_grad[chunk, :] = jnp.where(hid_ref[chunk, :] > 0, hid_grad, 0.0).astype(BF16)
 
     line = lax.broadcasted_iota(jnp.int32, (8, queries), 0)
     own_lane = lax.broadcasted_iota(jnp.int32, (8, queries), 1)
     own_d = jnp.sum(jnp.where(own_lane == line * group + info_ref[few], d, 0.0), 1, keepdims=True)
     live = lax.broadcasted_iota(jnp.int32, (8, width), 0) < few
-    emb_q = emb_q_ref[...]
     grad = scale * (sums / own_d - pos_emb[:8]) * (1.0 - emb_q * emb_q)
     grad = jnp.where(live, grad, 0.0)
     grad_q = jnp.concatenate([grad, jnp.zeros_like(grad)], 0).astype(BF16)
     hid_q = hid_q_ref[...]
     pre_grad_q = jnp.where(hid_q > 0, dot_lanes(grad_q, w_out_ref[...]), 0.0).astype(BF16)
-    out_ref[feats:, :] = (dot_rows(hid_ref[...], tanh_grad[...]) + dot_rows(hid_q, grad_q)).astype(BF16)
     in_total = dot_rows(pre_grad[...], x_ref[...]) + dot_rows(pre_grad_q, q_ref[...])
-    out_ref[:feats, :] = in_total.astype(BF16).T
+    summed[:feats, :] = in_total.astype(BF16).T
+    summed[feats:, :] = (dot_rows(hid_ref[...], tanh_grad[...]) + dot_rows(hid_q, grad_q)).astype(BF16)
+    half = mine_ref.shape[0]
+    core = info_ref[few + 2]
+
+    @pl.when(core == 0)
+    def _():
+        mine_ref[...] = summed[:half, :]
+        other_ref[...] = summed[half:, :]
+
+    @pl.when(core != 0)
+    def _():
+        mine_ref[...] = summed[half:, :]
+        other_ref[...] = summed[:half, :]
 
 
 def backward(info, far, near, few, scale):
@@ -285,16 +305,55 @@
     return pl.pallas_call(
         functools.partial(backward_kernel, few, scale),
         in_specs=[pl.BlockSpec(memory_space=pltpu.SMEM)] + [FAR] * len(far) + [NEAR] * len(near),
-        out_specs=NEAR,
-        out_shape=jax.ShapeDtypeStruct((feats + units, width), BF16),
+        out_specs=[NEAR] * 2,
+        out_shape=[jax.ShapeDtypeStruct(((feats + units) // 2, width), BF16)] * 2,
         scratch_shapes=[
             *[pltpu.VMEM(a.shape, a.dtype) for a in far],
             pltpu.VMEM((items, width), BF16),
             pltpu.VMEM((items, units), BF16),
+            pltpu.VMEM((feats + units, width), BF16),
             pltpu.SemaphoreType.DMA((1 + 3 * (items // ROWS),)),
         ],
         compiler_params=pltpu.CompilerParams(vmem_limit_bytes=VMEM),
     )(info, *pinned(*far), *near)
+
+
+def assemble_kernel(core_ref, mine_ref, other_ref, in_hbm, out_hbm, sems):
+    half = mine_ref.shape[0]
+    rest = in_hbm.shape[0] - half
+
+    def place(first, second):
+        copies = Copies(sems)
+        made = [
+            copies.start(first, in_hbm.at[pl.ds(0, half), :]),
+            copies.start(second.at[pl.ds(0, rest), :], in_hbm.at[pl.ds(half, rest), :]),
+            copies.start(second.at[pl.ds(rest, half - rest), :], out_hbm),
+        ]
+        for copy in made:
+            copy.wait()
+
+    @pl.when(core_ref[0] == 0)
+    def _():
+        place(mine_ref, other_ref)
+
+    @pl.when(core_ref[0] != 0)
+    def _():
+        place(other_ref, mine_ref)
+
+
+def assemble(mine, other, feats):
+    half, width = mine.shape
+    return pl.pallas_call(
+        assemble_kernel,
+        in_specs=[pl.BlockSpec(memory_space=pltpu.SMEM)] + [NEAR] * 2,
+        out_specs=[FAR] * 2,
+        out_shape=[
+            jax.ShapeDtypeStruct((feats, width), BF16),
+            jax.ShapeDtypeStruct((2 * half - feats, width), BF16),
+        ],
+        scratch_shapes=[pltpu.SemaphoreType.DMA((3,))],
+        compiler_params=pltpu.CompilerParams(vmem_limit_bytes=VMEM),
+    )(lax.axis_index("c").reshape(1), mine, other)
 
 
 def request_codes(rows, query_count, item_count, capacity, order, dp_count):
@@ -333,7 +392,8 @@
     named = jnp.concatenate([negatives.reshape(-1), positives])
     rows = jnp.take(owner_map, named, axis=0)
     pos_local = rows[few * negative_count :] - own_index * item_count
-    info = jnp.concatenate([pos_local, jnp.stack([lax.axis_index(YCZ), lax.axis_index("x")])])
+    places = [lax.axis_index(YCZ), lax.axis_index("x"), lax.axis_index("c")]
+    info = jnp.concatenate([pos_local, jnp.stack(places)])
     codes = request_codes(
         rows[: few * negative_count],
         few,
@@ -342,18 +402,18 @@
         lambda o: (o % yc_count) * z_count + o // yc_count,
         dp_count,
     )
-    codes = jnp.pad(codes[:, None, :], ((0, 0), (0, few - 1), (0, 0)))
-
-    own = jnp.tanh(total(arrived[:, :ROWS]))
+    codes = jnp.pad(codes[:, None, :], ((0, 0), (0, 1), (0, 0)))
+
+    own = total(arrived[:, :ROWS]).astype(BF16)
     own_q = jnp.tanh(total(arrived[:, ROWS:]))
-    sent_q = jnp.broadcast_to(own_q[None, :few].astype(BF16), (dp_count, few, width))
+    sent_q = jnp.broadcast_to(own_q[:few].astype(BF16).reshape(1, 2, -1), (dp_count, 2, few // 2 * width))
     message = exchange(jnp.concatenate([sent_q, codes], 2), YCZ)
-    message = message.reshape(queries, width + 128)
-    embs = [own]
+    message = message.reshape(2 * dp_count, -1)
+    layers = [own]
     for far in range(1, x_count):
-        embs.append(lax.ppermute(own, "x", [(i, (i + far) % x_count) for i in range(x_count)]))
-
-    weight, item_emb, all_q, pay = score(info, embs, message, few, capacity, scale, yc_count)
+        layers.append(lax.ppermute(own, "x", [(i, (i + far) % x_count) for i in range(x_count)]))
+
+    weight, layer_out, all_q, pay = score(info, layers, message, few, capacity, scale, yc_count)
     first = total(exchange(pay, ("y", "c")))
     mine = queries // yc_count
     d_rows = queries // width
@@ -372,15 +432,14 @@
     )
     feats_q = jnp.pad(query_feats, ((0, 16 - few), (0, 0)))
     near = (sums, w_out, item_feats, own_q, hidden_q, feats_q)
-    grads = backward(info, (all_q, weight, item_emb, hidden), near, few, scale)
-    depth = grads.shape[0]
-    c_count, y_count = lax.axis_size("c"), lax.axis_size("y")
-    grads = total(exchange(grads.reshape(c_count, depth // c_count, width), "c"))
-    grads = total(exchange(grads.astype(BF16).reshape(y_count, -1, width), "y"))
+    mine, other = backward(info, (all_q, weight, layer_out, hidden), near, few, scale)
+    y_count = lax.axis_size("y")
+    swap = [(0, 1), (1, 0)]
+    grads = (mine.astype(F32) + lax.ppermute(other, "c", swap).astype(F32)).astype(BF16)
+    grads = total(exchange(grads.reshape(y_count, -1, width), "y"))
     grads = total(spread(grads.astype(BF16), "z")).astype(BF16)
     grads = spread(grads, "y").reshape(-1, width)
-    grads = spread(grads, "c").reshape(-1, width)
-    return grads[: w_in.shape[0]], grads[w_in.shape[0] :]
+    return tuple(assemble(grads, lax.ppermute(grads, "c", swap), w_in.shape[0]))
 
 
 def solution(mesh):

time: 166 us -> 158 us (0.952)
  blocking collectives: 76.7 us -> 59.7 us
  starting transfers between devices: 43.1 us -> 52 us
    all_to_all x6 -> x4, blocking collectives: 76.7 us -> 59.7 us  [exchange(): return lax.all_to_all(blocks, axes, split_axis=0, concat_axis=0, tiled=True)]
    ppermute x0 -> x2, starting transfers between devices: none -> 8.99 us  [the longest x1 6.24 us: local(): return tuple(assemble(grads, lax.ppermute(grads, 'c', swap), w_in.shape[0]))]
    ppermute x0 -> x2, waiting for transfers between devices: none -> 2.47 us  [the longest x1 1.23 us: local(): lax.ppermute(other, 'c', swap).astype(F32)]
  transfers between devices with their start and end apart: 6 -> 8, of which waited for: 4 -> 5; matrix products, arithmetic and copies ran while one was open for 3% -> 3% of each run, Pallas kernels for 0% -> 0%
where the time goes in v5:
time: 158 us
  blocking collectives  59.7 us (38%)
  starting transfers between devices  52 us (33%)
  waiting for transfers between devices  22.7 us (14%)
  Pallas kernels  15.1 us (10%)
  local copies, waits for them, and re-layouts  4.08 us (3%)
  other arithmetic  2.14 us (1%)
    all_to_all x4, blocking collectives, exchange(): return lax.all_to_all(blocks, axes, split_axis=0, concat_axis=0, tiled=True)  59.7 us
    all_to_all x3, starting transfers between devices, exchange(): return lax.all_to_all(blocks, axes, split_axis=0, concat_axis=0, tiled=True)  34.6 us
    all_to_all x3, waiting for transfers between devices, exchange(): return lax.all_to_all(blocks, axes, split_axis=0, concat_axis=0, tiled=True)  20.2 us
    ppermute x3, starting transfers between devices, local(): lax.ppermute(own, 'x', [(i, (i + far) % x_count) for i in range(x_count)])  8.42 us
    ppermute x1, starting transfers between devices, local(): return tuple(assemble(grads, lax.ppermute(grads, 'c', swap), w_in.shape[0]))  6.24 us
    pallas_call x1, Pallas kernels, backward(): pl.pallas_call(functools.partial(backward_kernel, few, scale), in_specs=[...  5.38 us
    pallas_call x1, Pallas kernels, forward(): pl.pallas_call(forward_kernel, in_specs=[FAR] * 4, out_specs=[FAR] * 3, o...  4.56 us
    pallas_call x1, Pallas kernels, score(): pl.pallas_call(functools.partial(score_kernel, few, slots, scale), in_spe...  4.28 us
  transfers between devices with their start and end apart: 8, of which 5 were waited for; matrix products, arithmetic and copies ran while one was open for 3% of the time, Pallas kernels for 0%

profile of v5, /device:TPU:1, one launch (start us, length us, event | category | flops | bytes accessed | tf_op | source)
XLA Modules:
  0.0 157.7 jit_solution(6964766750771036507)
XLA Ops:
  0.6 4.6 %shard_map.86 = (f32[4,264,256]{2,1,0:T(8,128)}, bf16[1024,256]{1,0:T(8,128)(2,1)}, bf16[16,256]{1,0:T(8,128)(2,1)}) custom-call(bf16[4,1024]{1,0:T(4,128)(2,1)} %q_hbm.1, bf16[1024,1024]{1,0:T(8,128)(2,1)} %x_ref.1, bf16[1024,256]{1,0:T(8,128)(2,1)} %w_in_hbm.1, bf16[256,256]{1,0:T(8,128)(2,1)} %w_out_ref.1), custom_call_target="tpu_custom_call" | custom-call | tf_op jit(solution)/shard_map/pallas_call | solution.py:107
  5.2 4.9 %all-to-all-start = ((f32[4,264,256]{2,1,0:T(8,128)}), f32[4,264,256]{2,1,0:T(8,128)S(1)}, u32[]{:S(2)}, u32[]{:S(2)}) async-start(f32[4,264,256]{2,1,0:T(8,128)} %get-tuple-element.11), calls=%async_computation | async-start | bytes 2162688 | tf_op jit(solution)/shard_map/all_to_all | solution.py:20
  10.1 3.6 %gather_fusion = s32[516]{0:T(1024)S(1)} fusion(s32[131072]{0:T(1024)S(1)} %copy-done, s32[1024]{0:T(1024)S(1)} %pad_clamp_fusion), kind=kCustom, calls=%fused_computation | custom fusion | bytes 6192 | tf_op jit(solution)/shard_map/jit(_take)/gather | solution.py:393
  13.8 0.3 fusion
  14.1 0.7 fusion.1
  14.8 0.1 copy.14
  14.9 5.1 %all-to-all-done = f32[4,264,256]{2,1,0:T(8,128)S(1)} async-done(((f32[4,264,256]{2,1,0:T(8,128)}), f32[4,264,256]{2,1,0:T(8,128)S(1)}, u32[]{:S(2)}, u32[]{:S(2)}) %all-to-all-start) | async-done | bytes 1081376 | tf_op jit(solution)/shard_map/all_to_all | solution.py:20
  20.1 0.1 broadcast_in_dim.72
  20.2 1.0 fusion.2
  21.2 23.4 %all-to-all-start.1 = ((bf16[128,2,640]{2,1,0:T(2,128)(2,1)}), bf16[128,2,640]{2,1,0:T(2,128)(2,1)S(1)}, u32[]{:S(2)}, u32[]{:S(2)}) async-start(bf16[128,2,640]{2,1,0:T(2,128)(2,1)} %fusion.2), calls=%async_computation.1 | async-start | bytes 655360 | tf_op jit(solution)/shard_map/all_to_all | solution.py:20
  44.7 0.1 slice_reduce_fusion.own_ref
  44.7 2.2 %collective-permute-start = (bf16[256,256]{1,0:T(8,128)(2,1)S(1)}, bf16[256,256]{1,0:T(8,128)(2,1)S(1)}, u32[]{:S(2)}, u32[]{:S(2)}) collective-permute-start(bf16[256,256]{1,0:T(8,128)(2,1)S(1)} %slice_reduce_fusion.own_ref), channel_id=1, source_target_pairs={{0,1},{1,2},{2,3},{3,0},{4,5},{5,6},{6,7},{7,4},{8,9},{9,10},{10,1... | collective-permute-start | bytes 393224 | tf_op jit(solution)/shard_map/ppermute | solution.py:414
  46.9 3.7 %collective-permute-start.1 = (bf16[256,256]{1,0:T(8,128)(2,1)S(1)}, bf16[256,256]{1,0:T(8,128)(2,1)S(1)}, u32[]{:S(2)}, u32[]{:S(2)}) collective-permute-start(bf16[256,256]{1,0:T(8,128)(2,1)S(1)} %slice_reduce_fusion.own_ref), channel_id=1, source_target_pairs={{0,2},{1,3},{2,0},{3,1},{4,6},{5,7},{6,4},{7,5},{8,10},{9,11},{10,... | collective-permute-start | bytes 393224 | tf_op jit(solution)/shard_map/ppermute | solution.py:414
  50.6 2.5 %collective-permute-start.2 = (bf16[256,256]{1,0:T(8,128)(2,1)S(1)}, bf16[256,256]{1,0:T(8,128)(2,1)}, u32[]{:S(2)}, u32[]{:S(2)}) collective-permute-start(bf16[256,256]{1,0:T(8,128)(2,1)S(1)} %slice_reduce_fusion.own_ref), channel_id=1, source_target_pairs={{0,3},{1,0},{2,1},{3,2},{4,7},{5,4},{6,5},{7,6},{8,11},{9,8},{10,9... | collective-permute-start | bytes 393224 | tf_op jit(solution)/shard_map/ppermute | solution.py:414
  53.2 0.1 pad_add_fusion.info_ref
  53.3 8.1 %all-to-all-done.1 = bf16[128,2,640]{2,1,0:T(2,128)(2,1)S(1)} async-done(((bf16[128,2,640]{2,1,0:T(2,128)(2,1)}), bf16[128,2,640]{2,1,0:T(2,128)(2,1)S(1)}, u32[]{:S(2)}, u32[]{:S(2)}) %all-to-all-start.1) | async-done | bytes 327712 | tf_op jit(solution)/shard_map/all_to_all | solution.py:20
  61.4 0.1 reshape.150.msg_ref
  61.5 4.3 %shard_map.87 = (bf16[1024,512]{1,0:T(8,128)(2,1)}, bf16[1024,256]{1,0:T(8,128)(2,1)}, bf16[512,256]{1,0:T(8,128)(2,1)}, bf16[16,40,256]{2,1,0:T(8,128)(2,1)}) custom-call(s32[7]{0:T(128)S(1)} %pad_add_fusion.info_ref, bf16[256,256]{1,0:T(8,128)(2,1)S(1)} %slice_reduce_fusion.own_ref, bf16[256,256]{1,0:T(8,128)(2,1)S(1)} %collective-permute-done.by1_ref, ...), custom_call_target="tpu_custom_call" | custom-call | tf_op jit(solution)/shard_map/pallas_call | solution.py:206
  65.8 17.7 %all_to_all.35 = bf16[16,40,256]{2,1,0:T(8,128)(2,1)S(1)} all-to-all(bf16[16,40,256]{2,1,0:T(8,128)(2,1)} %get-tuple-element.16), channel_id=1, replica_groups=mesh['z'=8,'y'=8,'c'=2,'x'=4] {'y','c'}, dimensions={0} | all-to-all | bytes 655360 | tf_op jit(solution)/shard_map/all_to_all | solution.py:20
  83.7 0.6 pad_maximum_fusion
  84.3 6.4 %all-to-all-start.3 = ((bf16[8,8,256]{2,1,0:T(8,128)(2,1)}), bf16[8,8,256]{2,1,0:T(8,128)(2,1)S(1)}, u32[]{:S(2)}, u32[]{:S(2)}) async-start(bf16[8,8,256]{2,1,0:T(8,128)(2,1)} %pad_maximum_fusion), calls=%async_computation.3 | async-start | bytes 65536 | tf_op jit(solution)/shard_map/all_to_all | solution.py:20
  90.7 7.0 %all-to-all-done.3.sums_ref = bf16[8,8,256]{2,1,0:T(8,128)(2,1)S(1)} async-done(((bf16[8,8,256]{2,1,0:T(8,128)(2,1)}), bf16[8,8,256]{2,1,0:T(8,128)(2,1)S(1)}, u32[]{:S(2)}, u32[]{:S(2)}) %all-to-all-start.3) | async-done | bytes 32800 | tf_op jit(solution)/shard_map/all_to_all | solution.py:20
  97.8 5.4 %shard_map.88 = (bf16[640,256]{1,0:T(8,128)(2,1)S(1)}, bf16[640,256]{1,0:T(8,128)(2,1)S(1)}) custom-call(s32[7]{0:T(128)S(1)} %pad_add_fusion.info_ref, bf16[512,256]{1,0:T(8,128)(2,1)} %get-tuple-element.12.all_q_hbm, bf16[1024,512]{1,0:T(8,128)(2,1)} %get-tuple-element.13.weight_hbm, bf16[1024,256]{1,0:T(8,128)(2,1)} %get-tuple-element.14.layer_hbm, ...), custom_call_target="tpu_custom_call" | custom-call | tf_op jit(solution)/shard_map/pallas_call | solution.py:305
  103.2 2.7 %collective-permute-start.3 = (bf16[640,256]{1,0:T(8,128)(2,1)S(1)}, bf16[640,256]{1,0:T(8,128)(2,1)S(1)}, u32[]{:S(2)}, u32[]{:S(2)}) collective-permute-start(bf16[640,256]{1,0:T(8,128)(2,1)S(1)} %get-tuple-element.19), channel_id=1, source_target_pairs={{0,4},{4,0},{1,5},{5,1},{2,6},{6,2},{3,7},{7,3},{8,12},{12,8},{9,1... | collective-permute-start | bytes 983048 | tf_op jit(solution)/shard_map/ppermute | solution.py:438
  105.9 1.2 collective-permute-done.3
  107.2 0.1 add_convert_fusion
  107.3 15.6 %all_to_all.36 = bf16[8,80,256]{2,1,0:T(8,128)(2,1)S(1)} all-to-all(bf16[8,80,256]{2,1,0:T(8,128)(2,1)S(1)} %bitcast.17), channel_id=1, replica_groups=mesh['z'=8,'y'=8,'c'=2,'x'=4] {'y'}, dimensions={0} | all-to-all | bytes 655360 | tf_op jit(solution)/shard_map/all_to_all | solution.py:20
  123.0 13.4 %all_to_all.37 = bf16[8,80,256]{2,1,0:T(8,128)(2,1)S(1)} all-to-all(bf16[8,80,256]{2,1,0:T(8,128)(2,1)S(1)} %broadcast_in_dim.80), channel_id=1, replica_groups=mesh['z'=8,'y'=8,'c'=2,'x'=4] {'z'}, dimensions={0} | all-to-all | bytes 655360 | tf_op jit(solution)/shard_map/all_to_all | solution.py:20
  136.5 12.9 %all_to_all.38 = bf16[8,80,256]{2,1,0:T(8,128)(2,1)S(1)} all-to-all(bf16[8,80,256]{2,1,0:T(8,128)(2,1)S(1)} %broadcast_in_dim.81), channel_id=1, replica_groups=mesh['z'=8,'y'=8,'c'=2,'x'=4] {'y'}, dimensions={0} | all-to-all | bytes 655360 | tf_op jit(solution)/shard_map/all_to_all | solution.py:20
  149.4 6.2 %collective-permute-start.4 = (bf16[640,256]{1,0:T(8,128)(2,1)S(1)}, bf16[640,256]{1,0:T(8,128)(2,1)S(1)}, u32[]{:S(2)}, u32[]{:S(2)}) collective-permute-start(bf16[640,256]{1,0:T(8,128)(2,1)S(1)} %bitcast.15), channel_id=1, source_target_pairs={{0,4},{4,0},{1,5},{5,1},{2,6},{6,2},{3,7},{7,3},{8,12},{12,8},{9,1... | collective-permute-start | bytes 983048 | tf_op jit(solution)/shard_map/ppermute | solution.py:442
  155.6 1.2 collective-permute-done.4.other_ref
  156.9 0.9 shard_map.89
  (38 shorter events, 0.4 us)
Async XLA Ops:
  0.6 9.5 %copy-start = (s32[131072]{0:T(1024)S(1)}, s32[131072]{0:T(1024)}, u32[]{:S(2)}) copy-start(s32[131072]{0:T(1024)} %param.13) | copy-start | bytes 1572868
  5.2 4.9 %copy-start.5 = (s32[4,128]{1,0:T(4,128)S(1)}, s32[4,128]{1,0:T(4,128)}, u32[]{:S(2)}) copy-start(s32[4,128]{1,0:T(4,128)} %param.11) | copy-start | bytes 6148
  5.2 4.9 %copy-start.6 = (s32[4]{0:T(128)S(1)}, s32[4]{0:T(128)}, u32[]{:S(2)}) copy-start(s32[4]{0:T(128)} %param.12) | copy-start | bytes 52
  5.2 14.8 %all-to-all-start = ((f32[4,264,256]{2,1,0:T(8,128)}), f32[4,264,256]{2,1,0:T(8,128)S(1)}, u32[]{:S(2)}, u32[]{:S(2)}) async-start(f32[4,264,256]{2,1,0:T(8,128)} %get-tuple-element.11), calls=%async_computation | async-start | bytes 2162688 | tf_op jit(solution)/shard_map/all_to_all | solution.py:20
  21.2 40.1 %all-to-all-start.1 = ((bf16[128,2,640]{2,1,0:T(2,128)(2,1)}), bf16[128,2,640]{2,1,0:T(2,128)(2,1)S(1)}, u32[]{:S(2)}, u32[]{:S(2)}) async-start(bf16[128,2,640]{2,1,0:T(2,128)(2,1)} %fusion.2), calls=%async_computation.1 | async-start | bytes 655360 | tf_op jit(solution)/shard_map/all_to_all | solution.py:20
  44.7 16.8 %collective-permute-start = (bf16[256,256]{1,0:T(8,128)(2,1)S(1)}, bf16[256,256]{1,0:T(8,128)(2,1)S(1)}, u32[]{:S(2)}, u32[]{:S(2)}) collective-permute-start(bf16[256,256]{1,0:T(8,128)(2,1)S(1)} %slice_reduce_fusion.own_ref), channel_id=1, source_target_pairs={{0,1},{1,2},{2,3},{3,0},{4,5},{5,6},{6,7},{7,4},{8,9},{9,10},{10,1... | collective-permute-start | bytes 393224 | tf_op jit(solution)/shard_map/ppermute | solution.py:414
  46.9 14.6 %collective-permute-start.1 = (bf16[256,256]{1,0:T(8,128)(2,1)S(1)}, bf16[256,256]{1,0:T(8,128)(2,1)S(1)}, u32[]{:S(2)}, u32[]{:S(2)}) collective-permute-start(bf16[256,256]{1,0:T(8,128)(2,1)S(1)} %slice_reduce_fusion.own_ref), channel_id=1, source_target_pairs={{0,2},{1,3},{2,0},{3,1},{4,6},{5,7},{6,4},{7,5},{8,10},{9,11},{10,... | collective-permute-start | bytes 393224 | tf_op jit(solution)/shard_map/ppermute | solution.py:414
  50.6 10.9 %collective-permute-start.2 = (bf16[256,256]{1,0:T(8,128)(2,1)S(1)}, bf16[256,256]{1,0:T(8,128)(2,1)}, u32[]{:S(2)}, u32[]{:S(2)}) collective-permute-start(bf16[256,256]{1,0:T(8,128)(2,1)S(1)} %slice_reduce_fusion.own_ref), channel_id=1, source_target_pairs={{0,3},{1,0},{2,1},{3,2},{4,7},{5,4},{6,5},{7,6},{8,11},{9,8},{10,9... | collective-permute-start | bytes 393224 | tf_op jit(solution)/shard_map/ppermute | solution.py:414
  61.4 29.4 %copy-start.4 = (bf16[4,1024]{1,0:T(4,128)(2,1)S(1)}, bf16[4,1024]{1,0:T(4,128)(2,1)}, u32[]{:S(2)}) copy-start(bf16[4,1024]{1,0:T(4,128)(2,1)} %q_hbm.1) | copy-start | bytes 24580
  61.4 36.4 %copy-start.2 = (bf16[256,256]{1,0:T(8,128)(2,1)S(1)}, bf16[256,256]{1,0:T(8,128)(2,1)}, u32[]{:S(2)}) copy-start(bf16[256,256]{1,0:T(8,128)(2,1)} %w_out_ref.1) | copy-start | bytes 393220
  61.5 36.3 %copy-start.1 = (bf16[1024,1024]{1,0:T(8,128)(2,1)S(1)}, bf16[1024,1024]{1,0:T(8,128)(2,1)}, u32[]{:S(2)}) copy-start(bf16[1024,1024]{1,0:T(8,128)(2,1)} %x_ref.1) | copy-start | bytes 6291460
  61.5 36.3 %copy-start.3 = (bf16[16,256]{1,0:T(8,128)(2,1)S(1)}, bf16[16,256]{1,0:T(8,128)(2,1)}, u32[]{:S(2)}) copy-start(bf16[16,256]{1,0:T(8,128)(2,1)} %get-tuple-element.17.hid_q_ref) | copy-start | bytes 24580
  84.3 13.5 %all-to-all-start.3 = ((bf16[8,8,256]{2,1,0:T(8,128)(2,1)}), bf16[8,8,256]{2,1,0:T(8,128)(2,1)S(1)}, u32[]{:S(2)}, u32[]{:S(2)}) async-start(bf16[8,8,256]{2,1,0:T(8,128)(2,1)} %pad_maximum_fusion), calls=%async_computation.3 | async-start | bytes 65536 | tf_op jit(solution)/shard_map/all_to_all | solution.py:20
  103.2 4.0 %collective-permute-start.3 = (bf16[640,256]{1,0:T(8,128)(2,1)S(1)}, bf16[640,256]{1,0:T(8,128)(2,1)S(1)}, u32[]{:S(2)}, u32[]{:S(2)}) collective-permute-start(bf16[640,256]{1,0:T(8,128)(2,1)S(1)} %get-tuple-element.19), channel_id=1, source_target_pairs={{0,4},{4,0},{1,5},{5,1},{2,6},{6,2},{3,7},{7,3},{8,12},{12,8},{9,1... | collective-permute-start | bytes 983048 | tf_op jit(solution)/shard_map/ppermute | solution.py:438
  149.4 7.5 %collective-permute-start.4 = (bf16[640,256]{1,0:T(8,128)(2,1)S(1)}, bf16[640,256]{1,0:T(8,128)(2,1)S(1)}, u32[]{:S(2)}, u32[]{:S(2)}) collective-permute-start(bf16[640,256]{1,0:T(8,128)(2,1)S(1)} %bitcast.15), channel_id=1, source_target_pairs={{0,4},{4,0},{1,5},{5,1},{2,6},{6,2},{3,7},{7,3},{8,12},{12,8},{9,1... | collective-permute-start | bytes 983048 | tf_op jit(solution)/shard_map/ppermute | solution.py:442

commit v6 on v5

--- a/solution.py
+++ b/solution.py
@@ -59,33 +59,45 @@
 
 def forward_kernel(
     q_hbm, x_hbm, w_in_hbm, w_out_hbm, part_hbm, hid_hbm, hid_q_hbm,
-    q_buf, x_buf, w_in_buf, w_out_buf, part_buf, hid_buf, hid_q_buf, rows, sems,
+    q_buf, x_buf, w_in_buf, w_out_buf, part_buf, hid_buf, sems,
 ):
-    few = q_buf.shape[0]
-    chunks = blocks_of(x_buf.shape[0])
+    few, feats = q_buf.shape
+    steps = part_buf.shape[0]
+    lead = x_buf.shape[0] - steps * ROWS
     copies = Copies(sems)
     load_in = copies.start(w_in_hbm, w_in_buf)
     load_q = copies.start(q_hbm, q_buf)
-    load_x = [copies.start(x_hbm.at[chunks[0], :], x_buf.at[chunks[0], :])]
+    load_x = []
+    for i in range(steps):
+        source = x_hbm.at[pl.ds(i * ROWS, ROWS), :]
+        load_x.append(copies.start(source, x_buf.at[pl.ds(lead + i * ROWS, ROWS), :]))
     load_out = copies.start(w_out_hbm, w_out_buf)
-    for chunk in chunks[1:]:
-        load_x.append(copies.start(x_hbm.at[chunk, :], x_buf.at[chunk, :]))
-    rows[...] = jnp.zeros_like(rows)
+    load_q.wait()
+    padded = jnp.concatenate([q_buf[...].astype(F32), jnp.zeros((lead - few, feats), F32)], 0)
+    x_buf[:lead, :] = padded.astype(BF16)
+    stores = []
     load_in.wait()
-    load_q.wait()
-    rows[:few, :] = jnp.maximum(dot(q_buf[...], w_in_buf[...]), 0.0)
-    hid_q_buf[...] = rows[...].astype(BF16)
-    stores = [copies.start(hid_q_buf, hid_q_hbm)]
-    load_out.wait()
-    keep = dot(hid_q_buf[...], w_out_buf[...])[:8]
-    for i, chunk in enumerate(chunks):
-        load_x[i].wait()
-        hid = jnp.maximum(dot(x_buf[chunk, :], w_in_buf[...]), 0.0).astype(BF16)
-        hid_buf[chunk, :] = hid
-        part_buf[i, :ROWS, :] = dot(hid, w_out_buf[...])
-        part_buf[i, ROWS:, :] = keep
-        stores.append(copies.start(part_buf.at[i], part_hbm.at[i]))
-        stores.append(copies.start(hid_buf.at[chunk, :], hid_hbm.at[chunk, :]))
+    pair = 2
+    for i in range(0, steps, pair):
+        for load in load_x[i : i + pair]:
+            load.wait()
+        first = 0 if i == 0 else lead + i * ROWS
+        skip = lead if i == 0 else 0
+        span = pl.ds(first, skip + pair * ROWS)
+        hid = jnp.maximum(dot(x_buf[span, :], w_in_buf[...]), 0.0).astype(BF16)
+        hid_buf[span, :] = hid
+        if i == 0:
+            load_out.wait()
+            stores.append(copies.start(hid_buf.at[pl.ds(0, lead), :], hid_q_hbm))
+        out = dot(hid, w_out_buf[...])
+        if i == 0:
+            for j in range(steps):
+                part_buf[j, ROWS:, :] = out[:8]
+        for j in range(pair):
+            part_buf[i + j, :ROWS, :] = out[skip + j * ROWS : skip + (j + 1) * ROWS]
+            stores.append(copies.start(part_buf.at[i + j], part_hbm.at[i + j]))
+        rows = pl.ds(lead + i * ROWS, pair * ROWS)
+        stores.append(copies.start(hid_buf.at[rows, :], hid_hbm.at[pl.ds(i * ROWS, pair * ROWS), :]))
     for store in stores:
         store.wait()
 
@@ -115,13 +127,11 @@
         ],
         scratch_shapes=[
             pltpu.VMEM((few, feats), BF16),
-            pltpu.VMEM((items, feats), BF16),
+            pltpu.VMEM((16 + items, feats), BF16),
             pltpu.VMEM((feats, units), BF16),
             pltpu.VMEM((units, width), BF16),
             pltpu.VMEM((steps, ROWS + 8, width), F32),
-            pltpu.VMEM((items, units), BF16),
-            pltpu.VMEM((16, units), BF16),
-            pltpu.VMEM((16, units), F32),
+            pltpu.VMEM((16 + items, units), BF16),
             pltpu.SemaphoreType.DMA((4 + 3 * steps,)),
         ],
         compiler_params=pltpu.CompilerParams(vmem_limit_bytes=VMEM),
@@ -134,7 +144,7 @@
 
 def score_kernel(
     few, slots, scale, info_ref, own_ref, by1_ref, by2_ref, by3_ref, msg_ref,
-    weight_hbm, layer_hbm, all_q_hbm, pay_hbm, weight_ref, layer_ref, all_q_ref, pay_ref, code, digit, total_u, sems,
+    weight_hbm, layer_hbm, all_q_hbm, pay_hbm, weight_ref, layer_ref, all_q_ref, pay_ref, code, digit, total_u, emb, sems,
 ):
     copies = Copies(sems)
     lines = msg_ref.shape[0]
@@ -172,6 +182,7 @@
     total_d = jnp.zeros((1, queries), F32)
     for block, chunk in enumerate(blocks_of(layer_ref.shape[0])):
         e16 = jnp.tanh(layer_ref[chunk, :].astype(F32)).astype(BF16)
+        emb[chunk, :] = e16
         grown = jnp.exp(scale * dot_lanes(e16, all_q))
         ids = row_ids(block, (ROWS, group))
         digits = jnp.zeros((ROWS, group), F32)
@@ -184,9 +195,8 @@
         weight_ref[chunk, :] = weight16
         stores.append(copies.start(weight_ref.at[chunk, :], weight_hbm.at[chunk, :]))
         total_d = total_d + jnp.sum(weight, 0, keepdims=True)
-        part = dot_rows(weight16, e16)
-        total_u[...] = part if block == 0 else total_u[...] + part
-
+
+    total_u[...] = dot_rows(weight_ref[...], emb[...])
     d = jnp.concatenate([total_d[:, i * width : (i + 1) * width] for i in range(queries // width)], 0)
     high = d.astype(BF16).astype(F32)
     tail = jnp.concatenate([high, d - high, jnp.zeros((8 - 2 * d.shape[0], width), F32)], 0)
@@ -221,6 +231,7 @@
             pltpu.VMEM((slots + 8, queries // few), F32),
             pltpu.VMEM((slots + 8, queries // few), F32),
             pltpu.VMEM((queries, width), F32),
+            pltpu.VMEM((items, width), BF16),
             pltpu.SemaphoreType.DMA((3 + items // ROWS,)),
         ],
         compiler_params=pltpu.CompilerParams(vmem_limit_bytes=VMEM),
@@ -230,53 +241,55 @@
 def backward_kernel(
     few, scale, info_ref, all_q_hbm, weight_hbm, layer_hbm, hid_hbm, sums_ref, w_out_ref, x_ref,
     emb_q_ref, hid_q_ref, q_ref, mine_ref, other_ref,
-    all_q_ref, weight_ref, layer_ref, hid_ref, tanh_grad, pre_grad, summed, sems,
+    all_q_ref, weight_ref, layer_ref, hid_ref, item_grad, tanh_grad, pre_grad, summed, sems,
 ):
+    items, width = layer_ref.shape
+    feats = x_ref.shape[1]
+    halves = [pl.ds(i * 2 * ROWS, 2 * ROWS) for i in range(items // (2 * ROWS))]
     copies = Copies(sems)
     load_q = copies.start(all_q_hbm, all_q_ref)
-    loads = []
-    for chunk in blocks_of(layer_ref.shape[0]):
-        pairs = ((weight_hbm, weight_ref), (layer_hbm, layer_ref), (hid_hbm, hid_ref))
-        loads.append([copies.start(source.at[chunk, :], target.at[chunk, :]) for source, target in pairs])
+    load_weight = [copies.start(weight_hbm.at[half, :], weight_ref.at[half, :]) for half in halves]
+    load_layer = copies.start(layer_hbm, layer_ref)
+    load_hid = copies.start(hid_hbm, hid_ref)
+
     queries = all_q_ref.shape[0]
-    items, width = layer_ref.shape
-    feats = x_ref.shape[1]
     group = queries // few
     sums = jnp.sum(sums_ref[...].astype(F32), 0)
     d = sums[few : few + 2] + sums[few + 2 : few + 4]
     d = jnp.concatenate([d[0:1], d[1:2]], 1)
     factor = jnp.broadcast_to(scale / d, (8, queries)).T[:, :1]
+    line = lax.broadcasted_iota(jnp.int32, (8, queries), 0)
+    own_lane = lax.broadcasted_iota(jnp.int32, (8, queries), 1)
+    own_d = jnp.sum(jnp.where(own_lane == line * group + info_ref[few], d, 0.0), 1, keepdims=True)
     emb_q = emb_q_ref[...]
-    own_q = jnp.concatenate([emb_q, jnp.zeros_like(emb_q)], 0).astype(BF16)
+    own_q = emb_q.astype(BF16).astype(F32)
     load_q.wait()
-    scaled = all_q_ref[...].astype(F32) * factor
-    high = scaled.astype(BF16)
-    low = (scaled - high.astype(F32)).astype(BF16)
-
-    pos_emb = jnp.zeros((16, width), F32)
-    for block, chunk in enumerate(blocks_of(items)):
-        for copy in loads[block]:
-            copy.wait()
+    scaled = (all_q_ref[...].astype(F32) * factor).astype(BF16)
+    for half, load in zip(halves, load_weight):
+        load.wait()
+        item_grad[half, :] = dot(weight_ref[half, :], scaled)
+    load_layer.wait()
+    named = []
+    for i in range(few):
+        place = info_ref[i]
+        item_grad[pl.ds(place, 1), :] = item_grad[pl.ds(place, 1), :] - scale * own_q[i : i + 1]
+        base = (place // 16) * 16
+        near = layer_ref[pl.ds(pl.multiple_of(base, 16), 16), :].astype(F32)
+        at = lax.broadcasted_iota(jnp.int32, near.shape, 0) == place - base
+        named.append(jnp.sum(jnp.where(at, near, 0.0), 0, keepdims=True))
+    named.append(jnp.zeros((8 - few, width), F32))
+    pos_emb = jnp.tanh(jnp.concatenate(named, 0)).astype(BF16).astype(F32)
+
+    load_hid.wait()
+    for chunk in halves:
         e = jnp.tanh(layer_ref[chunk, :].astype(F32))
-        place = lax.broadcasted_iota(jnp.int32, (16, ROWS), 1) + block * ROWS
-        line = lax.broadcasted_iota(jnp.int32, (16, ROWS), 0)
-        picked = jnp.zeros((16, ROWS), F32)
-        for i in range(few):
-            picked = jnp.where((line == i) & (place == info_ref[i]), 1.0, picked)
-        picked = picked.astype(BF16)
-        pos_emb = pos_emb + dot(picked, e.astype(BF16))
-        weight = weight_ref[chunk, :]
-        item_grad = dot(weight, high) + dot(weight, low) - scale * dot_rows(picked, own_q)
-        grad = (item_grad * (1.0 - e * e)).astype(BF16)
+        grad = (item_grad[chunk, :] * (1.0 - e * e)).astype(BF16)
         tanh_grad[chunk, :] = grad
         hid_grad = dot_lanes(grad, w_out_ref[...])
         pre_grad[chunk, :] = jnp.where(hid_ref[chunk, :] > 0, hid_grad, 0.0).astype(BF16)
 
-    line = lax.broadcasted_iota(jnp.int32, (8, queries), 0)
-    own_lane = lax.broadcasted_iota(jnp.int32, (8, queries), 1)
-    own_d = jnp.sum(jnp.where(own_lane == line * group + info_ref[few], d, 0.0), 1, keepdims=True)
     live = lax.broadcasted_iota(jnp.int32, (8, width), 0) < few
-    grad = scale * (sums / own_d - pos_emb[:8]) * (1.0 - emb_q * emb_q)
+    grad = scale * (sums / own_d - pos_emb) * (1.0 - emb_q * emb_q)
     grad = jnp.where(live, grad, 0.0)
     grad_q = jnp.concatenate([grad, jnp.zeros_like(grad)], 0).astype(BF16)
     hid_q = hid_q_ref[...]
@@ -309,10 +322,11 @@
         out_shape=[jax.ShapeDtypeStruct(((feats + units) // 2, width), BF16)] * 2,
         scratch_shapes=[
             *[pltpu.VMEM(a.shape, a.dtype) for a in far],
+            pltpu.VMEM((items, width), F32),
             pltpu.VMEM((items, width), BF16),
             pltpu.VMEM((items, units), BF16),
             pltpu.VMEM((feats + units, width), BF16),
-            pltpu.SemaphoreType.DMA((1 + 3 * (items // ROWS),)),
+            pltpu.SemaphoreType.DMA((3 + items // (2 * ROWS),)),
         ],
         compiler_params=pltpu.CompilerParams(vmem_limit_bytes=VMEM),
     )(info, *pinned(*far), *near)
@@ -391,7 +405,7 @@
 
     named = jnp.concatenate([negatives.reshape(-1), positives])
     rows = jnp.take(owner_map, named, axis=0)
-    pos_local = rows[few * negative_count :] - own_index * item_count
+    pos_local = jnp.clip(rows[few * negative_count :] - own_index * item_count, 0, item_count - 1)
     places = [lax.axis_index(YCZ), lax.axis_index("x"), lax.axis_index("c")]
     info = jnp.concatenate([pos_local, jnp.stack(places)])
     codes = request_codes(

time: 158 us -> 157 us (level)
  Pallas kernels: 15.1 us -> 13.3 us
where the time goes in v6:
time: 157 us; the launch traced here: 156 us
  blocking collectives  59.7 us (38%)
  starting transfers between devices  52 us (33%)
  waiting for transfers between devices  22.7 us (14%)
  Pallas kernels  13.3 us (8%)
  local copies, waits for them, and re-layouts  4.08 us (3%)
  other arithmetic  2.15 us (1%)
    all_to_all x4, blocking collectives, exchange(): return lax.all_to_all(blocks, axes, split_axis=0, concat_axis=0, tiled=True)  59.7 us
    all_to_all x3, starting transfers between devices, exchange(): return lax.all_to_all(blocks, axes, split_axis=0, concat_axis=0, tiled=True)  34.6 us
    all_to_all x3, waiting for transfers between devices, exchange(): return lax.all_to_all(blocks, axes, split_axis=0, concat_axis=0, tiled=True)  20.2 us
    ppermute x3, starting transfers between devices, local(): lax.ppermute(own, 'x', [(i, (i + far) % x_count) for i in range(x_count)])  8.42 us
    ppermute x1, starting transfers between devices, local(): return tuple(assemble(grads, lax.ppermute(grads, 'c', swap), w_in.shape[0]))  6.24 us
    pallas_call x1, Pallas kernels, score(): pl.pallas_call(functools.partial(score_kernel, few, slots, scale), in_spe...  4.21 us
    pallas_call x1, Pallas kernels, forward(): pl.pallas_call(forward_kernel, in_specs=[FAR] * 4, out_specs=[FAR] * 3, o...  4.2 us
    pallas_call x1, Pallas kernels, backward(): pl.pallas_call(functools.partial(backward_kernel, few, scale), in_specs=[...  4.07 us
  transfers between devices with their start and end apart: 8, of which 5 were waited for; matrix products, arithmetic and copies ran while one was open for 3% of the time, Pallas kernels for 0%

profile of v6, /device:TPU:1, one launch (start us, length us, event | category | flops | bytes accessed | tf_op | source)
XLA Modules:
  0.0 156.0 jit_solution(2534949666239405064)
XLA Ops:
  0.6 4.2 %shard_map.86 = (f32[4,264,256]{2,1,0:T(8,128)}, bf16[1024,256]{1,0:T(8,128)(2,1)}, bf16[16,256]{1,0:T(8,128)(2,1)}) custom-call(bf16[4,1024]{1,0:T(4,128)(2,1)} %q_hbm.1, bf16[1024,1024]{1,0:T(8,128)(2,1)} %x_ref.1, bf16[1024,256]{1,0:T(8,128)(2,1)} %w_in_hbm.1, bf16[256,256]{1,0:T(8,128)(2,1)} %w_out_ref.1), custom_call_target="tpu_custom_call" | custom-call | tf_op jit(solution)/shard_map/pallas_call | solution.py:119
  4.9 4.9 %all-to-all-start = ((f32[4,264,256]{2,1,0:T(8,128)}), f32[4,264,256]{2,1,0:T(8,128)S(1)}, u32[]{:S(2)}, u32[]{:S(2)}) async-start(f32[4,264,256]{2,1,0:T(8,128)} %get-tuple-element.11), calls=%async_computation | async-start | bytes 2162688 | tf_op jit(solution)/shard_map/all_to_all | solution.py:20
  9.8 3.6 %gather_fusion = s32[516]{0:T(1024)S(1)} fusion(s32[131072]{0:T(1024)S(1)} %copy-done, s32[1024]{0:T(1024)S(1)} %pad_clamp_fusion), kind=kCustom, calls=%fused_computation | custom fusion | bytes 6192 | tf_op jit(solution)/shard_map/jit(_take)/gather | solution.py:407
  13.4 0.3 fusion
  13.7 0.7 fusion.1
  14.4 0.1 copy.14
  14.6 5.1 %all-to-all-done = f32[4,264,256]{2,1,0:T(8,128)S(1)} async-done(((f32[4,264,256]{2,1,0:T(8,128)}), f32[4,264,256]{2,1,0:T(8,128)S(1)}, u32[]{:S(2)}, u32[]{:S(2)}) %all-to-all-start) | async-done | bytes 1081376 | tf_op jit(solution)/shard_map/all_to_all | solution.py:20
  19.7 0.1 broadcast_in_dim.72
  19.8 1.0 fusion.2
  20.9 23.4 %all-to-all-start.1 = ((bf16[128,2,640]{2,1,0:T(2,128)(2,1)}), bf16[128,2,640]{2,1,0:T(2,128)(2,1)S(1)}, u32[]{:S(2)}, u32[]{:S(2)}) async-start(bf16[128,2,640]{2,1,0:T(2,128)(2,1)} %fusion.2), calls=%async_computation.1 | async-start | bytes 655360 | tf_op jit(solution)/shard_map/all_to_all | solution.py:20
  44.3 0.1 slice_reduce_fusion.own_ref
  44.4 2.2 %collective-permute-start = (bf16[256,256]{1,0:T(8,128)(2,1)S(1)}, bf16[256,256]{1,0:T(8,128)(2,1)S(1)}, u32[]{:S(2)}, u32[]{:S(2)}) collective-permute-start(bf16[256,256]{1,0:T(8,128)(2,1)S(1)} %slice_reduce_fusion.own_ref), channel_id=1, source_target_pairs={{0,1},{1,2},{2,3},{3,0},{4,5},{5,6},{6,7},{7,4},{8,9},{9,10},{10,1... | collective-permute-start | bytes 393224 | tf_op jit(solution)/shard_map/ppermute | solution.py:428
  46.6 3.7 %collective-permute-start.1 = (bf16[256,256]{1,0:T(8,128)(2,1)S(1)}, bf16[256,256]{1,0:T(8,128)(2,1)S(1)}, u32[]{:S(2)}, u32[]{:S(2)}) collective-permute-start(bf16[256,256]{1,0:T(8,128)(2,1)S(1)} %slice_reduce_fusion.own_ref), channel_id=1, source_target_pairs={{0,2},{1,3},{2,0},{3,1},{4,6},{5,7},{6,4},{7,5},{8,10},{9,11},{10,... | collective-permute-start | bytes 393224 | tf_op jit(solution)/shard_map/ppermute | solution.py:428
  50.3 2.5 %collective-permute-start.2 = (bf16[256,256]{1,0:T(8,128)(2,1)S(1)}, bf16[256,256]{1,0:T(8,128)(2,1)}, u32[]{:S(2)}, u32[]{:S(2)}) collective-permute-start(bf16[256,256]{1,0:T(8,128)(2,1)S(1)} %slice_reduce_fusion.own_ref), channel_id=1, source_target_pairs={{0,3},{1,0},{2,1},{3,2},{4,7},{5,4},{6,5},{7,6},{8,11},{9,8},{10,9... | collective-permute-start | bytes 393224 | tf_op jit(solution)/shard_map/ppermute | solution.py:428
  52.8 0.1 pad_add_fusion.info_ref
  52.9 8.1 %all-to-all-done.1 = bf16[128,2,640]{2,1,0:T(2,128)(2,1)S(1)} async-done(((bf16[128,2,640]{2,1,0:T(2,128)(2,1)}), bf16[128,2,640]{2,1,0:T(2,128)(2,1)S(1)}, u32[]{:S(2)}, u32[]{:S(2)}) %all-to-all-start.1) | async-done | bytes 327712 | tf_op jit(solution)/shard_map/all_to_all | solution.py:20
  61.0 0.1 reshape.150.msg_ref
  61.2 4.2 %shard_map.87 = (bf16[1024,512]{1,0:T(8,128)(2,1)}, bf16[1024,256]{1,0:T(8,128)(2,1)}, bf16[512,256]{1,0:T(8,128)(2,1)}, bf16[16,40,256]{2,1,0:T(8,128)(2,1)}) custom-call(s32[7]{0:T(128)S(1)} %pad_add_fusion.info_ref, bf16[256,256]{1,0:T(8,128)(2,1)S(1)} %slice_reduce_fusion.own_ref, bf16[256,256]{1,0:T(8,128)(2,1)S(1)} %collective-permute-done.by1_ref, ...), custom_call_target="tpu_custom_call" | custom-call | tf_op jit(solution)/shard_map/pallas_call | solution.py:216
  65.4 17.7 %all_to_all.35 = bf16[16,40,256]{2,1,0:T(8,128)(2,1)S(1)} all-to-all(bf16[16,40,256]{2,1,0:T(8,128)(2,1)} %get-tuple-element.16), channel_id=1, replica_groups=mesh['z'=8,'y'=8,'c'=2,'x'=4] {'y','c'}, dimensions={0} | all-to-all | bytes 655360 | tf_op jit(solution)/shard_map/all_to_all | solution.py:20
  83.3 0.6 pad_maximum_fusion
  83.9 6.4 %all-to-all-start.3 = ((bf16[8,8,256]{2,1,0:T(8,128)(2,1)}), bf16[8,8,256]{2,1,0:T(8,128)(2,1)S(1)}, u32[]{:S(2)}, u32[]{:S(2)}) async-start(bf16[8,8,256]{2,1,0:T(8,128)(2,1)} %pad_maximum_fusion), calls=%async_computation.3 | async-start | bytes 65536 | tf_op jit(solution)/shard_map/all_to_all | solution.py:20
  90.3 7.0 %all-to-all-done.3.sums_ref = bf16[8,8,256]{2,1,0:T(8,128)(2,1)S(1)} async-done(((bf16[8,8,256]{2,1,0:T(8,128)(2,1)}), bf16[8,8,256]{2,1,0:T(8,128)(2,1)S(1)}, u32[]{:S(2)}, u32[]{:S(2)}) %all-to-all-start.3) | async-done | bytes 32800 | tf_op jit(solution)/shard_map/all_to_all | solution.py:20
  97.4 4.1 %shard_map.88 = (bf16[640,256]{1,0:T(8,128)(2,1)S(1)}, bf16[640,256]{1,0:T(8,128)(2,1)S(1)}) custom-call(s32[7]{0:T(128)S(1)} %pad_add_fusion.info_ref, bf16[512,256]{1,0:T(8,128)(2,1)} %get-tuple-element.12.all_q_hbm, bf16[1024,512]{1,0:T(8,128)(2,1)} %get-tuple-element.13.weight_hbm, bf16[1024,256]{1,0:T(8,128)(2,1)} %get-tuple-element.14.layer_hbm, ...), custom_call_target="tpu_custom_call" | custom-call | tf_op jit(solution)/shard_map/pallas_call | solution.py:318
  101.4 2.7 %collective-permute-start.3 = (bf16[640,256]{1,0:T(8,128)(2,1)S(1)}, bf16[640,256]{1,0:T(8,128)(2,1)S(1)}, u32[]{:S(2)}, u32[]{:S(2)}) collective-permute-start(bf16[640,256]{1,0:T(8,128)(2,1)S(1)} %get-tuple-element.19), channel_id=1, source_target_pairs={{0,4},{4,0},{1,5},{5,1},{2,6},{6,2},{3,7},{7,3},{8,12},{12,8},{9,1... | collective-permute-start | bytes 983048 | tf_op jit(solution)/shard_map/ppermute | solution.py:452
  104.2 1.2 collective-permute-done.3
  105.4 0.1 add_convert_fusion
  105.5 15.6 %all_to_all.36 = bf16[8,80,256]{2,1,0:T(8,128)(2,1)S(1)} all-to-all(bf16[8,80,256]{2,1,0:T(8,128)(2,1)S(1)} %bitcast.17), channel_id=1, replica_groups=mesh['z'=8,'y'=8,'c'=2,'x'=4] {'y'}, dimensions={0} | all-to-all | bytes 655360 | tf_op jit(solution)/shard_map/all_to_all | solution.py:20
  121.2 13.4 %all_to_all.37 = bf16[8,80,256]{2,1,0:T(8,128)(2,1)S(1)} all-to-all(bf16[8,80,256]{2,1,0:T(8,128)(2,1)S(1)} %broadcast_in_dim.80), channel_id=1, replica_groups=mesh['z'=8,'y'=8,'c'=2,'x'=4] {'z'}, dimensions={0} | all-to-all | bytes 655360 | tf_op jit(solution)/shard_map/all_to_all | solution.py:20
  134.7 12.9 %all_to_all.38 = bf16[8,80,256]{2,1,0:T(8,128)(2,1)S(1)} all-to-all(bf16[8,80,256]{2,1,0:T(8,128)(2,1)S(1)} %broadcast_in_dim.81), channel_id=1, replica_groups=mesh['z'=8,'y'=8,'c'=2,'x'=4] {'y'}, dimensions={0} | all-to-all | bytes 655360 | tf_op jit(solution)/shard_map/all_to_all | solution.py:20
  147.6 6.2 %collective-permute-start.4 = (bf16[640,256]{1,0:T(8,128)(2,1)S(1)}, bf16[640,256]{1,0:T(8,128)(2,1)S(1)}, u32[]{:S(2)}, u32[]{:S(2)}) collective-permute-start(bf16[640,256]{1,0:T(8,128)(2,1)S(1)} %bitcast.15), channel_id=1, source_target_pairs={{0,4},{4,0},{1,5},{5,1},{2,6},{6,2},{3,7},{7,3},{8,12},{12,8},{9,1... | collective-permute-start | bytes 983048 | tf_op jit(solution)/shard_map/ppermute | solution.py:456
  153.9 1.2 collective-permute-done.4.other_ref
  155.1 0.9 shard_map.89
  (38 shorter events, 0.4 us)
Async XLA Ops:
  0.6 9.1 %copy-start = (s32[131072]{0:T(1024)S(1)}, s32[131072]{0:T(1024)}, u32[]{:S(2)}) copy-start(s32[131072]{0:T(1024)} %param.13) | copy-start | bytes 1572868
  4.8 4.9 %copy-start.5 = (s32[4,128]{1,0:T(4,128)S(1)}, s32[4,128]{1,0:T(4,128)}, u32[]{:S(2)}) copy-start(s32[4,128]{1,0:T(4,128)} %param.11) | copy-start | bytes 6148
  4.9 4.9 %copy-start.6 = (s32[4]{0:T(128)S(1)}, s32[4]{0:T(128)}, u32[]{:S(2)}) copy-start(s32[4]{0:T(128)} %param.12) | copy-start | bytes 52
  4.9 14.8 %all-to-all-start = ((f32[4,264,256]{2,1,0:T(8,128)}), f32[4,264,256]{2,1,0:T(8,128)S(1)}, u32[]{:S(2)}, u32[]{:S(2)}) async-start(f32[4,264,256]{2,1,0:T(8,128)} %get-tuple-element.11), calls=%async_computation | async-start | bytes 2162688 | tf_op jit(solution)/shard_map/all_to_all | solution.py:20
  20.9 40.1 %all-to-all-start.1 = ((bf16[128,2,640]{2,1,0:T(2,128)(2,1)}), bf16[128,2,640]{2,1,0:T(2,128)(2,1)S(1)}, u32[]{:S(2)}, u32[]{:S(2)}) async-start(bf16[128,2,640]{2,1,0:T(2,128)(2,1)} %fusion.2), calls=%async_computation.1 | async-start | bytes 655360 | tf_op jit(solution)/shard_map/all_to_all | solution.py:20
  44.4 16.8 %collective-permute-start = (bf16[256,256]{1,0:T(8,128)(2,1)S(1)}, bf16[256,256]{1,0:T(8,128)(2,1)S(1)}, u32[]{:S(2)}, u32[]{:S(2)}) collective-permute-start(bf16[256,256]{1,0:T(8,128)(2,1)S(1)} %slice_reduce_fusion.own_ref), channel_id=1, source_target_pairs={{0,1},{1,2},{2,3},{3,0},{4,5},{5,6},{6,7},{7,4},{8,9},{9,10},{10,1... | collective-permute-start | bytes 393224 | tf_op jit(solution)/shard_map/ppermute | solution.py:428
  46.6 14.6 %collective-permute-start.1 = (bf16[256,256]{1,0:T(8,128)(2,1)S(1)}, bf16[256,256]{1,0:T(8,128)(2,1)S(1)}, u32[]{:S(2)}, u32[]{:S(2)}) collective-permute-start(bf16[256,256]{1,0:T(8,128)(2,1)S(1)} %slice_reduce_fusion.own_ref), channel_id=1, source_target_pairs={{0,2},{1,3},{2,0},{3,1},{4,6},{5,7},{6,4},{7,5},{8,10},{9,11},{10,... | collective-permute-start | bytes 393224 | tf_op jit(solution)/shard_map/ppermute | solution.py:428
  50.3 10.9 %collective-permute-start.2 = (bf16[256,256]{1,0:T(8,128)(2,1)S(1)}, bf16[256,256]{1,0:T(8,128)(2,1)}, u32[]{:S(2)}, u32[]{:S(2)}) collective-permute-start(bf16[256,256]{1,0:T(8,128)(2,1)S(1)} %slice_reduce_fusion.own_ref), channel_id=1, source_target_pairs={{0,3},{1,0},{2,1},{3,2},{4,7},{5,4},{6,5},{7,6},{8,11},{9,8},{10,9... | collective-permute-start | bytes 393224 | tf_op jit(solution)/shard_map/ppermute | solution.py:428
  61.0 29.3 %copy-start.4 = (bf16[4,1024]{1,0:T(4,128)(2,1)S(1)}, bf16[4,1024]{1,0:T(4,128)(2,1)}, u32[]{:S(2)}) copy-start(bf16[4,1024]{1,0:T(4,128)(2,1)} %q_hbm.1) | copy-start | bytes 24580
  61.0 36.4 %copy-start.2 = (bf16[256,256]{1,0:T(8,128)(2,1)S(1)}, bf16[256,256]{1,0:T(8,128)(2,1)}, u32[]{:S(2)}) copy-start(bf16[256,256]{1,0:T(8,128)(2,1)} %w_out_ref.1) | copy-start | bytes 393220
  61.1 36.2 %copy-start.1 = (bf16[1024,1024]{1,0:T(8,128)(2,1)S(1)}, bf16[1024,1024]{1,0:T(8,128)(2,1)}, u32[]{:S(2)}) copy-start(bf16[1024,1024]{1,0:T(8,128)(2,1)} %x_ref.1) | copy-start | bytes 6291460
  61.1 36.2 %copy-start.3 = (bf16[16,256]{1,0:T(8,128)(2,1)S(1)}, bf16[16,256]{1,0:T(8,128)(2,1)}, u32[]{:S(2)}) copy-start(bf16[16,256]{1,0:T(8,128)(2,1)} %get-tuple-element.17.hid_q_ref) | copy-start | bytes 24580
  83.9 13.5 %all-to-all-start.3 = ((bf16[8,8,256]{2,1,0:T(8,128)(2,1)}), bf16[8,8,256]{2,1,0:T(8,128)(2,1)S(1)}, u32[]{:S(2)}, u32[]{:S(2)}) async-start(bf16[8,8,256]{2,1,0:T(8,128)(2,1)} %pad_maximum_fusion), calls=%async_computation.3 | async-start | bytes 65536 | tf_op jit(solution)/shard_map/all_to_all | solution.py:20
  101.4 4.0 %collective-permute-start.3 = (bf16[640,256]{1,0:T(8,128)(2,1)S(1)}, bf16[640,256]{1,0:T(8,128)(2,1)S(1)}, u32[]{:S(2)}, u32[]{:S(2)}) collective-permute-start(bf16[640,256]{1,0:T(8,128)(2,1)S(1)} %get-tuple-element.19), channel_id=1, source_target_pairs={{0,4},{4,0},{1,5},{5,1},{2,6},{6,2},{3,7},{7,3},{8,12},{12,8},{9,1... | collective-permute-start | bytes 983048 | tf_op jit(solution)/shard_map/ppermute | solution.py:452
  147.6 7.5 %collective-permute-start.4 = (bf16[640,256]{1,0:T(8,128)(2,1)S(1)}, bf16[640,256]{1,0:T(8,128)(2,1)S(1)}, u32[]{:S(2)}, u32[]{:S(2)}) collective-permute-start(bf16[640,256]{1,0:T(8,128)(2,1)S(1)} %bitcast.15), channel_id=1, source_target_pairs={{0,4},{4,0},{1,5},{5,1},{2,6},{6,2},{3,7},{7,3},{8,12},{12,8},{9,1... | collective-permute-start | bytes 983048 | tf_op jit(solution)/shard_map/ppermute | solution.py:456

commit v7 on v6

--- a/solution.py
+++ b/solution.py
@@ -144,7 +144,7 @@
 
 def score_kernel(
     few, slots, scale, info_ref, own_ref, by1_ref, by2_ref, by3_ref, msg_ref,
-    weight_hbm, layer_hbm, all_q_hbm, pay_hbm, weight_ref, layer_ref, all_q_ref, pay_ref, code, digit, total_u, emb, sems,
+    weight_hbm, layer_hbm, all_q_hbm, pay_ref, weight_ref, layer_ref, all_q_ref, code, digit, total_u, emb, sems,
 ):
     copies = Copies(sems)
     lines = msg_ref.shape[0]
@@ -203,7 +203,6 @@
     for y in range(pay_ref.shape[0]):
         mine = [total_u[i * group + y * 8 : i * group + y * 8 + 8, :] for i in range(few)]
         pay_ref[y] = jnp.concatenate([*mine, tail], 0).astype(BF16)
-    stores.append(copies.start(pay_ref, pay_hbm))
     for store in stores:
         store.wait()
 
@@ -216,18 +215,17 @@
     return pl.pallas_call(
         functools.partial(score_kernel, few, slots, scale),
         in_specs=[pl.BlockSpec(memory_space=pltpu.SMEM)] + [NEAR] * (len(layers) + 1),
-        out_specs=[FAR] * 4,
+        out_specs=[FAR] * 3 + [NEAR],
         out_shape=[
             pltpu.HBM((items, queries), BF16),
             pltpu.HBM((items, width), BF16),
             pltpu.HBM((queries, width), BF16),
-            pltpu.HBM(pay, BF16),
+            jax.ShapeDtypeStruct(pay, BF16),
         ],
         scratch_shapes=[
             pltpu.VMEM((items, queries), BF16),
             pltpu.VMEM((items, width), BF16),
             pltpu.VMEM((queries, width), BF16),
-            pltpu.VMEM(pay, BF16),
             pltpu.VMEM((slots + 8, queries // few), F32),
             pltpu.VMEM((slots + 8, queries // few), F32),
             pltpu.VMEM((queries, width), F32),
@@ -239,9 +237,9 @@
 
 
 def backward_kernel(
-    few, scale, info_ref, all_q_hbm, weight_hbm, layer_hbm, hid_hbm, sums_ref, w_out_ref, x_ref,
+    few, scale, info_ref, all_q_hbm, weight_hbm, layer_hbm, hid_hbm, x_hbm, sums_ref, w_out_ref,
     emb_q_ref, hid_q_ref, q_ref, mine_ref, other_ref,
-    all_q_ref, weight_ref, layer_ref, hid_ref, item_grad, tanh_grad, pre_grad, summed, sems,
+    all_q_ref, weight_ref, layer_ref, hid_ref, x_ref, item_grad, tanh_grad, pre_grad, summed, sems,
 ):
     items, width = layer_ref.shape
     feats = x_ref.shape[1]
@@ -251,6 +249,7 @@
     load_weight = [copies.start(weight_hbm.at[half, :], weight_ref.at[half, :]) for half in halves]
     load_layer = copies.start(layer_hbm, layer_ref)
     load_hid = copies.start(hid_hbm, hid_ref)
+    load_x = copies.start(x_hbm, x_ref)
 
     queries = all_q_ref.shape[0]
     group = queries // few
@@ -294,6 +293,7 @@
     grad_q = jnp.concatenate([grad, jnp.zeros_like(grad)], 0).astype(BF16)
     hid_q = hid_q_ref[...]
     pre_grad_q = jnp.where(hid_q > 0, dot_lanes(grad_q, w_out_ref[...]), 0.0).astype(BF16)
+    load_x.wait()
     in_total = dot_rows(pre_grad[...], x_ref[...]) + dot_rows(pre_grad_q, q_ref[...])
     summed[:feats, :] = in_total.astype(BF16).T
     summed[feats:, :] = (dot_rows(hid_ref[...], tanh_grad[...]) + dot_rows(hid_q, grad_q)).astype(BF16)
@@ -314,7 +314,7 @@
 def backward(info, far, near, few, scale):
     items, width = far[2].shape
     units = far[3].shape[1]
-    feats = near[2].shape[1]
+    feats = far[4].shape[1]
     return pl.pallas_call(
         functools.partial(backward_kernel, few, scale),
         in_specs=[pl.BlockSpec(memory_space=pltpu.SMEM)] + [FAR] * len(far) + [NEAR] * len(near),
@@ -326,7 +326,7 @@
             pltpu.VMEM((items, width), BF16),
             pltpu.VMEM((items, units), BF16),
             pltpu.VMEM((feats + units, width), BF16),
-            pltpu.SemaphoreType.DMA((3 + items // (2 * ROWS),)),
+            pltpu.SemaphoreType.DMA((4 + items // (2 * ROWS),)),
         ],
         compiler_params=pltpu.CompilerParams(vmem_limit_bytes=VMEM),
     )(info, *pinned(*far), *near)
@@ -445,8 +445,8 @@
         "z",
     )
     feats_q = jnp.pad(query_feats, ((0, 16 - few), (0, 0)))
-    near = (sums, w_out, item_feats, own_q, hidden_q, feats_q)
-    mine, other = backward(info, (all_q, weight, layer_out, hidden), near, few, scale)
+    near = (sums, w_out, own_q, hidden_q, feats_q)
+    mine, other = backward(info, (all_q, weight, layer_out, hidden, item_feats), near, few, scale)
     y_count = lax.axis_size("y")
     swap = [(0, 1), (1, 0)]
     grads = (mine.astype(F32) + lax.ppermute(other, "c", swap).astype(F32)).astype(BF16)

time: 157 us -> 156 us (level)
  no operation moved by 1% of the time
where the time goes in v7:
time: 156 us; the launch traced here: 155 us
  blocking collectives  59.5 us (38%)
  starting transfers between devices  52 us (33%)
  waiting for transfers between devices  22.7 us (15%)
  Pallas kernels  12.6 us (8%)
  local copies, waits for them, and re-layouts  4.08 us (3%)
  other arithmetic  2.15 us (1%)
    all_to_all x4, blocking collectives, exchange(): return lax.all_to_all(blocks, axes, split_axis=0, concat_axis=0, tiled=True)  59.5 us
    all_to_all x3, starting transfers between devices, exchange(): return lax.all_to_all(blocks, axes, split_axis=0, concat_axis=0, tiled=True)  34.6 us
    all_to_all x3, waiting for transfers between devices, exchange(): return lax.all_to_all(blocks, axes, split_axis=0, concat_axis=0, tiled=True)  20.2 us
    ppermute x3, starting transfers between devices, local(): lax.ppermute(own, 'x', [(i, (i + far) % x_count) for i in range(x_count)])  8.41 us
    ppermute x1, starting transfers between devices, local(): return tuple(assemble(grads, lax.ppermute(grads, 'c', swap), w_in.shape[0]))  6.24 us
    pallas_call x1, Pallas kernels, forward(): pl.pallas_call(forward_kernel, in_specs=[FAR] * 4, out_specs=[FAR] * 3, o...  4.2 us
    pallas_call x1, Pallas kernels, backward(): pl.pallas_call(functools.partial(backward_kernel, few, scale), in_specs=[...  4.15 us
    gather x1, local copies, waits for them, and re-layouts, local(): rows = jnp.take(owner_map, named, axis=0)  3.56 us
  transfers between devices with their start and end apart: 8, of which 5 were waited for; matrix products, arithmetic and copies ran while one was open for 3% of the time, Pallas kernels for 0%

profile of v7, /device:TPU:1, one launch (start us, length us, event | category | flops | bytes accessed | tf_op | source)
XLA Modules:
  0.0 155.0 jit_solution(16065105871382686235)
XLA Ops:
  0.6 4.2 %shard_map.86 = (f32[4,264,256]{2,1,0:T(8,128)}, bf16[1024,256]{1,0:T(8,128)(2,1)}, bf16[16,256]{1,0:T(8,128)(2,1)}) custom-call(bf16[4,1024]{1,0:T(4,128)(2,1)} %q_hbm.1, bf16[1024,1024]{1,0:T(8,128)(2,1)} %x_hbm.3, bf16[1024,256]{1,0:T(8,128)(2,1)} %w_in_hbm.1, bf16[256,256]{1,0:T(8,128)(2,1)} %w_out_ref.1), custom_call_target="tpu_custom_call" | custom-call | tf_op jit(solution)/shard_map/pallas_call | solution.py:119
  4.9 4.9 %all-to-all-start = ((f32[4,264,256]{2,1,0:T(8,128)}), f32[4,264,256]{2,1,0:T(8,128)S(1)}, u32[]{:S(2)}, u32[]{:S(2)}) async-start(f32[4,264,256]{2,1,0:T(8,128)} %get-tuple-element.11), calls=%async_computation | async-start | bytes 2162688 | tf_op jit(solution)/shard_map/all_to_all | solution.py:20
  9.8 3.6 %gather_fusion = s32[516]{0:T(1024)S(1)} fusion(s32[131072]{0:T(1024)S(1)} %copy-done, s32[1024]{0:T(1024)S(1)} %pad_clamp_fusion), kind=kCustom, calls=%fused_computation | custom fusion | bytes 6192 | tf_op jit(solution)/shard_map/jit(_take)/gather | solution.py:407
  13.4 0.3 fusion
  13.7 0.7 fusion.1
  14.4 0.1 copy.14
  14.6 5.1 %all-to-all-done = f32[4,264,256]{2,1,0:T(8,128)S(1)} async-done(((f32[4,264,256]{2,1,0:T(8,128)}), f32[4,264,256]{2,1,0:T(8,128)S(1)}, u32[]{:S(2)}, u32[]{:S(2)}) %all-to-all-start) | async-done | bytes 1081376 | tf_op jit(solution)/shard_map/all_to_all | solution.py:20
  19.7 0.1 broadcast_in_dim.72
  19.8 1.0 fusion.2
  20.9 23.4 %all-to-all-start.1 = ((bf16[128,2,640]{2,1,0:T(2,128)(2,1)}), bf16[128,2,640]{2,1,0:T(2,128)(2,1)S(1)}, u32[]{:S(2)}, u32[]{:S(2)}) async-start(bf16[128,2,640]{2,1,0:T(2,128)(2,1)} %fusion.2), calls=%async_computation.1 | async-start | bytes 655360 | tf_op jit(solution)/shard_map/all_to_all | solution.py:20
  44.3 0.1 slice_reduce_fusion.own_ref
  44.4 2.2 %collective-permute-start = (bf16[256,256]{1,0:T(8,128)(2,1)S(1)}, bf16[256,256]{1,0:T(8,128)(2,1)S(1)}, u32[]{:S(2)}, u32[]{:S(2)}) collective-permute-start(bf16[256,256]{1,0:T(8,128)(2,1)S(1)} %slice_reduce_fusion.own_ref), channel_id=1, source_target_pairs={{0,1},{1,2},{2,3},{3,0},{4,5},{5,6},{6,7},{7,4},{8,9},{9,10},{10,1... | collective-permute-start | bytes 393224 | tf_op jit(solution)/shard_map/ppermute | solution.py:428
  46.6 3.7 %collective-permute-start.1 = (bf16[256,256]{1,0:T(8,128)(2,1)S(1)}, bf16[256,256]{1,0:T(8,128)(2,1)S(1)}, u32[]{:S(2)}, u32[]{:S(2)}) collective-permute-start(bf16[256,256]{1,0:T(8,128)(2,1)S(1)} %slice_reduce_fusion.own_ref), channel_id=1, source_target_pairs={{0,2},{1,3},{2,0},{3,1},{4,6},{5,7},{6,4},{7,5},{8,10},{9,11},{10,... | collective-permute-start | bytes 393224 | tf_op jit(solution)/shard_map/ppermute | solution.py:428
  50.3 2.5 %collective-permute-start.2 = (bf16[256,256]{1,0:T(8,128)(2,1)S(1)}, bf16[256,256]{1,0:T(8,128)(2,1)S(1)}, u32[]{:S(2)}, u32[]{:S(2)}) collective-permute-start(bf16[256,256]{1,0:T(8,128)(2,1)S(1)} %slice_reduce_fusion.own_ref), channel_id=1, source_target_pairs={{0,3},{1,0},{2,1},{3,2},{4,7},{5,4},{6,5},{7,6},{8,11},{9,8},{10,9... | collective-permute-start | bytes 393224 | tf_op jit(solution)/shard_map/ppermute | solution.py:428
  52.8 0.1 pad_add_fusion.info_ref
  52.9 8.1 %all-to-all-done.1 = bf16[128,2,640]{2,1,0:T(2,128)(2,1)S(1)} async-done(((bf16[128,2,640]{2,1,0:T(2,128)(2,1)}), bf16[128,2,640]{2,1,0:T(2,128)(2,1)S(1)}, u32[]{:S(2)}, u32[]{:S(2)}) %all-to-all-start.1) | async-done | bytes 327712 | tf_op jit(solution)/shard_map/all_to_all | solution.py:20
  61.0 0.1 reshape.150.msg_ref
  61.2 3.4 %shard_map.87 = (bf16[1024,512]{1,0:T(8,128)(2,1)}, bf16[1024,256]{1,0:T(8,128)(2,1)}, bf16[512,256]{1,0:T(8,128)(2,1)}, bf16[16,40,256]{2,1,0:T(8,128)(2,1)S(1)}) custom-call(s32[7]{0:T(128)S(1)} %pad_add_fusion.info_ref, bf16[256,256]{1,0:T(8,128)(2,1)S(1)} %slice_reduce_fusion.own_ref, bf16[256,256]{1,0:T(8,128)(2,1)S(1)} %collective-permute-done.by1_ref, ...), custom_call_target="tpu_custom_call" | custom-call | tf_op jit(solution)/shard_map/pallas_call | solution.py:215
  64.6 17.5 %all_to_all.35 = bf16[16,40,256]{2,1,0:T(8,128)(2,1)S(1)} all-to-all(bf16[16,40,256]{2,1,0:T(8,128)(2,1)S(1)} %get-tuple-element.16), channel_id=1, replica_groups=mesh['z'=8,'y'=8,'c'=2,'x'=4] {'y','c'}, dimensions={0} | all-to-all | bytes 655360 | tf_op jit(solution)/shard_map/all_to_all | solution.py:20
  82.2 0.6 pad_maximum_fusion
  82.9 6.4 %all-to-all-start.3 = ((bf16[8,8,256]{2,1,0:T(8,128)(2,1)}), bf16[8,8,256]{2,1,0:T(8,128)(2,1)S(1)}, u32[]{:S(2)}, u32[]{:S(2)}) async-start(bf16[8,8,256]{2,1,0:T(8,128)(2,1)} %pad_maximum_fusion), calls=%async_computation.3 | async-start | bytes 65536 | tf_op jit(solution)/shard_map/all_to_all | solution.py:20
  89.3 7.0 %all-to-all-done.3.sums_ref = bf16[8,8,256]{2,1,0:T(8,128)(2,1)S(1)} async-done(((bf16[8,8,256]{2,1,0:T(8,128)(2,1)}), bf16[8,8,256]{2,1,0:T(8,128)(2,1)S(1)}, u32[]{:S(2)}, u32[]{:S(2)}) %all-to-all-start.3) | async-done | bytes 32800 | tf_op jit(solution)/shard_map/all_to_all | solution.py:20
  96.3 4.1 %shard_map.88 = (bf16[640,256]{1,0:T(8,128)(2,1)S(1)}, bf16[640,256]{1,0:T(8,128)(2,1)S(1)}) custom-call(s32[7]{0:T(128)S(1)} %pad_add_fusion.info_ref, bf16[512,256]{1,0:T(8,128)(2,1)} %get-tuple-element.12.all_q_hbm, bf16[1024,512]{1,0:T(8,128)(2,1)} %get-tuple-element.13.weight_hbm, bf16[1024,256]{1,0:T(8,128)(2,1)} %get-tuple-element.14.layer_hbm, ...), custom_call_target="tpu_custom_call" | custom-call | tf_op jit(solution)/shard_map/pallas_call | solution.py:318
  100.5 2.7 %collective-permute-start.3 = (bf16[640,256]{1,0:T(8,128)(2,1)S(1)}, bf16[640,256]{1,0:T(8,128)(2,1)S(1)}, u32[]{:S(2)}, u32[]{:S(2)}) collective-permute-start(bf16[640,256]{1,0:T(8,128)(2,1)S(1)} %get-tuple-element.19), channel_id=1, source_target_pairs={{0,4},{4,0},{1,5},{5,1},{2,6},{6,2},{3,7},{7,3},{8,12},{12,8},{9,1... | collective-permute-start | bytes 983048 | tf_op jit(solution)/shard_map/ppermute | solution.py:452
  103.2 1.2 collective-permute-done.3
  104.5 0.1 add_convert_fusion
  104.6 15.6 %all_to_all.36 = bf16[8,80,256]{2,1,0:T(8,128)(2,1)S(1)} all-to-all(bf16[8,80,256]{2,1,0:T(8,128)(2,1)S(1)} %bitcast.17), channel_id=1, replica_groups=mesh['z'=8,'y'=8,'c'=2,'x'=4] {'y'}, dimensions={0} | all-to-all | bytes 655360 | tf_op jit(solution)/shard_map/all_to_all | solution.py:20
  120.2 13.4 %all_to_all.37 = bf16[8,80,256]{2,1,0:T(8,128)(2,1)S(1)} all-to-all(bf16[8,80,256]{2,1,0:T(8,128)(2,1)S(1)} %broadcast_in_dim.80), channel_id=1, replica_groups=mesh['z'=8,'y'=8,'c'=2,'x'=4] {'z'}, dimensions={0} | all-to-all | bytes 655360 | tf_op jit(solution)/shard_map/all_to_all | solution.py:20
  133.8 12.9 %all_to_all.38 = bf16[8,80,256]{2,1,0:T(8,128)(2,1)S(1)} all-to-all(bf16[8,80,256]{2,1,0:T(8,128)(2,1)S(1)} %broadcast_in_dim.81), channel_id=1, replica_groups=mesh['z'=8,'y'=8,'c'=2,'x'=4] {'y'}, dimensions={0} | all-to-all | bytes 655360 | tf_op jit(solution)/shard_map/all_to_all | solution.py:20
  146.7 6.2 %collective-permute-start.4 = (bf16[640,256]{1,0:T(8,128)(2,1)S(1)}, bf16[640,256]{1,0:T(8,128)(2,1)S(1)}, u32[]{:S(2)}, u32[]{:S(2)}) collective-permute-start(bf16[640,256]{1,0:T(8,128)(2,1)S(1)} %bitcast.15), channel_id=1, source_target_pairs={{0,4},{4,0},{1,5},{5,1},{2,6},{6,2},{3,7},{7,3},{8,12},{12,8},{9,1... | collective-permute-start | bytes 983048 | tf_op jit(solution)/shard_map/ppermute | solution.py:456
  152.9 1.2 collective-permute-done.4.other_ref
  154.1 0.9 shard_map.89
  (36 shorter events, 0.4 us)
Async XLA Ops:
  0.6 9.1 %copy-start = (s32[131072]{0:T(1024)S(1)}, s32[131072]{0:T(1024)}, u32[]{:S(2)}) copy-start(s32[131072]{0:T(1024)} %param.13) | copy-start | bytes 1572868
  4.8 4.9 %copy-start.4 = (s32[4,128]{1,0:T(4,128)S(1)}, s32[4,128]{1,0:T(4,128)}, u32[]{:S(2)}) copy-start(s32[4,128]{1,0:T(4,128)} %param.11) | copy-start | bytes 6148
  4.9 4.9 %copy-start.5 = (s32[4]{0:T(128)S(1)}, s32[4]{0:T(128)}, u32[]{:S(2)}) copy-start(s32[4]{0:T(128)} %param.12) | copy-start | bytes 52
  4.9 14.8 %all-to-all-start = ((f32[4,264,256]{2,1,0:T(8,128)}), f32[4,264,256]{2,1,0:T(8,128)S(1)}, u32[]{:S(2)}, u32[]{:S(2)}) async-start(f32[4,264,256]{2,1,0:T(8,128)} %get-tuple-element.11), calls=%async_computation | async-start | bytes 2162688 | tf_op jit(solution)/shard_map/all_to_all | solution.py:20
  20.9 40.1 %all-to-all-start.1 = ((bf16[128,2,640]{2,1,0:T(2,128)(2,1)}), bf16[128,2,640]{2,1,0:T(2,128)(2,1)S(1)}, u32[]{:S(2)}, u32[]{:S(2)}) async-start(bf16[128,2,640]{2,1,0:T(2,128)(2,1)} %fusion.2), calls=%async_computation.1 | async-start | bytes 655360 | tf_op jit(solution)/shard_map/all_to_all | solution.py:20
  44.4 16.8 %collective-permute-start = (bf16[256,256]{1,0:T(8,128)(2,1)S(1)}, bf16[256,256]{1,0:T(8,128)(2,1)S(1)}, u32[]{:S(2)}, u32[]{:S(2)}) collective-permute-start(bf16[256,256]{1,0:T(8,128)(2,1)S(1)} %slice_reduce_fusion.own_ref), channel_id=1, source_target_pairs={{0,1},{1,2},{2,3},{3,0},{4,5},{5,6},{6,7},{7,4},{8,9},{9,10},{10,1... | collective-permute-start | bytes 393224 | tf_op jit(solution)/shard_map/ppermute | solution.py:428
  46.6 14.6 %collective-permute-start.1 = (bf16[256,256]{1,0:T(8,128)(2,1)S(1)}, bf16[256,256]{1,0:T(8,128)(2,1)S(1)}, u32[]{:S(2)}, u32[]{:S(2)}) collective-permute-start(bf16[256,256]{1,0:T(8,128)(2,1)S(1)} %slice_reduce_fusion.own_ref), channel_id=1, source_target_pairs={{0,2},{1,3},{2,0},{3,1},{4,6},{5,7},{6,4},{7,5},{8,10},{9,11},{10,... | collective-permute-start | bytes 393224 | tf_op jit(solution)/shard_map/ppermute | solution.py:428
  50.3 10.9 %collective-permute-start.2 = (bf16[256,256]{1,0:T(8,128)(2,1)S(1)}, bf16[256,256]{1,0:T(8,128)(2,1)S(1)}, u32[]{:S(2)}, u32[]{:S(2)}) collective-permute-start(bf16[256,256]{1,0:T(8,128)(2,1)S(1)} %slice_reduce_fusion.own_ref), channel_id=1, source_target_pairs={{0,3},{1,0},{2,1},{3,2},{4,7},{5,4},{6,5},{7,6},{8,11},{9,8},{10,9... | collective-permute-start | bytes 393224 | tf_op jit(solution)/shard_map/ppermute | solution.py:428
  61.1 28.1 %copy-start.3 = (bf16[4,1024]{1,0:T(4,128)(2,1)S(1)}, bf16[4,1024]{1,0:T(4,128)(2,1)}, u32[]{:S(2)}) copy-start(bf16[4,1024]{1,0:T(4,128)(2,1)} %q_hbm.1) | copy-start | bytes 24580
  61.1 35.2 %copy-start.1 = (bf16[256,256]{1,0:T(8,128)(2,1)S(1)}, bf16[256,256]{1,0:T(8,128)(2,1)}, u32[]{:S(2)}) copy-start(bf16[256,256]{1,0:T(8,128)(2,1)} %w_out_ref.1) | copy-start | bytes 393220
  61.1 35.2 %copy-start.2 = (bf16[16,256]{1,0:T(8,128)(2,1)S(1)}, bf16[16,256]{1,0:T(8,128)(2,1)}, u32[]{:S(2)}) copy-start(bf16[16,256]{1,0:T(8,128)(2,1)} %get-tuple-element.17.hid_q_ref) | copy-start | bytes 24580
  82.9 13.5 %all-to-all-start.3 = ((bf16[8,8,256]{2,1,0:T(8,128)(2,1)}), bf16[8,8,256]{2,1,0:T(8,128)(2,1)S(1)}, u32[]{:S(2)}, u32[]{:S(2)}) async-start(bf16[8,8,256]{2,1,0:T(8,128)(2,1)} %pad_maximum_fusion), calls=%async_computation.3 | async-start | bytes 65536 | tf_op jit(solution)/shard_map/all_to_all | solution.py:20
  100.5 4.0 %collective-permute-start.3 = (bf16[640,256]{1,0:T(8,128)(2,1)S(1)}, bf16[640,256]{1,0:T(8,128)(2,1)S(1)}, u32[]{:S(2)}, u32[]{:S(2)}) collective-permute-start(bf16[640,256]{1,0:T(8,128)(2,1)S(1)} %get-tuple-element.19), channel_id=1, source_target_pairs={{0,4},{4,0},{1,5},{5,1},{2,6},{6,2},{3,7},{7,3},{8,12},{12,8},{9,1... | collective-permute-start | bytes 983048 | tf_op jit(solution)/shard_map/ppermute | solution.py:452
  146.7 7.5 %collective-permute-start.4 = (bf16[640,256]{1,0:T(8,128)(2,1)S(1)}, bf16[640,256]{1,0:T(8,128)(2,1)S(1)}, u32[]{:S(2)}, u32[]{:S(2)}) collective-permute-start(bf16[640,256]{1,0:T(8,128)(2,1)S(1)} %bitcast.15), channel_id=1, source_target_pairs={{0,4},{4,0},{1,5},{5,1},{2,6},{6,2},{3,7},{7,3},{8,12},{12,8},{9,1... | collective-permute-start | bytes 983048 | tf_op jit(solution)/shard_map/ppermute | solution.py:456

commit v8 on v7

--- a/solution.py
+++ b/solution.py
@@ -142,20 +142,10 @@
     return (lax.broadcasted_iota(jnp.int32, shape, 0) + block * shape[0]).astype(F32)
 
 
-def score_kernel(
-    few, slots, scale, info_ref, own_ref, by1_ref, by2_ref, by3_ref, msg_ref,
-    weight_hbm, layer_hbm, all_q_hbm, pay_ref, weight_ref, layer_ref, all_q_ref, code, digit, total_u, emb, sems,
-):
-    copies = Copies(sems)
+def counts_kernel(few, slots, info_ref, msg_ref, all_q_ref, digit_ref, code, digit):
     lines = msg_ref.shape[0]
-    width = layer_ref.shape[1]
-    queries = lines * 2
-    group = queries // few
-    near = (own_ref, by1_ref, by2_ref, by3_ref)
-    for far, ref in enumerate(near):
-        first = lax.rem(info_ref[few + 1] + len(near) - far, len(near)) * ROWS
-        layer_ref[pl.ds(pl.multiple_of(first, ROWS), ROWS), :] = ref[...]
-
+    width = all_q_ref.shape[1]
+    group = lines * 2 // few
     line = lax.broadcasted_iota(jnp.int32, (lines, lines), 0)
     column = lax.broadcasted_iota(jnp.int32, (lines, lines), 1)
     order = jnp.where(column == (line % group) * 2 + line // group, 1.0, 0.0).astype(BF16)
@@ -164,9 +154,7 @@
     for i in range(few):
         first = (i % 2) * width
         parts.append(turned[(i // 2) * group : (i // 2 + 1) * group, first : first + width])
-    all_q = jnp.concatenate(parts, 0).astype(BF16)
-    all_q_ref[...] = all_q
-    stores = [copies.start(layer_ref, layer_hbm), copies.start(all_q_ref, all_q_hbm)]
+    all_q_ref[...] = jnp.concatenate(parts, 0).astype(BF16)
     asked = turned[:group, 2 * width :].T
     who = asked[2 * slots : 3 * slots]
     code[:slots, :] = jnp.where(who > 0.0, asked[:slots] * 32.0 + asked[slots : 2 * slots], -1.0)
@@ -178,17 +166,51 @@
     for i in range(few):
         code[slots + i : slots + i + 1, :] = jnp.where(lane == info_ref[few], info_ref[i], -1).astype(F32)
         digit[slots + i : slots + i + 1, :] = jnp.full((1, group), 32.0**i, F32)
+    for block, chunk in enumerate(blocks_of(digit_ref.shape[0])):
+        ids = row_ids(block, (ROWS, group))
+        digits = jnp.zeros((ROWS, group), F32)
+        for s in range(slots + few):
+            digits = digits + jnp.where(code[s : s + 1, :] == ids, digit[s : s + 1, :], 0.0)
+        digit_ref[chunk, :] = digits.astype(jnp.int32)
+
+
+def counts(info, message, few, slots, items, width):
+    lines = message.shape[0]
+    group = 2 * lines // few
+    return pl.pallas_call(
+        functools.partial(counts_kernel, few, slots),
+        in_specs=[pl.BlockSpec(memory_space=pltpu.SMEM), NEAR],
+        out_specs=[NEAR] * 2,
+        out_shape=[
+            jax.ShapeDtypeStruct((2 * lines, width), BF16),
+            jax.ShapeDtypeStruct((items, group), jnp.int32),
+        ],
+        scratch_shapes=[pltpu.VMEM((slots + 8, group), F32)] * 2,
+        compiler_params=pltpu.CompilerParams(vmem_limit_bytes=VMEM),
+        cost_estimate=pl.CostEstimate(flops=3 * 2**30, bytes_accessed=2**20, transcendentals=0),
+    )(info, message)
+
+
+def score_kernel(
+    few, scale, info_ref, own_ref, by1_ref, by2_ref, by3_ref, all_q_ref, digit_ref,
+    weight_hbm, layer_hbm, all_q_hbm, pay_ref, weight_ref, layer_ref, total_u, emb, sems,
+):
+    copies = Copies(sems)
+    queries, width = all_q_ref.shape
+    group = queries // few
+    near = (own_ref, by1_ref, by2_ref, by3_ref)
+    for far, ref in enumerate(near):
+        first = lax.rem(info_ref[few + 1] + len(near) - far, len(near)) * ROWS
+        layer_ref[pl.ds(pl.multiple_of(first, ROWS), ROWS), :] = ref[...]
+    stores = [copies.start(layer_ref, layer_hbm), copies.start(all_q_ref, all_q_hbm)]
+    all_q = all_q_ref[...]
 
     total_d = jnp.zeros((1, queries), F32)
     for block, chunk in enumerate(blocks_of(layer_ref.shape[0])):
         e16 = jnp.tanh(layer_ref[chunk, :].astype(F32)).astype(BF16)
         emb[chunk, :] = e16
         grown = jnp.exp(scale * dot_lanes(e16, all_q))
-        ids = row_ids(block, (ROWS, group))
-        digits = jnp.zeros((ROWS, group), F32)
-        for s in range(slots + few):
-            digits = digits + jnp.where(code[s : s + 1, :] == ids, digit[s : s + 1, :], 0.0)
-        digits = digits.astype(jnp.int32)
+        digits = digit_ref[chunk, :]
         times = [((digits >> (5 * i)) & 31).astype(F32) for i in range(few)]
         weight = jnp.concatenate(times, 1) * grown
         weight16 = weight.astype(BF16)
@@ -207,14 +229,14 @@
         store.wait()
 
 
-def score(info, layers, message, few, slots, scale, peers):
+def score(info, layers, all_q, digits, few, scale, peers):
     share, width = layers[0].shape
     items = share * len(layers)
-    queries = 2 * message.shape[0]
+    queries = all_q.shape[0]
     pay = (peers, queries // peers + 8, width)
     return pl.pallas_call(
-        functools.partial(score_kernel, few, slots, scale),
-        in_specs=[pl.BlockSpec(memory_space=pltpu.SMEM)] + [NEAR] * (len(layers) + 1),
+        functools.partial(score_kernel, few, scale),
+        in_specs=[pl.BlockSpec(memory_space=pltpu.SMEM)] + [NEAR] * (len(layers) + 2),
         out_specs=[FAR] * 3 + [NEAR],
         out_shape=[
             pltpu.HBM((items, queries), BF16),
@@ -225,15 +247,12 @@
         scratch_shapes=[
             pltpu.VMEM((items, queries), BF16),
             pltpu.VMEM((items, width), BF16),
-            pltpu.VMEM((queries, width), BF16),
-            pltpu.VMEM((slots + 8, queries // few), F32),
-            pltpu.VMEM((slots + 8, queries // few), F32),
             pltpu.VMEM((queries, width), F32),
             pltpu.VMEM((items, width), BF16),
             pltpu.SemaphoreType.DMA((3 + items // ROWS,)),
         ],
         compiler_params=pltpu.CompilerParams(vmem_limit_bytes=VMEM),
-    )(info, *layers, message)
+    )(info, *layers, all_q, digits)
 
 
 def backward_kernel(
@@ -427,7 +446,8 @@
     for far in range(1, x_count):
         layers.append(lax.ppermute(own, "x", [(i, (i + far) % x_count) for i in range(x_count)]))
 
-    weight, layer_out, all_q, pay = score(info, layers, message, few, capacity, scale, yc_count)
+    all_q, digits = counts(info, message, few, capacity, item_count, width)
+    weight, layer_out, all_q, pay = score(info, layers, all_q, digits, few, scale, yc_count)
     first = total(exchange(pay, ("y", "c")))
     mine = queries // yc_count
     d_rows = queries // width

time: 156 us -> 155 us (level)
    pallas_call x1 -> x2, Pallas kernels: 3.36 us -> 4.49 us  [the longest x1 2.32 us: counts(): pl.pallas_call(functools.partial(counts_kernel, few, slots), in_specs=[pl...]
  transfers between devices with their start and end apart: 8 -> 8, of which waited for: 5 -> 5; matrix products, arithmetic and copies ran while one was open for 3% -> 3% of each run, Pallas kernels for 0% -> 2%
where the time goes in v8:
time: 155 us; the launch traced here: 154 us
  blocking collectives  58.4 us (38%)
  starting transfers between devices  50.9 us (33%)
  waiting for transfers between devices  22.7 us (15%)
  Pallas kernels  13.7 us (9%)
  local copies, waits for them, and re-layouts  4.08 us (3%)
  other arithmetic  2.14 us (1%)
    all_to_all x4, blocking collectives, exchange(): return lax.all_to_all(blocks, axes, split_axis=0, concat_axis=0, tiled=True)  58.4 us
    all_to_all x3, starting transfers between devices, exchange(): return lax.all_to_all(blocks, axes, split_axis=0, concat_axis=0, tiled=True)  33.5 us
    all_to_all x3, waiting for transfers between devices, exchange(): return lax.all_to_all(blocks, axes, split_axis=0, concat_axis=0, tiled=True)  20.2 us
    ppermute x3, starting transfers between devices, local(): lax.ppermute(own, 'x', [(i, (i + far) % x_count) for i in range(x_count)])  8.41 us
    ppermute x1, starting transfers between devices, local(): return tuple(assemble(grads, lax.ppermute(grads, 'c', swap), w_in.shape[0]))  6.24 us
    pallas_call x1, Pallas kernels, forward(): pl.pallas_call(forward_kernel, in_specs=[FAR] * 4, out_specs=[FAR] * 3, o...  4.2 us
    pallas_call x1, Pallas kernels, backward(): pl.pallas_call(functools.partial(backward_kernel, few, scale), in_specs=[...  4.16 us
    gather x1, local copies, waits for them, and re-layouts, local(): rows = jnp.take(owner_map, named, axis=0)  3.56 us
  transfers between devices with their start and end apart: 8, of which 5 were waited for; matrix products, arithmetic and copies ran while one was open for 3% of the time, Pallas kernels for 2%

profile of v8, /device:TPU:1, one launch (start us, length us, event | category | flops | bytes accessed | tf_op | source)
XLA Modules:
  0.0 153.9 jit_solution(6466480330089821841)
XLA Ops:
  0.6 4.2 %shard_map.86 = (f32[4,264,256]{2,1,0:T(8,128)}, bf16[1024,256]{1,0:T(8,128)(2,1)}, bf16[16,256]{1,0:T(8,128)(2,1)}) custom-call(bf16[4,1024]{1,0:T(4,128)(2,1)} %q_hbm.1, bf16[1024,1024]{1,0:T(8,128)(2,1)} %x_hbm.3, bf16[1024,256]{1,0:T(8,128)(2,1)} %w_in_hbm.1, bf16[256,256]{1,0:T(8,128)(2,1)} %w_out_ref.1), custom_call_target="tpu_custom_call" | custom-call | tf_op jit(solution)/shard_map/pallas_call | solution.py:119
  4.9 4.9 %all-to-all-start = ((f32[4,264,256]{2,1,0:T(8,128)}), f32[4,264,256]{2,1,0:T(8,128)S(1)}, u32[]{:S(2)}, u32[]{:S(2)}) async-start(f32[4,264,256]{2,1,0:T(8,128)} %get-tuple-element.13), calls=%async_computation | async-start | bytes 2162688 | tf_op jit(solution)/shard_map/all_to_all | solution.py:20
  9.8 3.6 %gather_fusion = s32[516]{0:T(1024)S(1)} fusion(s32[131072]{0:T(1024)S(1)} %copy-done, s32[1024]{0:T(1024)S(1)} %pad_clamp_fusion), kind=kCustom, calls=%fused_computation | custom fusion | bytes 6192 | tf_op jit(solution)/shard_map/jit(_take)/gather | solution.py:426
  13.4 0.3 fusion
  13.7 0.7 fusion.1
  14.4 0.1 copy.14
  14.6 5.1 %all-to-all-done = f32[4,264,256]{2,1,0:T(8,128)S(1)} async-done(((f32[4,264,256]{2,1,0:T(8,128)}), f32[4,264,256]{2,1,0:T(8,128)S(1)}, u32[]{:S(2)}, u32[]{:S(2)}) %all-to-all-start) | async-done | bytes 1081376 | tf_op jit(solution)/shard_map/all_to_all | solution.py:20
  19.7 0.1 broadcast_in_dim.72
  19.8 1.0 fusion.2
  20.9 23.4 %all-to-all-start.1 = ((bf16[128,2,640]{2,1,0:T(2,128)(2,1)}), bf16[128,2,640]{2,1,0:T(2,128)(2,1)S(1)}, u32[]{:S(2)}, u32[]{:S(2)}) async-start(bf16[128,2,640]{2,1,0:T(2,128)(2,1)} %fusion.2), calls=%async_computation.1 | async-start | bytes 655360 | tf_op jit(solution)/shard_map/all_to_all | solution.py:20
  44.3 0.1 pad_add_fusion.info_ref
  44.5 2.2 %collective-permute-start = (bf16[256,256]{1,0:T(8,128)(2,1)S(1)}, bf16[256,256]{1,0:T(8,128)(2,1)S(1)}, u32[]{:S(2)}, u32[]{:S(2)}) collective-permute-start(bf16[256,256]{1,0:T(8,128)(2,1)S(1)} %slice_reduce_fusion.own_ref), channel_id=1, source_target_pairs={{0,1},{1,2},{2,3},{3,0},{4,5},{5,6},{6,7},{7,4},{8,9},{9,10},{10,1... | collective-permute-start | bytes 393224 | tf_op jit(solution)/shard_map/ppermute | solution.py:447
  46.7 3.7 %collective-permute-start.1 = (bf16[256,256]{1,0:T(8,128)(2,1)S(1)}, bf16[256,256]{1,0:T(8,128)(2,1)S(1)}, u32[]{:S(2)}, u32[]{:S(2)}) collective-permute-start(bf16[256,256]{1,0:T(8,128)(2,1)S(1)} %slice_reduce_fusion.own_ref), channel_id=1, source_target_pairs={{0,2},{1,3},{2,0},{3,1},{4,6},{5,7},{6,4},{7,5},{8,10},{9,11},{10,... | collective-permute-start | bytes 393224 | tf_op jit(solution)/shard_map/ppermute | solution.py:447
  50.4 2.5 %collective-permute-start.2 = (bf16[256,256]{1,0:T(8,128)(2,1)S(1)}, bf16[256,256]{1,0:T(8,128)(2,1)S(1)}, u32[]{:S(2)}, u32[]{:S(2)}) collective-permute-start(bf16[256,256]{1,0:T(8,128)(2,1)S(1)} %slice_reduce_fusion.own_ref), channel_id=1, source_target_pairs={{0,3},{1,0},{2,1},{3,2},{4,7},{5,4},{6,5},{7,6},{8,11},{9,8},{10,9... | collective-permute-start | bytes 393224 | tf_op jit(solution)/shard_map/ppermute | solution.py:447
  52.9 8.1 %all-to-all-done.1 = bf16[128,2,640]{2,1,0:T(2,128)(2,1)S(1)} async-done(((bf16[128,2,640]{2,1,0:T(2,128)(2,1)}), bf16[128,2,640]{2,1,0:T(2,128)(2,1)S(1)}, u32[]{:S(2)}, u32[]{:S(2)}) %all-to-all-start.1) | async-done | bytes 327712 | tf_op jit(solution)/shard_map/all_to_all | solution.py:20
  61.0 0.1 reshape.150.msg_ref
  61.1 2.3 %shard_map.87 = (bf16[512,256]{1,0:T(8,128)(2,1)S(1)}, s32[1024,128]{1,0:T(8,128)S(1)}) custom-call(s32[7]{0:T(128)S(1)} %pad_add_fusion.info_ref, bf16[256,640]{1,0:T(8,128)(2,1)S(1)} %reshape.150.msg_ref), custom_call_target="tpu_custom_call" | custom-call | flops 3221225472 | bytes 1048576 | tf_op jit(solution)/shard_map/pallas_call | solution.py:180
  63.5 2.2 %shard_map.88 = (bf16[1024,512]{1,0:T(8,128)(2,1)}, bf16[1024,256]{1,0:T(8,128)(2,1)}, bf16[512,256]{1,0:T(8,128)(2,1)}, bf16[16,40,256]{2,1,0:T(8,128)(2,1)S(1)}) custom-call(s32[7]{0:T(128)S(1)} %pad_add_fusion.info_ref, bf16[256,256]{1,0:T(8,128)(2,1)S(1)} %slice_reduce_fusion.own_ref, bf16[256,256]{1,0:T(8,128)(2,1)S(1)} %collective-permute-done.by1_ref, ...), custom_call_target="tpu_custom_call" | custom-call | tf_op jit(solution)/shard_map/pallas_call | solution.py:237
  65.7 16.5 %all_to_all.35 = bf16[16,40,256]{2,1,0:T(8,128)(2,1)S(1)} all-to-all(bf16[16,40,256]{2,1,0:T(8,128)(2,1)S(1)} %get-tuple-element.20), channel_id=1, replica_groups=mesh['z'=8,'y'=8,'c'=2,'x'=4] {'y','c'}, dimensions={0} | all-to-all | bytes 655360 | tf_op jit(solution)/shard_map/all_to_all | solution.py:20
  82.3 0.6 pad_maximum_fusion
  82.9 5.2 %all-to-all-start.3 = ((bf16[8,8,256]{2,1,0:T(8,128)(2,1)}), bf16[8,8,256]{2,1,0:T(8,128)(2,1)S(1)}, u32[]{:S(2)}, u32[]{:S(2)}) async-start(bf16[8,8,256]{2,1,0:T(8,128)(2,1)} %pad_maximum_fusion), calls=%async_computation.3 | async-start | bytes 65536 | tf_op jit(solution)/shard_map/all_to_all | solution.py:20
  88.2 7.0 %all-to-all-done.3.sums_ref = bf16[8,8,256]{2,1,0:T(8,128)(2,1)S(1)} async-done(((bf16[8,8,256]{2,1,0:T(8,128)(2,1)}), bf16[8,8,256]{2,1,0:T(8,128)(2,1)S(1)}, u32[]{:S(2)}, u32[]{:S(2)}) %all-to-all-start.3) | async-done | bytes 32800 | tf_op jit(solution)/shard_map/all_to_all | solution.py:20
  95.2 4.2 %shard_map.89 = (bf16[640,256]{1,0:T(8,128)(2,1)S(1)}, bf16[640,256]{1,0:T(8,128)(2,1)S(1)}) custom-call(s32[7]{0:T(128)S(1)} %pad_add_fusion.info_ref, bf16[512,256]{1,0:T(8,128)(2,1)} %get-tuple-element.16.all_q_hbm, bf16[1024,512]{1,0:T(8,128)(2,1)} %get-tuple-element.17.weight_hbm, bf16[1024,256]{1,0:T(8,128)(2,1)} %get-tuple-element.18.layer_hbm, ...), custom_call_target="tpu_custom_call" | custom-call | tf_op jit(solution)/shard_map/pallas_call | solution.py:337
  99.4 2.7 %collective-permute-start.3 = (bf16[640,256]{1,0:T(8,128)(2,1)S(1)}, bf16[640,256]{1,0:T(8,128)(2,1)S(1)}, u32[]{:S(2)}, u32[]{:S(2)}) collective-permute-start(bf16[640,256]{1,0:T(8,128)(2,1)S(1)} %get-tuple-element.23), channel_id=1, source_target_pairs={{0,4},{4,0},{1,5},{5,1},{2,6},{6,2},{3,7},{7,3},{8,12},{12,8},{9,1... | collective-permute-start | bytes 983048 | tf_op jit(solution)/shard_map/ppermute | solution.py:472
  102.1 1.2 collective-permute-done.3
  103.4 0.1 add_convert_fusion
  103.4 15.6 %all_to_all.36 = bf16[8,80,256]{2,1,0:T(8,128)(2,1)S(1)} all-to-all(bf16[8,80,256]{2,1,0:T(8,128)(2,1)S(1)} %bitcast.17), channel_id=1, replica_groups=mesh['z'=8,'y'=8,'c'=2,'x'=4] {'y'}, dimensions={0} | all-to-all | bytes 655360 | tf_op jit(solution)/shard_map/all_to_all | solution.py:20
  119.2 13.4 %all_to_all.37 = bf16[8,80,256]{2,1,0:T(8,128)(2,1)S(1)} all-to-all(bf16[8,80,256]{2,1,0:T(8,128)(2,1)S(1)} %broadcast_in_dim.80), channel_id=1, replica_groups=mesh['z'=8,'y'=8,'c'=2,'x'=4] {'z'}, dimensions={0} | all-to-all | bytes 655360 | tf_op jit(solution)/shard_map/all_to_all | solution.py:20
  132.7 12.9 %all_to_all.38 = bf16[8,80,256]{2,1,0:T(8,128)(2,1)S(1)} all-to-all(bf16[8,80,256]{2,1,0:T(8,128)(2,1)S(1)} %broadcast_in_dim.81), channel_id=1, replica_groups=mesh['z'=8,'y'=8,'c'=2,'x'=4] {'y'}, dimensions={0} | all-to-all | bytes 655360 | tf_op jit(solution)/shard_map/all_to_all | solution.py:20
  145.6 6.2 %collective-permute-start.4 = (bf16[640,256]{1,0:T(8,128)(2,1)S(1)}, bf16[640,256]{1,0:T(8,128)(2,1)S(1)}, u32[]{:S(2)}, u32[]{:S(2)}) collective-permute-start(bf16[640,256]{1,0:T(8,128)(2,1)S(1)} %bitcast.15), channel_id=1, source_target_pairs={{0,4},{4,0},{1,5},{5,1},{2,6},{6,2},{3,7},{7,3},{8,12},{12,8},{9,1... | collective-permute-start | bytes 983048 | tf_op jit(solution)/shard_map/ppermute | solution.py:476
  151.8 1.2 collective-permute-done.4.other_ref
  153.1 0.9 shard_map.90
  (37 shorter events, 0.4 us)
Async XLA Ops:
  0.6 9.1 %copy-start = (s32[131072]{0:T(1024)S(1)}, s32[131072]{0:T(1024)}, u32[]{:S(2)}) copy-start(s32[131072]{0:T(1024)} %param.13) | copy-start | bytes 1572868
  4.8 4.9 %copy-start.4 = (s32[4,128]{1,0:T(4,128)S(1)}, s32[4,128]{1,0:T(4,128)}, u32[]{:S(2)}) copy-start(s32[4,128]{1,0:T(4,128)} %param.11) | copy-start | bytes 6148
  4.9 4.9 %copy-start.5 = (s32[4]{0:T(128)S(1)}, s32[4]{0:T(128)}, u32[]{:S(2)}) copy-start(s32[4]{0:T(128)} %param.12) | copy-start | bytes 52
  4.9 14.8 %all-to-all-start = ((f32[4,264,256]{2,1,0:T(8,128)}), f32[4,264,256]{2,1,0:T(8,128)S(1)}, u32[]{:S(2)}, u32[]{:S(2)}) async-start(f32[4,264,256]{2,1,0:T(8,128)} %get-tuple-element.13), calls=%async_computation | async-start | bytes 2162688 | tf_op jit(solution)/shard_map/all_to_all | solution.py:20
  20.9 40.1 %all-to-all-start.1 = ((bf16[128,2,640]{2,1,0:T(2,128)(2,1)}), bf16[128,2,640]{2,1,0:T(2,128)(2,1)S(1)}, u32[]{:S(2)}, u32[]{:S(2)}) async-start(bf16[128,2,640]{2,1,0:T(2,128)(2,1)} %fusion.2), calls=%async_computation.1 | async-start | bytes 655360 | tf_op jit(solution)/shard_map/all_to_all | solution.py:20
  44.5 19.0 %collective-permute-start = (bf16[256,256]{1,0:T(8,128)(2,1)S(1)}, bf16[256,256]{1,0:T(8,128)(2,1)S(1)}, u32[]{:S(2)}, u32[]{:S(2)}) collective-permute-start(bf16[256,256]{1,0:T(8,128)(2,1)S(1)} %slice_reduce_fusion.own_ref), channel_id=1, source_target_pairs={{0,1},{1,2},{2,3},{3,0},{4,5},{5,6},{6,7},{7,4},{8,9},{9,10},{10,1... | collective-permute-start | bytes 393224 | tf_op jit(solution)/shard_map/ppermute | solution.py:447
  46.7 16.8 %collective-permute-start.1 = (bf16[256,256]{1,0:T(8,128)(2,1)S(1)}, bf16[256,256]{1,0:T(8,128)(2,1)S(1)}, u32[]{:S(2)}, u32[]{:S(2)}) collective-permute-start(bf16[256,256]{1,0:T(8,128)(2,1)S(1)} %slice_reduce_fusion.own_ref), channel_id=1, source_target_pairs={{0,2},{1,3},{2,0},{3,1},{4,6},{5,7},{6,4},{7,5},{8,10},{9,11},{10,... | collective-permute-start | bytes 393224 | tf_op jit(solution)/shard_map/ppermute | solution.py:447
  50.4 13.1 %collective-permute-start.2 = (bf16[256,256]{1,0:T(8,128)(2,1)S(1)}, bf16[256,256]{1,0:T(8,128)(2,1)S(1)}, u32[]{:S(2)}, u32[]{:S(2)}) collective-permute-start(bf16[256,256]{1,0:T(8,128)(2,1)S(1)} %slice_reduce_fusion.own_ref), channel_id=1, source_target_pairs={{0,3},{1,0},{2,1},{3,2},{4,7},{5,4},{6,5},{7,6},{8,11},{9,8},{10,9... | collective-permute-start | bytes 393224 | tf_op jit(solution)/shard_map/ppermute | solution.py:447
  63.5 24.7 %copy-start.3 = (bf16[4,1024]{1,0:T(4,128)(2,1)S(1)}, bf16[4,1024]{1,0:T(4,128)(2,1)}, u32[]{:S(2)}) copy-start(bf16[4,1024]{1,0:T(4,128)(2,1)} %q_hbm.1) | copy-start | bytes 24580
  63.5 31.7 %copy-start.1 = (bf16[256,256]{1,0:T(8,128)(2,1)S(1)}, bf16[256,256]{1,0:T(8,128)(2,1)}, u32[]{:S(2)}) copy-start(bf16[256,256]{1,0:T(8,128)(2,1)} %w_out_ref.1) | copy-start | bytes 393220
  63.5 31.7 %copy-start.2 = (bf16[16,256]{1,0:T(8,128)(2,1)S(1)}, bf16[16,256]{1,0:T(8,128)(2,1)}, u32[]{:S(2)}) copy-start(bf16[16,256]{1,0:T(8,128)(2,1)} %get-tuple-element.21.hid_q_ref) | copy-start | bytes 24580
  82.9 12.3 %all-to-all-start.3 = ((bf16[8,8,256]{2,1,0:T(8,128)(2,1)}), bf16[8,8,256]{2,1,0:T(8,128)(2,1)S(1)}, u32[]{:S(2)}, u32[]{:S(2)}) async-start(bf16[8,8,256]{2,1,0:T(8,128)(2,1)} %pad_maximum_fusion), calls=%async_computation.3 | async-start | bytes 65536 | tf_op jit(solution)/shard_map/all_to_all | solution.py:20
  99.4 4.0 %collective-permute-start.3 = (bf16[640,256]{1,0:T(8,128)(2,1)S(1)}, bf16[640,256]{1,0:T(8,128)(2,1)S(1)}, u32[]{:S(2)}, u32[]{:S(2)}) collective-permute-start(bf16[640,256]{1,0:T(8,128)(2,1)S(1)} %get-tuple-element.23), channel_id=1, source_target_pairs={{0,4},{4,0},{1,5},{5,1},{2,6},{6,2},{3,7},{7,3},{8,12},{12,8},{9,1... | collective-permute-start | bytes 983048 | tf_op jit(solution)/shard_map/ppermute | solution.py:472
  145.6 7.5 %collective-permute-start.4 = (bf16[640,256]{1,0:T(8,128)(2,1)S(1)}, bf16[640,256]{1,0:T(8,128)(2,1)S(1)}, u32[]{:S(2)}, u32[]{:S(2)}) collective-permute-start(bf16[640,256]{1,0:T(8,128)(2,1)S(1)} %bitcast.15), channel_id=1, source_target_pairs={{0,4},{4,0},{1,5},{5,1},{2,6},{6,2},{3,7},{7,3},{8,12},{12,8},{9,1... | collective-permute-start | bytes 983048 | tf_op jit(solution)/shard_map/ppermute | solution.py:476

commit v9 on v8

--- a/solution.py
+++ b/solution.py
@@ -142,7 +142,20 @@
     return (lax.broadcasted_iota(jnp.int32, shape, 0) + block * shape[0]).astype(F32)
 
 
-def counts_kernel(few, slots, info_ref, msg_ref, all_q_ref, digit_ref, code, digit):
+def weighed(scale, few, layer, all_q, digits):
+    emb = jnp.tanh(layer.astype(F32)).astype(BF16)
+    times = [((digits >> (5 * i)) & 31).astype(F32) for i in range(few)]
+    weight = jnp.concatenate(times, 1) * jnp.exp(scale * dot_lanes(emb, all_q))
+    return emb, weight
+
+
+def share_of(info_ref, few, far):
+    return pl.ds(pl.multiple_of(lax.bitwise_xor(info_ref[few + 1], far) * ROWS, ROWS), ROWS)
+
+
+def counts_kernel(
+    few, slots, scale, info_ref, msg_ref, own_ref, all_q_ref, digit_ref, weight_ref, d_ref, code, digit
+):
     lines = msg_ref.shape[0]
     width = all_q_ref.shape[1]
     group = lines * 2 // few
@@ -172,27 +185,34 @@
         for s in range(slots + few):
             digits = digits + jnp.where(code[s : s + 1, :] == ids, digit[s : s + 1, :], 0.0)
         digit_ref[chunk, :] = digits.astype(jnp.int32)
-
-
-def counts(info, message, few, slots, items, width):
+    own_digits = digit_ref[share_of(info_ref, few, 0), :]
+    weight = weighed(scale, few, own_ref[...], all_q_ref[...], own_digits)[1]
+    weight_ref[...] = weight.astype(BF16)
+    d_ref[...] = jnp.sum(weight, 0, keepdims=True)
+
+
+def counts(info, message, own, few, slots, scale, items):
+    width = own.shape[1]
     lines = message.shape[0]
     group = 2 * lines // few
     return pl.pallas_call(
-        functools.partial(counts_kernel, few, slots),
-        in_specs=[pl.BlockSpec(memory_space=pltpu.SMEM), NEAR],
-        out_specs=[NEAR] * 2,
+        functools.partial(counts_kernel, few, slots, scale),
+        in_specs=[pl.BlockSpec(memory_space=pltpu.SMEM), NEAR, NEAR],
+        out_specs=[NEAR] * 4,
         out_shape=[
             jax.ShapeDtypeStruct((2 * lines, width), BF16),
             jax.ShapeDtypeStruct((items, group), jnp.int32),
+            jax.ShapeDtypeStruct((own.shape[0], 2 * lines), BF16),
+            jax.ShapeDtypeStruct((1, 2 * lines), F32),
         ],
         scratch_shapes=[pltpu.VMEM((slots + 8, group), F32)] * 2,
         compiler_params=pltpu.CompilerParams(vmem_limit_bytes=VMEM),
         cost_estimate=pl.CostEstimate(flops=3 * 2**30, bytes_accessed=2**20, transcendentals=0),
-    )(info, message)
+    )(info, message, own)
 
 
 def score_kernel(
-    few, scale, info_ref, own_ref, by1_ref, by2_ref, by3_ref, all_q_ref, digit_ref,
+    few, scale, info_ref, own_ref, by2_ref, by1_ref, by3_ref, all_q_ref, digit_ref, own_weight_ref, own_d_ref,
     weight_hbm, layer_hbm, all_q_hbm, pay_ref, weight_ref, layer_ref, total_u, emb, sems,
 ):
     copies = Copies(sems)
@@ -200,23 +220,22 @@
     group = queries // few
     near = (own_ref, by1_ref, by2_ref, by3_ref)
     for far, ref in enumerate(near):
-        first = lax.rem(info_ref[few + 1] + len(near) - far, len(near)) * ROWS
-        layer_ref[pl.ds(pl.multiple_of(first, ROWS), ROWS), :] = ref[...]
+        layer_ref[share_of(info_ref, few, far), :] = ref[...]
     stores = [copies.start(layer_ref, layer_hbm), copies.start(all_q_ref, all_q_hbm)]
     all_q = all_q_ref[...]
 
-    total_d = jnp.zeros((1, queries), F32)
-    for block, chunk in enumerate(blocks_of(layer_ref.shape[0])):
-        e16 = jnp.tanh(layer_ref[chunk, :].astype(F32)).astype(BF16)
-        emb[chunk, :] = e16
-        grown = jnp.exp(scale * dot_lanes(e16, all_q))
-        digits = digit_ref[chunk, :]
-        times = [((digits >> (5 * i)) & 31).astype(F32) for i in range(few)]
-        weight = jnp.concatenate(times, 1) * grown
-        weight16 = weight.astype(BF16)
-        weight_ref[chunk, :] = weight16
+    total_d = own_d_ref[...]
+    for far, ref in enumerate(near):
+        chunk = share_of(info_ref, few, far)
+        if far == 0:
+            emb[chunk, :] = jnp.tanh(ref[...].astype(F32)).astype(BF16)
+            weight_ref[chunk, :] = own_weight_ref[...]
+        else:
+            e16, weight = weighed(scale, few, ref[...], all_q, digit_ref[chunk, :])
+            emb[chunk, :] = e16
+            weight_ref[chunk, :] = weight.astype(BF16)
+            total_d = total_d + jnp.sum(weight, 0, keepdims=True)
         stores.append(copies.start(weight_ref.at[chunk, :], weight_hbm.at[chunk, :]))
-        total_d = total_d + jnp.sum(weight, 0, keepdims=True)
 
     total_u[...] = dot_rows(weight_ref[...], emb[...])
     d = jnp.concatenate([total_d[:, i * width : (i + 1) * width] for i in range(queries // width)], 0)
@@ -229,14 +248,14 @@
         store.wait()
 
 
-def score(info, layers, all_q, digits, few, scale, peers):
+def score(info, layers, counted, few, scale, peers):
     share, width = layers[0].shape
     items = share * len(layers)
-    queries = all_q.shape[0]
+    queries = counted[0].shape[0]
     pay = (peers, queries // peers + 8, width)
     return pl.pallas_call(
         functools.partial(score_kernel, few, scale),
-        in_specs=[pl.BlockSpec(memory_space=pltpu.SMEM)] + [NEAR] * (len(layers) + 2),
+        in_specs=[pl.BlockSpec(memory_space=pltpu.SMEM)] + [NEAR] * (len(layers) + len(counted)),
         out_specs=[FAR] * 3 + [NEAR],
         out_shape=[
             pltpu.HBM((items, queries), BF16),
@@ -252,7 +271,7 @@
             pltpu.SemaphoreType.DMA((3 + items // ROWS,)),
         ],
         compiler_params=pltpu.CompilerParams(vmem_limit_bytes=VMEM),
-    )(info, *layers, all_q, digits)
+    )(info, *layers, *counted)
 
 
 def backward_kernel(
@@ -443,11 +462,11 @@
     message = exchange(jnp.concatenate([sent_q, codes], 2), YCZ)
     message = message.reshape(2 * dp_count, -1)
     layers = [own]
-    for far in range(1, x_count):
-        layers.append(lax.ppermute(own, "x", [(i, (i + far) % x_count) for i in range(x_count)]))
-
-    all_q, digits = counts(info, message, few, capacity, item_count, width)
-    weight, layer_out, all_q, pay = score(info, layers, all_q, digits, few, scale, yc_count)
+    for far in (2, 1, 3):
+        layers.append(lax.ppermute(own, "x", [(i, i ^ far) for i in range(x_count)]))
+
+    counted = counts(info, message, own, few, capacity, scale, item_count)
+    weight, layer_out, all_q, pay = score(info, layers, counted, few, scale, yc_count)
     first = total(exchange(pay, ("y", "c")))
     mine = queries // yc_count
     d_rows = queries // width

time: 155 us -> 154 us (level)
  no operation moved by 1% of the time
where the time goes in v9:
time: 154 us
  blocking collectives  58.4 us (38%)
  starting transfers between devices  51.2 us (33%)
  waiting for transfers between devices  22.1 us (14%)
  Pallas kernels  13.8 us (9%)
  local copies, waits for them, and re-layouts  4.08 us (3%)
  other arithmetic  2.14 us (1%)
    all_to_all x4, blocking collectives, exchange(): return lax.all_to_all(blocks, axes, split_axis=0, concat_axis=0, tiled=True)  58.4 us
    all_to_all x3, starting transfers between devices, exchange(): return lax.all_to_all(blocks, axes, split_axis=0, concat_axis=0, tiled=True)  33.3 us
    all_to_all x3, waiting for transfers between devices, exchange(): return lax.all_to_all(blocks, axes, split_axis=0, concat_axis=0, tiled=True)  19.7 us
    ppermute x3, starting transfers between devices, local(): lax.ppermute(own, 'x', [(i, i ^ far) for i in range(x_count)])  8.98 us
    ppermute x1, starting transfers between devices, local(): return tuple(assemble(grads, lax.ppermute(grads, 'c', swap), w_in.shape[0]))  6.24 us
    pallas_call x1, Pallas kernels, forward(): pl.pallas_call(forward_kernel, in_specs=[FAR] * 4, out_specs=[FAR] * 3, o...  4.2 us
    pallas_call x1, Pallas kernels, backward(): pl.pallas_call(functools.partial(backward_kernel, few, scale), in_specs=[...  4.15 us
    gather x1, local copies, waits for them, and re-layouts, local(): rows = jnp.take(owner_map, named, axis=0)  3.56 us
  transfers between devices with their start and end apart: 8, of which 5 were waited for; matrix products, arithmetic and copies ran while one was open for 3% of the time, Pallas kernels for 2%

profile of v9, /device:TPU:1, one launch (start us, length us, event | category | flops | bytes accessed | tf_op | source)
XLA Modules:
  0.0 153.8 jit_solution(3081450936994579771)
XLA Ops:
  0.6 4.2 %shard_map.86 = (f32[4,264,256]{2,1,0:T(8,128)}, bf16[1024,256]{1,0:T(8,128)(2,1)}, bf16[16,256]{1,0:T(8,128)(2,1)}) custom-call(bf16[4,1024]{1,0:T(4,128)(2,1)} %q_hbm.1, bf16[1024,1024]{1,0:T(8,128)(2,1)} %x_hbm.3, bf16[1024,256]{1,0:T(8,128)(2,1)} %w_in_hbm.1, bf16[256,256]{1,0:T(8,128)(2,1)} %w_out_ref.1), custom_call_target="tpu_custom_call" | custom-call | tf_op jit(solution)/shard_map/pallas_call | solution.py:119
  4.9 4.9 %all-to-all-start = ((f32[4,264,256]{2,1,0:T(8,128)}), f32[4,264,256]{2,1,0:T(8,128)S(1)}, u32[]{:S(2)}, u32[]{:S(2)}) async-start(f32[4,264,256]{2,1,0:T(8,128)} %get-tuple-element.15), calls=%async_computation | async-start | bytes 2162688 | tf_op jit(solution)/shard_map/all_to_all | solution.py:20
  9.8 3.6 %gather_fusion = s32[516]{0:T(1024)S(1)} fusion(s32[131072]{0:T(1024)S(1)} %copy-done, s32[1024]{0:T(1024)S(1)} %pad_clamp_fusion), kind=kCustom, calls=%fused_computation | custom fusion | bytes 6192 | tf_op jit(solution)/shard_map/jit(_take)/gather | solution.py:445
  13.4 0.3 fusion
  13.7 0.7 fusion.1
  14.4 0.1 copy.14
  14.6 5.1 %all-to-all-done = f32[4,264,256]{2,1,0:T(8,128)S(1)} async-done(((f32[4,264,256]{2,1,0:T(8,128)}), f32[4,264,256]{2,1,0:T(8,128)S(1)}, u32[]{:S(2)}, u32[]{:S(2)}) %all-to-all-start) | async-done | bytes 1081376 | tf_op jit(solution)/shard_map/all_to_all | solution.py:20
  19.7 0.1 broadcast_in_dim.72
  19.8 1.0 fusion.2
  20.9 23.4 %all-to-all-start.1 = ((bf16[128,2,640]{2,1,0:T(2,128)(2,1)}), bf16[128,2,640]{2,1,0:T(2,128)(2,1)S(1)}, u32[]{:S(2)}, u32[]{:S(2)}) async-start(bf16[128,2,640]{2,1,0:T(2,128)(2,1)} %fusion.2), calls=%async_computation.1 | async-start | bytes 655360 | tf_op jit(solution)/shard_map/all_to_all | solution.py:20
  44.3 0.1 pad_add_fusion.info_ref
  44.5 2.2 %collective-permute-start = (bf16[256,256]{1,0:T(8,128)(2,1)S(1)}, bf16[256,256]{1,0:T(8,128)(2,1)S(1)}, u32[]{:S(2)}, u32[]{:S(2)}) collective-permute-start(bf16[256,256]{1,0:T(8,128)(2,1)S(1)} %slice_reduce_fusion.own_ref), channel_id=1, source_target_pairs={{0,2},{1,3},{2,0},{3,1},{4,6},{5,7},{6,4},{7,5},{8,10},{9,11},{10,... | collective-permute-start | bytes 393224 | tf_op jit(solution)/shard_map/ppermute | solution.py:466
  46.6 3.1 %collective-permute-start.1 = (bf16[256,256]{1,0:T(8,128)(2,1)S(1)}, bf16[256,256]{1,0:T(8,128)(2,1)S(1)}, u32[]{:S(2)}, u32[]{:S(2)}) collective-permute-start(bf16[256,256]{1,0:T(8,128)(2,1)S(1)} %slice_reduce_fusion.own_ref), channel_id=1, source_target_pairs={{0,1},{1,0},{2,3},{3,2},{4,5},{5,4},{6,7},{7,6},{8,9},{9,8},{10,11... | collective-permute-start | bytes 393224 | tf_op jit(solution)/shard_map/ppermute | solution.py:466
  49.7 3.7 %collective-permute-start.2 = (bf16[256,256]{1,0:T(8,128)(2,1)S(1)}, bf16[256,256]{1,0:T(8,128)(2,1)S(1)}, u32[]{:S(2)}, u32[]{:S(2)}) collective-permute-start(bf16[256,256]{1,0:T(8,128)(2,1)S(1)} %slice_reduce_fusion.own_ref), channel_id=1, source_target_pairs={{0,3},{1,2},{2,1},{3,0},{4,7},{5,6},{6,5},{7,4},{8,11},{9,10},{10,... | collective-permute-start | bytes 393224 | tf_op jit(solution)/shard_map/ppermute | solution.py:466
  53.5 7.5 %all-to-all-done.1 = bf16[128,2,640]{2,1,0:T(2,128)(2,1)S(1)} async-done(((bf16[128,2,640]{2,1,0:T(2,128)(2,1)}), bf16[128,2,640]{2,1,0:T(2,128)(2,1)S(1)}, u32[]{:S(2)}, u32[]{:S(2)}) %all-to-all-start.1) | async-done | bytes 327712 | tf_op jit(solution)/shard_map/all_to_all | solution.py:20
  61.0 0.1 reshape.150.msg_ref
  61.1 2.6 %shard_map.87 = (bf16[512,256]{1,0:T(8,128)(2,1)S(1)}, s32[1024,128]{1,0:T(8,128)S(1)}, bf16[256,512]{1,0:T(8,128)(2,1)S(1)}, f32[1,512]{1,0:T(1,128)S(1)}) custom-call(s32[7]{0:T(128)S(1)} %pad_add_fusion.info_ref, bf16[256,640]{1,0:T(8,128)(2,1)S(1)} %reshape.150.msg_ref, bf16[256,256]{1,0:T(8,128)(2,1)S(1)} %slice_reduce_fusion.own_ref), custom_call_target="tpu_custom_call" | custom-call | flops 3221225472 | bytes 1048576 | tf_op jit(solution)/shard_map/pallas_call | solution.py:198
  63.7 2.1 %shard_map.88 = (bf16[1024,512]{1,0:T(8,128)(2,1)}, bf16[1024,256]{1,0:T(8,128)(2,1)}, bf16[512,256]{1,0:T(8,128)(2,1)}, bf16[16,40,256]{2,1,0:T(8,128)(2,1)S(1)}) custom-call(s32[7]{0:T(128)S(1)} %pad_add_fusion.info_ref, bf16[256,256]{1,0:T(8,128)(2,1)S(1)} %slice_reduce_fusion.own_ref, bf16[256,256]{1,0:T(8,128)(2,1)S(1)} %collective-permute-done.by2_ref, ...), custom_call_target="tpu_custom_call" | custom-call | tf_op jit(solution)/shard_map/pallas_call | solution.py:256
  65.8 16.5 %all_to_all.35 = bf16[16,40,256]{2,1,0:T(8,128)(2,1)S(1)} all-to-all(bf16[16,40,256]{2,1,0:T(8,128)(2,1)S(1)} %get-tuple-element.24), channel_id=1, replica_groups=mesh['z'=8,'y'=8,'c'=2,'x'=4] {'y','c'}, dimensions={0} | all-to-all | bytes 655360 | tf_op jit(solution)/shard_map/all_to_all | solution.py:20
  82.4 0.6 pad_maximum_fusion
  83.0 5.0 %all-to-all-start.3 = ((bf16[8,8,256]{2,1,0:T(8,128)(2,1)}), bf16[8,8,256]{2,1,0:T(8,128)(2,1)S(1)}, u32[]{:S(2)}, u32[]{:S(2)}) async-start(bf16[8,8,256]{2,1,0:T(8,128)(2,1)} %pad_maximum_fusion), calls=%async_computation.3 | async-start | bytes 65536 | tf_op jit(solution)/shard_map/all_to_all | solution.py:20
  88.1 7.0 %all-to-all-done.3.sums_ref = bf16[8,8,256]{2,1,0:T(8,128)(2,1)S(1)} async-done(((bf16[8,8,256]{2,1,0:T(8,128)(2,1)}), bf16[8,8,256]{2,1,0:T(8,128)(2,1)S(1)}, u32[]{:S(2)}, u32[]{:S(2)}) %all-to-all-start.3) | async-done | bytes 32800 | tf_op jit(solution)/shard_map/all_to_all | solution.py:20
  95.1 4.1 %shard_map.89 = (bf16[640,256]{1,0:T(8,128)(2,1)S(1)}, bf16[640,256]{1,0:T(8,128)(2,1)S(1)}) custom-call(s32[7]{0:T(128)S(1)} %pad_add_fusion.info_ref, bf16[512,256]{1,0:T(8,128)(2,1)} %get-tuple-element.20.all_q_hbm, bf16[1024,512]{1,0:T(8,128)(2,1)} %get-tuple-element.21.weight_hbm, bf16[1024,256]{1,0:T(8,128)(2,1)} %get-tuple-element.22.layer_hbm, ...), custom_call_target="tpu_custom_call" | custom-call | tf_op jit(solution)/shard_map/pallas_call | solution.py:356
  99.3 2.7 %collective-permute-start.3 = (bf16[640,256]{1,0:T(8,128)(2,1)S(1)}, bf16[640,256]{1,0:T(8,128)(2,1)S(1)}, u32[]{:S(2)}, u32[]{:S(2)}) collective-permute-start(bf16[640,256]{1,0:T(8,128)(2,1)S(1)} %get-tuple-element.27), channel_id=1, source_target_pairs={{0,4},{4,0},{1,5},{5,1},{2,6},{6,2},{3,7},{7,3},{8,12},{12,8},{9,1... | collective-permute-start | bytes 983048 | tf_op jit(solution)/shard_map/ppermute | solution.py:491
  102.0 1.2 collective-permute-done.3
  103.3 0.1 add_convert_fusion
  103.4 15.6 %all_to_all.36 = bf16[8,80,256]{2,1,0:T(8,128)(2,1)S(1)} all-to-all(bf16[8,80,256]{2,1,0:T(8,128)(2,1)S(1)} %bitcast.17), channel_id=1, replica_groups=mesh['z'=8,'y'=8,'c'=2,'x'=4] {'y'}, dimensions={0} | all-to-all | bytes 655360 | tf_op jit(solution)/shard_map/all_to_all | solution.py:20
  119.0 13.4 %all_to_all.37 = bf16[8,80,256]{2,1,0:T(8,128)(2,1)S(1)} all-to-all(bf16[8,80,256]{2,1,0:T(8,128)(2,1)S(1)} %broadcast_in_dim.80), channel_id=1, replica_groups=mesh['z'=8,'y'=8,'c'=2,'x'=4] {'z'}, dimensions={0} | all-to-all | bytes 655360 | tf_op jit(solution)/shard_map/all_to_all | solution.py:20
  132.6 12.9 %all_to_all.38 = bf16[8,80,256]{2,1,0:T(8,128)(2,1)S(1)} all-to-all(bf16[8,80,256]{2,1,0:T(8,128)(2,1)S(1)} %broadcast_in_dim.81), channel_id=1, replica_groups=mesh['z'=8,'y'=8,'c'=2,'x'=4] {'y'}, dimensions={0} | all-to-all | bytes 655360 | tf_op jit(solution)/shard_map/all_to_all | solution.py:20
  145.5 6.2 %collective-permute-start.4 = (bf16[640,256]{1,0:T(8,128)(2,1)S(1)}, bf16[640,256]{1,0:T(8,128)(2,1)S(1)}, u32[]{:S(2)}, u32[]{:S(2)}) collective-permute-start(bf16[640,256]{1,0:T(8,128)(2,1)S(1)} %bitcast.15), channel_id=1, source_target_pairs={{0,4},{4,0},{1,5},{5,1},{2,6},{6,2},{3,7},{7,3},{8,12},{12,8},{9,1... | collective-permute-start | bytes 983048 | tf_op jit(solution)/shard_map/ppermute | solution.py:495
  151.7 1.2 collective-permute-done.4.other_ref
  152.9 0.9 shard_map.90
  (37 shorter events, 0.4 us)
Async XLA Ops:
  0.6 9.1 %copy-start = (s32[131072]{0:T(1024)S(1)}, s32[131072]{0:T(1024)}, u32[]{:S(2)}) copy-start(s32[131072]{0:T(1024)} %param.13) | copy-start | bytes 1572868
  4.8 4.9 %copy-start.4 = (s32[4,128]{1,0:T(4,128)S(1)}, s32[4,128]{1,0:T(4,128)}, u32[]{:S(2)}) copy-start(s32[4,128]{1,0:T(4,128)} %param.11) | copy-start | bytes 6148
  4.9 4.9 %copy-start.5 = (s32[4]{0:T(128)S(1)}, s32[4]{0:T(128)}, u32[]{:S(2)}) copy-start(s32[4]{0:T(128)} %param.12) | copy-start | bytes 52
  4.9 14.8 %all-to-all-start = ((f32[4,264,256]{2,1,0:T(8,128)}), f32[4,264,256]{2,1,0:T(8,128)S(1)}, u32[]{:S(2)}, u32[]{:S(2)}) async-start(f32[4,264,256]{2,1,0:T(8,128)} %get-tuple-element.15), calls=%async_computation | async-start | bytes 2162688 | tf_op jit(solution)/shard_map/all_to_all | solution.py:20
  20.9 40.1 %all-to-all-start.1 = ((bf16[128,2,640]{2,1,0:T(2,128)(2,1)}), bf16[128,2,640]{2,1,0:T(2,128)(2,1)S(1)}, u32[]{:S(2)}, u32[]{:S(2)}) async-start(bf16[128,2,640]{2,1,0:T(2,128)(2,1)} %fusion.2), calls=%async_computation.1 | async-start | bytes 655360 | tf_op jit(solution)/shard_map/all_to_all | solution.py:20
  44.5 19.2 %collective-permute-start = (bf16[256,256]{1,0:T(8,128)(2,1)S(1)}, bf16[256,256]{1,0:T(8,128)(2,1)S(1)}, u32[]{:S(2)}, u32[]{:S(2)}) collective-permute-start(bf16[256,256]{1,0:T(8,128)(2,1)S(1)} %slice_reduce_fusion.own_ref), channel_id=1, source_target_pairs={{0,2},{1,3},{2,0},{3,1},{4,6},{5,7},{6,4},{7,5},{8,10},{9,11},{10,... | collective-permute-start | bytes 393224 | tf_op jit(solution)/shard_map/ppermute | solution.py:466
  46.6 17.0 %collective-permute-start.1 = (bf16[256,256]{1,0:T(8,128)(2,1)S(1)}, bf16[256,256]{1,0:T(8,128)(2,1)S(1)}, u32[]{:S(2)}, u32[]{:S(2)}) collective-permute-start(bf16[256,256]{1,0:T(8,128)(2,1)S(1)} %slice_reduce_fusion.own_ref), channel_id=1, source_target_pairs={{0,1},{1,0},{2,3},{3,2},{4,5},{5,4},{6,7},{7,6},{8,9},{9,8},{10,11... | collective-permute-start | bytes 393224 | tf_op jit(solution)/shard_map/ppermute | solution.py:466
  49.7 14.0 %collective-permute-start.2 = (bf16[256,256]{1,0:T(8,128)(2,1)S(1)}, bf16[256,256]{1,0:T(8,128)(2,1)S(1)}, u32[]{:S(2)}, u32[]{:S(2)}) collective-permute-start(bf16[256,256]{1,0:T(8,128)(2,1)S(1)} %slice_reduce_fusion.own_ref), channel_id=1, source_target_pairs={{0,3},{1,2},{2,1},{3,0},{4,7},{5,6},{6,5},{7,4},{8,11},{9,10},{10,... | collective-permute-start | bytes 393224 | tf_op jit(solution)/shard_map/ppermute | solution.py:466
  63.7 24.3 %copy-start.3 = (bf16[4,1024]{1,0:T(4,128)(2,1)S(1)}, bf16[4,1024]{1,0:T(4,128)(2,1)}, u32[]{:S(2)}) copy-start(bf16[4,1024]{1,0:T(4,128)(2,1)} %q_hbm.1) | copy-start | bytes 24580
  63.7 31.4 %copy-start.1 = (bf16[256,256]{1,0:T(8,128)(2,1)S(1)}, bf16[256,256]{1,0:T(8,128)(2,1)}, u32[]{:S(2)}) copy-start(bf16[256,256]{1,0:T(8,128)(2,1)} %w_out_ref.1) | copy-start | bytes 393220
  63.7 31.4 %copy-start.2 = (bf16[16,256]{1,0:T(8,128)(2,1)S(1)}, bf16[16,256]{1,0:T(8,128)(2,1)}, u32[]{:S(2)}) copy-start(bf16[16,256]{1,0:T(8,128)(2,1)} %get-tuple-element.25.hid_q_ref) | copy-start | bytes 24580
  83.0 12.1 %all-to-all-start.3 = ((bf16[8,8,256]{2,1,0:T(8,128)(2,1)}), bf16[8,8,256]{2,1,0:T(8,128)(2,1)S(1)}, u32[]{:S(2)}, u32[]{:S(2)}) async-start(bf16[8,8,256]{2,1,0:T(8,128)(2,1)} %pad_maximum_fusion), calls=%async_computation.3 | async-start | bytes 65536 | tf_op jit(solution)/shard_map/all_to_all | solution.py:20
  99.3 4.0 %collective-permute-start.3 = (bf16[640,256]{1,0:T(8,128)(2,1)S(1)}, bf16[640,256]{1,0:T(8,128)(2,1)S(1)}, u32[]{:S(2)}, u32[]{:S(2)}) collective-permute-start(bf16[640,256]{1,0:T(8,128)(2,1)S(1)} %get-tuple-element.27), channel_id=1, source_target_pairs={{0,4},{4,0},{1,5},{5,1},{2,6},{6,2},{3,7},{7,3},{8,12},{12,8},{9,1... | collective-permute-start | bytes 983048 | tf_op jit(solution)/shard_map/ppermute | solution.py:491
  145.5 7.5 %collective-permute-start.4 = (bf16[640,256]{1,0:T(8,128)(2,1)S(1)}, bf16[640,256]{1,0:T(8,128)(2,1)S(1)}, u32[]{:S(2)}, u32[]{:S(2)}) collective-permute-start(bf16[640,256]{1,0:T(8,128)(2,1)S(1)} %bitcast.15), channel_id=1, source_target_pairs={{0,4},{4,0},{1,5},{5,1},{2,6},{6,2},{3,7},{7,3},{8,12},{12,8},{9,1... | collective-permute-start | bytes 983048 | tf_op jit(solution)/shard_map/ppermute | solution.py:495

commit v10 on v9

--- a/solution.py
+++ b/solution.py
@@ -454,12 +454,13 @@
         lambda o: (o % yc_count) * z_count + o // yc_count,
         dp_count,
     )
-    codes = jnp.pad(codes[:, None, :], ((0, 0), (0, 1), (0, 0)))
+    codes = jnp.pad(codes[:, None, :], ((0, 0), (0, 1), (few // 2 * width, 0)))
+    codes = lax.optimization_barrier(codes)
 
     own = total(arrived[:, :ROWS]).astype(BF16)
     own_q = jnp.tanh(total(arrived[:, ROWS:]))
-    sent_q = jnp.broadcast_to(own_q[:few].astype(BF16).reshape(1, 2, -1), (dp_count, 2, few // 2 * width))
-    message = exchange(jnp.concatenate([sent_q, codes], 2), YCZ)
+    sent_q = jnp.pad(own_q[:few].astype(BF16).reshape(1, 2, -1), ((0, 0), (0, 0), (0, 128)))
+    message = exchange(codes + sent_q, YCZ)
     message = message.reshape(2 * dp_count, -1)
     layers = [own]
     for far in (2, 1, 3):

time: 154 us -> 154 us (level)
  no operation moved by 1% of the time
where the time goes in v10:
time: 154 us
  blocking collectives  58.4 us (38%)
  starting transfers between devices  51.2 us (33%)
  waiting for transfers between devices  22.3 us (14%)
  Pallas kernels  13.8 us (9%)
  local copies, waits for them, and re-layouts  4.91 us (3%)
    all_to_all x4, blocking collectives, exchange(): return lax.all_to_all(blocks, axes, split_axis=0, concat_axis=0, tiled=True)  58.4 us
    all_to_all x3, starting transfers between devices, exchange(): return lax.all_to_all(blocks, axes, split_axis=0, concat_axis=0, tiled=True)  33.3 us
    all_to_all x3, waiting for transfers between devices, exchange(): return lax.all_to_all(blocks, axes, split_axis=0, concat_axis=0, tiled=True)  19.9 us
    ppermute x3, starting transfers between devices, local(): lax.ppermute(own, 'x', [(i, i ^ far) for i in range(x_count)])  8.98 us
    ppermute x1, starting transfers between devices, local(): return tuple(assemble(grads, lax.ppermute(grads, 'c', swap), w_in.shape[0]))  6.24 us
    pallas_call x1, Pallas kernels, forward(): pl.pallas_call(forward_kernel, in_specs=[FAR] * 4, out_specs=[FAR] * 3, o...  4.2 us
    pallas_call x1, Pallas kernels, backward(): pl.pallas_call(functools.partial(backward_kernel, few, scale), in_specs=[...  4.14 us
    gather x1, local copies, waits for them, and re-layouts, local(): rows = jnp.take(owner_map, named, axis=0)  3.56 us
  transfers between devices with their start and end apart: 8, of which 5 were waited for; matrix products, arithmetic and copies ran while one was open for 3% of the time, Pallas kernels for 2%

profile of v10, /device:TPU:1, one launch (start us, length us, event | category | flops | bytes accessed | tf_op | source)
XLA Modules:
  0.0 153.7 jit_solution(1658940348373239931)
XLA Ops:
  0.6 4.2 %shard_map.86 = (f32[4,264,256]{2,1,0:T(8,128)}, bf16[1024,256]{1,0:T(8,128)(2,1)}, bf16[16,256]{1,0:T(8,128)(2,1)}) custom-call(bf16[4,1024]{1,0:T(4,128)(2,1)} %q_hbm.1, bf16[1024,1024]{1,0:T(8,128)(2,1)} %x_hbm.3, bf16[1024,256]{1,0:T(8,128)(2,1)} %w_in_hbm.1, bf16[256,256]{1,0:T(8,128)(2,1)} %w_out_ref.1), custom_call_target="tpu_custom_call" | custom-call | tf_op jit(solution)/shard_map/pallas_call | solution.py:119
  4.9 4.9 %all-to-all-start = ((f32[4,264,256]{2,1,0:T(8,128)}), f32[4,264,256]{2,1,0:T(8,128)S(1)}, u32[]{:S(2)}, u32[]{:S(2)}) async-start(f32[4,264,256]{2,1,0:T(8,128)} %get-tuple-element.15), calls=%async_computation | async-start | bytes 2162688 | tf_op jit(solution)/shard_map/all_to_all | solution.py:20
  9.8 3.6 %gather_fusion = s32[516]{0:T(1024)S(1)} fusion(s32[131072]{0:T(1024)S(1)} %copy-done, s32[1024]{0:T(1024)S(1)} %pad_clamp_fusion), kind=kCustom, calls=%fused_computation | custom fusion | bytes 6192 | tf_op jit(solution)/shard_map/jit(_take)/gather | solution.py:445
  13.4 0.3 fusion
  13.7 0.6 fusion.1
  14.4 5.3 %all-to-all-done = f32[4,264,256]{2,1,0:T(8,128)S(1)} async-done(((f32[4,264,256]{2,1,0:T(8,128)}), f32[4,264,256]{2,1,0:T(8,128)S(1)}, u32[]{:S(2)}, u32[]{:S(2)}) %all-to-all-start) | async-done | bytes 1081376 | tf_op jit(solution)/shard_map/all_to_all | solution.py:20
  19.7 1.1 copy.14
  20.8 23.4 %all-to-all-start.1 = ((bf16[128,2,640]{2,1,0:T(2,128)(2,1)}), bf16[128,2,640]{2,1,0:T(2,128)(2,1)S(1)}, u32[]{:S(2)}, u32[]{:S(2)}) async-start(bf16[128,2,640]{2,1,0:T(2,128)(2,1)} %copy.14), calls=%async_computation.1 | async-start | bytes 655360 | tf_op jit(solution)/shard_map/all_to_all | solution.py:20
  44.2 0.1 pad_add_fusion.info_ref
  44.3 0.1 slice_reduce_fusion.own_ref
  44.4 2.2 %collective-permute-start = (bf16[256,256]{1,0:T(8,128)(2,1)S(1)}, bf16[256,256]{1,0:T(8,128)(2,1)S(1)}, u32[]{:S(2)}, u32[]{:S(2)}) collective-permute-start(bf16[256,256]{1,0:T(8,128)(2,1)S(1)} %slice_reduce_fusion.own_ref), channel_id=1, source_target_pairs={{0,2},{1,3},{2,0},{3,1},{4,6},{5,7},{6,4},{7,5},{8,10},{9,11},{10,... | collective-permute-start | bytes 393224 | tf_op jit(solution)/shard_map/ppermute | solution.py:467
  46.6 3.1 %collective-permute-start.1 = (bf16[256,256]{1,0:T(8,128)(2,1)S(1)}, bf16[256,256]{1,0:T(8,128)(2,1)S(1)}, u32[]{:S(2)}, u32[]{:S(2)}) collective-permute-start(bf16[256,256]{1,0:T(8,128)(2,1)S(1)} %slice_reduce_fusion.own_ref), channel_id=1, source_target_pairs={{0,1},{1,0},{2,3},{3,2},{4,5},{5,4},{6,7},{7,6},{8,9},{9,8},{10,11... | collective-permute-start | bytes 393224 | tf_op jit(solution)/shard_map/ppermute | solution.py:467
  49.7 3.7 %collective-permute-start.2 = (bf16[256,256]{1,0:T(8,128)(2,1)S(1)}, bf16[256,256]{1,0:T(8,128)(2,1)S(1)}, u32[]{:S(2)}, u32[]{:S(2)}) collective-permute-start(bf16[256,256]{1,0:T(8,128)(2,1)S(1)} %slice_reduce_fusion.own_ref), channel_id=1, source_target_pairs={{0,3},{1,2},{2,1},{3,0},{4,7},{5,6},{6,5},{7,4},{8,11},{9,10},{10,... | collective-permute-start | bytes 393224 | tf_op jit(solution)/shard_map/ppermute | solution.py:467
  53.4 7.5 %all-to-all-done.1 = bf16[128,2,640]{2,1,0:T(2,128)(2,1)S(1)} async-done(((bf16[128,2,640]{2,1,0:T(2,128)(2,1)}), bf16[128,2,640]{2,1,0:T(2,128)(2,1)S(1)}, u32[]{:S(2)}, u32[]{:S(2)}) %all-to-all-start.1) | async-done | bytes 327712 | tf_op jit(solution)/shard_map/all_to_all | solution.py:20
  60.9 0.1 reshape.152.msg_ref
  61.0 2.6 %shard_map.87 = (bf16[512,256]{1,0:T(8,128)(2,1)S(1)}, s32[1024,128]{1,0:T(8,128)S(1)}, bf16[256,512]{1,0:T(8,128)(2,1)S(1)}, f32[1,512]{1,0:T(1,128)S(1)}) custom-call(s32[7]{0:T(128)S(1)} %pad_add_fusion.info_ref, bf16[256,640]{1,0:T(8,128)(2,1)S(1)} %reshape.152.msg_ref, bf16[256,256]{1,0:T(8,128)(2,1)S(1)} %slice_reduce_fusion.own_ref), custom_call_target="tpu_custom_call" | custom-call | flops 3221225472 | bytes 1048576 | tf_op jit(solution)/shard_map/pallas_call | solution.py:198
  63.7 2.1 %shard_map.88 = (bf16[1024,512]{1,0:T(8,128)(2,1)}, bf16[1024,256]{1,0:T(8,128)(2,1)}, bf16[512,256]{1,0:T(8,128)(2,1)}, bf16[16,40,256]{2,1,0:T(8,128)(2,1)S(1)}) custom-call(s32[7]{0:T(128)S(1)} %pad_add_fusion.info_ref, bf16[256,256]{1,0:T(8,128)(2,1)S(1)} %slice_reduce_fusion.own_ref, bf16[256,256]{1,0:T(8,128)(2,1)S(1)} %collective-permute-done.by2_ref, ...), custom_call_target="tpu_custom_call" | custom-call | tf_op jit(solution)/shard_map/pallas_call | solution.py:256
  65.7 16.5 %all_to_all.35 = bf16[16,40,256]{2,1,0:T(8,128)(2,1)S(1)} all-to-all(bf16[16,40,256]{2,1,0:T(8,128)(2,1)S(1)} %get-tuple-element.24), channel_id=1, replica_groups=mesh['z'=8,'y'=8,'c'=2,'x'=4] {'y','c'}, dimensions={0} | all-to-all | bytes 655360 | tf_op jit(solution)/shard_map/all_to_all | solution.py:20
  82.2 0.1 convert_reduce_fusion
  82.3 0.6 pad_maximum_fusion
  83.0 5.0 %all-to-all-start.3 = ((bf16[8,8,256]{2,1,0:T(8,128)(2,1)}), bf16[8,8,256]{2,1,0:T(8,128)(2,1)S(1)}, u32[]{:S(2)}, u32[]{:S(2)}) async-start(bf16[8,8,256]{2,1,0:T(8,128)(2,1)} %pad_maximum_fusion), calls=%async_computation.3 | async-start | bytes 65536 | tf_op jit(solution)/shard_map/all_to_all | solution.py:20
  88.0 7.0 %all-to-all-done.3.sums_ref = bf16[8,8,256]{2,1,0:T(8,128)(2,1)S(1)} async-done(((bf16[8,8,256]{2,1,0:T(8,128)(2,1)}), bf16[8,8,256]{2,1,0:T(8,128)(2,1)S(1)}, u32[]{:S(2)}, u32[]{:S(2)}) %all-to-all-start.3) | async-done | bytes 32800 | tf_op jit(solution)/shard_map/all_to_all | solution.py:20
  95.1 4.1 %shard_map.89 = (bf16[640,256]{1,0:T(8,128)(2,1)S(1)}, bf16[640,256]{1,0:T(8,128)(2,1)S(1)}) custom-call(s32[7]{0:T(128)S(1)} %pad_add_fusion.info_ref, bf16[512,256]{1,0:T(8,128)(2,1)} %get-tuple-element.20.all_q_hbm, bf16[1024,512]{1,0:T(8,128)(2,1)} %get-tuple-element.21.weight_hbm, bf16[1024,256]{1,0:T(8,128)(2,1)} %get-tuple-element.22.layer_hbm, ...), custom_call_target="tpu_custom_call" | custom-call | tf_op jit(solution)/shard_map/pallas_call | solution.py:356
  99.2 2.7 %collective-permute-start.3 = (bf16[640,256]{1,0:T(8,128)(2,1)S(1)}, bf16[640,256]{1,0:T(8,128)(2,1)S(1)}, u32[]{:S(2)}, u32[]{:S(2)}) collective-permute-start(bf16[640,256]{1,0:T(8,128)(2,1)S(1)} %get-tuple-element.27), channel_id=1, source_target_pairs={{0,4},{4,0},{1,5},{5,1},{2,6},{6,2},{3,7},{7,3},{8,12},{12,8},{9,1... | collective-permute-start | bytes 983048 | tf_op jit(solution)/shard_map/ppermute | solution.py:492
  101.9 1.2 collective-permute-done.3
  103.2 0.1 add_convert_fusion
  103.3 15.6 %all_to_all.36 = bf16[8,80,256]{2,1,0:T(8,128)(2,1)S(1)} all-to-all(bf16[8,80,256]{2,1,0:T(8,128)(2,1)S(1)} %bitcast.19), channel_id=1, replica_groups=mesh['z'=8,'y'=8,'c'=2,'x'=4] {'y'}, dimensions={0} | all-to-all | bytes 655360 | tf_op jit(solution)/shard_map/all_to_all | solution.py:20
  119.0 13.4 %all_to_all.37 = bf16[8,80,256]{2,1,0:T(8,128)(2,1)S(1)} all-to-all(bf16[8,80,256]{2,1,0:T(8,128)(2,1)S(1)} %broadcast_in_dim.71), channel_id=1, replica_groups=mesh['z'=8,'y'=8,'c'=2,'x'=4] {'z'}, dimensions={0} | all-to-all | bytes 655360 | tf_op jit(solution)/shard_map/all_to_all | solution.py:20
  132.5 12.9 %all_to_all.38 = bf16[8,80,256]{2,1,0:T(8,128)(2,1)S(1)} all-to-all(bf16[8,80,256]{2,1,0:T(8,128)(2,1)S(1)} %broadcast_in_dim.72), channel_id=1, replica_groups=mesh['z'=8,'y'=8,'c'=2,'x'=4] {'y'}, dimensions={0} | all-to-all | bytes 655360 | tf_op jit(solution)/shard_map/all_to_all | solution.py:20
  145.4 6.2 %collective-permute-start.4 = (bf16[640,256]{1,0:T(8,128)(2,1)S(1)}, bf16[640,256]{1,0:T(8,128)(2,1)S(1)}, u32[]{:S(2)}, u32[]{:S(2)}) collective-permute-start(bf16[640,256]{1,0:T(8,128)(2,1)S(1)} %bitcast.17), channel_id=1, source_target_pairs={{0,4},{4,0},{1,5},{5,1},{2,6},{6,2},{3,7},{7,3},{8,12},{12,8},{9,1... | collective-permute-start | bytes 983048 | tf_op jit(solution)/shard_map/ppermute | solution.py:496
  151.6 1.2 collective-permute-done.4.other_ref
  152.9 0.9 shard_map.90
  (38 shorter events, 0.4 us)
Async XLA Ops:
  0.6 9.1 %copy-start = (s32[131072]{0:T(1024)S(1)}, s32[131072]{0:T(1024)}, u32[]{:S(2)}) copy-start(s32[131072]{0:T(1024)} %param.13) | copy-start | bytes 1572868
  4.8 4.9 %copy-start.4 = (s32[4,128]{1,0:T(4,128)S(1)}, s32[4,128]{1,0:T(4,128)}, u32[]{:S(2)}) copy-start(s32[4,128]{1,0:T(4,128)} %param.11) | copy-start | bytes 6148
  4.9 4.9 %copy-start.5 = (s32[4]{0:T(128)S(1)}, s32[4]{0:T(128)}, u32[]{:S(2)}) copy-start(s32[4]{0:T(128)} %param.12) | copy-start | bytes 52
  4.9 14.8 %all-to-all-start = ((f32[4,264,256]{2,1,0:T(8,128)}), f32[4,264,256]{2,1,0:T(8,128)S(1)}, u32[]{:S(2)}, u32[]{:S(2)}) async-start(f32[4,264,256]{2,1,0:T(8,128)} %get-tuple-element.15), calls=%async_computation | async-start | bytes 2162688 | tf_op jit(solution)/shard_map/all_to_all | solution.py:20
  20.8 40.1 %all-to-all-start.1 = ((bf16[128,2,640]{2,1,0:T(2,128)(2,1)}), bf16[128,2,640]{2,1,0:T(2,128)(2,1)S(1)}, u32[]{:S(2)}, u32[]{:S(2)}) async-start(bf16[128,2,640]{2,1,0:T(2,128)(2,1)} %copy.14), calls=%async_computation.1 | async-start | bytes 655360 | tf_op jit(solution)/shard_map/all_to_all | solution.py:20
  44.4 19.2 %collective-permute-start = (bf16[256,256]{1,0:T(8,128)(2,1)S(1)}, bf16[256,256]{1,0:T(8,128)(2,1)S(1)}, u32[]{:S(2)}, u32[]{:S(2)}) collective-permute-start(bf16[256,256]{1,0:T(8,128)(2,1)S(1)} %slice_reduce_fusion.own_ref), channel_id=1, source_target_pairs={{0,2},{1,3},{2,0},{3,1},{4,6},{5,7},{6,4},{7,5},{8,10},{9,11},{10,... | collective-permute-start | bytes 393224 | tf_op jit(solution)/shard_map/ppermute | solution.py:467
  46.6 17.0 %collective-permute-start.1 = (bf16[256,256]{1,0:T(8,128)(2,1)S(1)}, bf16[256,256]{1,0:T(8,128)(2,1)S(1)}, u32[]{:S(2)}, u32[]{:S(2)}) collective-permute-start(bf16[256,256]{1,0:T(8,128)(2,1)S(1)} %slice_reduce_fusion.own_ref), channel_id=1, source_target_pairs={{0,1},{1,0},{2,3},{3,2},{4,5},{5,4},{6,7},{7,6},{8,9},{9,8},{10,11... | collective-permute-start | bytes 393224 | tf_op jit(solution)/shard_map/ppermute | solution.py:467
  49.7 14.0 %collective-permute-start.2 = (bf16[256,256]{1,0:T(8,128)(2,1)S(1)}, bf16[256,256]{1,0:T(8,128)(2,1)S(1)}, u32[]{:S(2)}, u32[]{:S(2)}) collective-permute-start(bf16[256,256]{1,0:T(8,128)(2,1)S(1)} %slice_reduce_fusion.own_ref), channel_id=1, source_target_pairs={{0,3},{1,2},{2,1},{3,0},{4,7},{5,6},{6,5},{7,4},{8,11},{9,10},{10,... | collective-permute-start | bytes 393224 | tf_op jit(solution)/shard_map/ppermute | solution.py:467
  63.6 24.3 %copy-start.3 = (bf16[4,1024]{1,0:T(4,128)(2,1)S(1)}, bf16[4,1024]{1,0:T(4,128)(2,1)}, u32[]{:S(2)}) copy-start(bf16[4,1024]{1,0:T(4,128)(2,1)} %q_hbm.1) | copy-start | bytes 24580
  63.7 31.4 %copy-start.1 = (bf16[256,256]{1,0:T(8,128)(2,1)S(1)}, bf16[256,256]{1,0:T(8,128)(2,1)}, u32[]{:S(2)}) copy-start(bf16[256,256]{1,0:T(8,128)(2,1)} %w_out_ref.1) | copy-start | bytes 393220
  63.7 31.4 %copy-start.2 = (bf16[16,256]{1,0:T(8,128)(2,1)S(1)}, bf16[16,256]{1,0:T(8,128)(2,1)}, u32[]{:S(2)}) copy-start(bf16[16,256]{1,0:T(8,128)(2,1)} %get-tuple-element.25.hid_q_ref) | copy-start | bytes 24580
  83.0 12.1 %all-to-all-start.3 = ((bf16[8,8,256]{2,1,0:T(8,128)(2,1)}), bf16[8,8,256]{2,1,0:T(8,128)(2,1)S(1)}, u32[]{:S(2)}, u32[]{:S(2)}) async-start(bf16[8,8,256]{2,1,0:T(8,128)(2,1)} %pad_maximum_fusion), calls=%async_computation.3 | async-start | bytes 65536 | tf_op jit(solution)/shard_map/all_to_all | solution.py:20
  99.2 4.0 %collective-permute-start.3 = (bf16[640,256]{1,0:T(8,128)(2,1)S(1)}, bf16[640,256]{1,0:T(8,128)(2,1)S(1)}, u32[]{:S(2)}, u32[]{:S(2)}) collective-permute-start(bf16[640,256]{1,0:T(8,128)(2,1)S(1)} %get-tuple-element.27), channel_id=1, source_target_pairs={{0,4},{4,0},{1,5},{5,1},{2,6},{6,2},{3,7},{7,3},{8,12},{12,8},{9,1... | collective-permute-start | bytes 983048 | tf_op jit(solution)/shard_map/ppermute | solution.py:492
  145.4 7.5 %collective-permute-start.4 = (bf16[640,256]{1,0:T(8,128)(2,1)S(1)}, bf16[640,256]{1,0:T(8,128)(2,1)S(1)}, u32[]{:S(2)}, u32[]{:S(2)}) collective-permute-start(bf16[640,256]{1,0:T(8,128)(2,1)S(1)} %bitcast.17), channel_id=1, source_target_pairs={{0,4},{4,0},{1,5},{5,1},{2,6},{6,2},{3,7},{7,3},{8,12},{12,8},{9,1... | collective-permute-start | bytes 983048 | tf_op jit(solution)/shard_map/ppermute | solution.py:496
